TPU v7x, 32 devices: a whole 2x2x4 slice. The times are simulated.
32 devices in a mesh: depth: 8 (over z, x), strip: 4 (over y, core).
Axes of the slice: x: 2, y: 2, z: 4, core: 2. Of those that a mesh axis runs over, the one named last changes fastest.
Arguments:
- density: bfloat16 [32, 64, 1024], P('depth', 'strip'), may hold values from -6 to 6
- tf_bins: int32 [32, 64, 1024], P('depth', 'strip'), may hold values from 0 to 15
- tf_table: float32 [4, 16], replicated, may hold values from 0.2 to 2
- brick_order: int32 [4, 8], P('strip'), may hold values from 0 to 7, each once within a row
Outputs:
- image: float32 [4, 65536], P(None, ('strip', 'depth'))
Inputs may be any that keep to these rules, and one draw needn't show every extreme that they name: `tf_bins`: each voxel's bin indexes a column of tf_table. `brick_order`: each row lists every brick once.
All inputs are finite; a program needn't handle non-finite values.
Results may differ from a plain program's by a relative error of at most 0.0017.
Values may be sent and summed in bfloat16 or wider, within the bound.
No kernel may reach another device: no remote copies, remote signals or barrier semaphores. Data moves between devices by JAX's collectives and lax.ppermute only.
A program may use at most 64 MiB of HBM per device.

v0:
```python
import jax
import jax.numpy as jnp
from jax import lax
from jax.sharding import PartitionSpec as P

LIGHT_X = 0.36
LIGHT_Y = 0.48
LIGHT_Z = 0.8
SHADE_GAIN = 1.5


def with_halo(cells, sides, width):
    for axis, dim in sides:
        count = lax.axis_size(axis)
        ends = count - 1
        head = lax.slice_in_dim(cells, 0, width, axis=dim)
        tail = lax.slice_in_dim(cells, cells.shape[dim] - width, cells.shape[dim], axis=dim)
        cells = jnp.concatenate(
            [
                lax.ppermute(tail, axis, [(i, (i + 1) % count) for i in range(ends)]),
                cells,
                lax.ppermute(head, axis, [((i + 1) % count, i) for i in range(ends)]),
            ],
            axis=dim,
        )
    return cells


def shear_plane(values, plane_index):
    across = values.shape[-1]
    offset = 3 * plane_index // 8
    fraction = (3 * plane_index % 8).astype(jnp.float32) / 8.0
    columns = jnp.arange(across, dtype=jnp.int32)
    first = jnp.where(columns < across - offset, jnp.roll(values, -offset, axis=2), 0.0)
    second = jnp.where(columns < across - offset - 1, jnp.roll(first, -1, axis=2), 0.0)
    return (1.0 - fraction) * first + fraction * second


def plane_terms(window, tf_plane, tf_table, plane_index, total_planes):
    beneath = window[0]
    middle = window[1]
    overhead = window[2]
    centre = middle[1:-1]
    sideways = jnp.pad(centre, ((0, 0), (1, 1)))
    slope_across = 0.5 * (sideways[:, 2:] - sideways[:, :-2])
    slope_down = 0.5 * (middle[2:] - middle[:-2])
    slope_deep = 0.5 * (overhead[1:-1] - beneath[1:-1])
    lengths = jnp.sqrt(
        1.0 + slope_across * slope_across + slope_down * slope_down + slope_deep * slope_deep
    )
    shading = (LIGHT_X * slope_across + LIGHT_Y * slope_down + LIGHT_Z * slope_deep) / lengths
    classes = jnp.arange(tf_table.shape[1], dtype=jnp.int32)
    onehot = (tf_plane[None, :, :] == classes[:, None, None]).astype(jnp.float32)
    looked = jnp.einsum("cm,myx->cyx", tf_table, onehot, precision=lax.Precision.HIGHEST)
    extinction = looked[0] * (1.0 + centre * centre) / total_planes
    opacity = 1.0 - jnp.exp(-extinction)
    emitted = looked[1:] * (opacity * jnp.exp(SHADE_GAIN * shading))[None]
    return shear_plane(jnp.concatenate([extinction[None], emitted], axis=0), plane_index)


def order_mask(sequence):
    bricks = sequence.shape[0]
    slots = jnp.arange(bricks, dtype=jnp.int32)
    onehot = (sequence[:, None] == slots[None, :]).astype(jnp.int32)
    position = jnp.sum(onehot * slots[:, None], axis=0)
    return (position[None, :] < position[:, None]).astype(jnp.float32)


def per_device(density, tf_bins, tf_table, brick_order):
    planes = density.shape[0]
    height = density.shape[1]
    across = density.shape[2]
    bricks = lax.axis_size("depth")
    block = with_halo(density, (("depth", 0), ("strip", 1)), 1)
    first_plane = lax.axis_index("depth") * planes
    total_planes = planes * bricks
    colour = jnp.zeros((3, height, across), jnp.float32)
    depth_sum = jnp.zeros((height, across), jnp.float32)
    for plane_at in range(planes):
        window = block[plane_at : plane_at + 3].astype(jnp.float32)
        sheared = plane_terms(
            window, tf_bins[plane_at], tf_table, first_plane + plane_at, total_planes
        )
        colour = colour + jnp.exp(-depth_sum)[None] * sheared[1:]
        depth_sum = depth_sum + sheared[0]
    pixels = height * across
    before = order_mask(brick_order[0])
    flat_colour = colour.reshape(3, pixels)
    flat_depth = depth_sum.reshape(1, pixels)
    depths = lax.all_to_all(
        flat_depth.astype(jnp.bfloat16), "depth", split_axis=1, concat_axis=0, tiled=True
    ).astype(flat_depth.dtype)
    prefix = jnp.dot(before, depths, precision=lax.Precision.HIGHEST)
    own_prefix = lax.all_to_all(
        prefix.astype(jnp.bfloat16), "depth", split_axis=0, concat_axis=1, tiled=True
    ).astype(prefix.dtype)
    shown = lax.psum_scatter(
        jnp.exp(-own_prefix) * flat_colour, "depth", scatter_dimension=1, tiled=True
    )
    remaining = jnp.exp(-jnp.sum(depths, axis=0))
    return jnp.concatenate([shown, remaining[None]], axis=0)


def solution(mesh):
    in_specs = (P("depth", "strip", None), P("depth", "strip", None), P(), P("strip", None))
    out_specs = P(None, ("strip", "depth"))
    return jax.shard_map(
        per_device, mesh=mesh, in_specs=in_specs, out_specs=out_specs, check_vma=False
    )
```

profile of v0, /device:TPU:0, one launch (start us, length us, event | category | flops | bytes accessed | tf_op | source)
XLA Modules:
  0.0 218.9 jit_solution(8450788332974451485)
XLA Ops:
  6.5 0.8 fusion.84
  7.3 1.3 collective-permute-start.1
  8.6 5.5 %collective-permute-start = (bf16[1,16,1024]{2,1,0:T(8,128)(2,1)S(1)}, bf16[1,16,1024]{2,1,0:T(8,128)(2,1)S(1)}, u32[]{:S(2)}, u32[]{:S(2)}) collective-permute-start(bf16[1,16,1024]{2,1,0:T(8,128)(2,1)S(1)} %get-tuple-element.31), channel_id=1, source_target_pairs={{0,4},{4,8},{8,12},{12,16},{16,20},{20,24},{24,28},{1,5},{5,9},{9,... | collective-permute-start | bytes 98312 | tf_op jit(solution)/shard_map/ppermute | solution.py:20
  14.2 0.7 select_reduce_fusion
  15.0 1.0 slice_bitcast_fusion.3
  15.9 0.4 convolution_bitcast_fusion.1
  16.3 0.4 convolution_bitcast_fusion
  16.8 0.4 fusion.1
  17.2 0.4 fusion.2
  17.6 0.9 constant_dynamic-update-slice_fusion.1
  18.6 1.5 collective-permute-start.2
  20.1 1.3 collective-permute-start.3
  22.1 3.2 %collective-permute-done.3 = bf16[6,1,1024]{2,1,0:T(2,128)(2,1)S(1)} collective-permute-done((bf16[6,1,1024]{2,1,0:T(2,128)(2,1)S(1)}, bf16[6,1,1024]{2,1,0:T(2,128)(2,1)S(1)}, u32[]{:S(2)}, u32[]{:S(2)}) %collective-permute-start.3) | collective-permute-done | bytes 12320 | tf_op jit(solution)/shard_map/ppermute | solution.py:22
  26.7 0.7 fusion.21
  28.1 0.7 fusion.9
  29.0 0.6 fusion.26
  30.0 0.3 copy_add_fusion
  30.4 0.7 fusion.30
  31.2 0.5 broadcast.127
  31.8 0.8 reduce
  32.6 0.6 reshape.175
  33.2 5.7 %all-to-all-start = ((bf16[8,2,1024]{2,1,0:T(2,128)(2,1)}), bf16[8,2,1024]{2,1,0:T(2,128)(2,1)S(1)}, u32[]{:S(2)}, u32[]{:S(2)}) async-start(bf16[8,2,1024]{2,1,0:T(2,128)(2,1)} %reshape.175), calls=%async_computation | async-start | bytes 65536 | tf_op jit(solution)/shard_map/all_to_all | solution.py:90
  39.0 6.6 %all-to-all-done = bf16[8,2,1024]{2,1,0:T(2,128)(2,1)S(1)} async-done(((bf16[8,2,1024]{2,1,0:T(2,128)(2,1)}), bf16[8,2,1024]{2,1,0:T(2,128)(2,1)S(1)}, u32[]{:S(2)}, u32[]{:S(2)}) %all-to-all-start) | async-done | bytes 32800 | tf_op jit(solution)/shard_map/all_to_all | solution.py:90
  45.8 0.6 reduce.1
  46.5 0.6 reshape.177
  47.1 3.3 %all-to-all-start.1 = ((bf16[8,2,1024]{2,1,0:T(2,128)(2,1)}), bf16[8,2,1024]{2,1,0:T(2,128)(2,1)S(1)}, u32[]{:S(2)}, u32[]{:S(2)}) async-start(bf16[8,2,1024]{2,1,0:T(2,128)(2,1)} %reshape.177), calls=%async_computation.1 | async-start | bytes 65536 | tf_op jit(solution)/shard_map/all_to_all | solution.py:94
  50.5 0.3 fusion.23
  50.8 6.3 %all-to-all-done.1 = bf16[8,2,1024]{2,1,0:T(2,128)(2,1)S(1)} async-done(((bf16[8,2,1024]{2,1,0:T(2,128)(2,1)}), bf16[8,2,1024]{2,1,0:T(2,128)(2,1)S(1)}, u32[]{:S(2)}, u32[]{:S(2)}) %all-to-all-start.1) | async-done | bytes 32800 | tf_op jit(solution)/shard_map/all_to_all | solution.py:94
  57.4 5.1 %copy.81 = f32[3,16384]{0,1:T(8,128)} copy(f32[3,16384]{1,0:T(4,128)S(1)} %broadcast_multiply_fusion) | data formatting | bytes 393216
  62.5 147.4 %reduce-scatter.4.cloned.1.call-done = f32[2048,3]{1,0:T(8,128)} async-done(((f32[16384,3]{1,0:T(8,128)}), f32[2048,3]{1,0:T(8,128)}) %reduce-scatter.4.cloned.1.call-update) | async-done | bytes 24592
  209.9 1.6 copy.82
  211.4 0.6 pad_maximum_fusion.2
  (60 shorter events, 3.9 us)
Async XLA Ops:
  6.5 9.4 %copy-start = (f32[4,16]{1,0:T(4,128)S(1)}, f32[4,16]{1,0:T(4,128)}, u32[]{:S(2)}) copy-start(f32[4,16]{1,0:T(4,128)} %param.8) | copy-start | bytes 772
  7.3 11.2 %collective-permute-start.1 = (bf16[1,16,1024]{2,1,0:T(8,128)(2,1)S(1)}, bf16[1,16,1024]{2,1,0:T(8,128)(2,1)S(1)}, u32[]{:S(2)}, u32[]{:S(2)}) collective-permute-start(bf16[1,16,1024]{2,1,0:T(8,128)(2,1)S(1)} %get-tuple-element.30), channel_id=1, source_target_pairs={{4,0},{8,4},{12,8},{16,12},{20,16},{24,20},{28,24},{5,1},{9,5},{13... | collective-permute-start | bytes 98312 | tf_op jit(solution)/shard_map/ppermute | solution.py:22
  8.6 9.0 %collective-permute-start = (bf16[1,16,1024]{2,1,0:T(8,128)(2,1)S(1)}, bf16[1,16,1024]{2,1,0:T(8,128)(2,1)S(1)}, u32[]{:S(2)}, u32[]{:S(2)}) collective-permute-start(bf16[1,16,1024]{2,1,0:T(8,128)(2,1)S(1)} %get-tuple-element.31), channel_id=1, source_target_pairs={{0,4},{4,8},{8,12},{12,16},{16,20},{20,24},{24,28},{1,5},{5,9},{9,... | collective-permute-start | bytes 98312 | tf_op jit(solution)/shard_map/ppermute | solution.py:20
  18.6 3.4 %collective-permute-start.2 = (bf16[6,1,1024]{2,1,0:T(2,128)(2,1)S(1)}, bf16[6,1,1024]{2,1,0:T(2,128)(2,1)S(1)}, u32[]{:S(2)}, u32[]{:S(2)}) collective-permute-start(bf16[6,1,1024]{2,1,0:T(2,128)(2,1)S(1)} %get-tuple-element.28), channel_id=1, source_target_pairs={{0,1},{1,2},{2,3},{4,5},{5,6},{6,7},{8,9},{9,10},{10,11},{12,13},{... | collective-permute-start | bytes 36872 | tf_op jit(solution)/shard_map/ppermute | solution.py:20
  20.1 5.2 %collective-permute-start.3 = (bf16[6,1,1024]{2,1,0:T(2,128)(2,1)S(1)}, bf16[6,1,1024]{2,1,0:T(2,128)(2,1)S(1)}, u32[]{:S(2)}, u32[]{:S(2)}) collective-permute-start(bf16[6,1,1024]{2,1,0:T(2,128)(2,1)S(1)} %get-tuple-element.29), channel_id=1, source_target_pairs={{1,0},{2,1},{3,2},{5,4},{6,5},{7,6},{9,8},{10,9},{11,10},{13,12},{... | collective-permute-start | bytes 36872 | tf_op jit(solution)/shard_map/ppermute | solution.py:22
  33.2 12.4 %all-to-all-start = ((bf16[8,2,1024]{2,1,0:T(2,128)(2,1)}), bf16[8,2,1024]{2,1,0:T(2,128)(2,1)S(1)}, u32[]{:S(2)}, u32[]{:S(2)}) async-start(bf16[8,2,1024]{2,1,0:T(2,128)(2,1)} %reshape.175), calls=%async_computation | async-start | bytes 65536 | tf_op jit(solution)/shard_map/all_to_all | solution.py:90
  47.1 10.0 %all-to-all-start.1 = ((bf16[8,2,1024]{2,1,0:T(2,128)(2,1)}), bf16[8,2,1024]{2,1,0:T(2,128)(2,1)S(1)}, u32[]{:S(2)}, u32[]{:S(2)}) async-start(bf16[8,2,1024]{2,1,0:T(2,128)(2,1)} %reshape.177), calls=%async_computation.1 | async-start | bytes 65536 | tf_op jit(solution)/shard_map/all_to_all | solution.py:94
  50.5 159.4 %reduce-scatter.4.cloned.1.call-start = ((), (), s32[]{:S(2)}) async-start(), calls=%async_computation.3 | async-start | bytes 9437184
Sparse Core Ops, SparseCore 0:
  62.6 147.2 reduce-scatter.3
where the time goes:
time: 219 us
  waiting for transfers between devices  164 us (75%)
  starting transfers between devices  18.6 us (8%)
  between operations  14.1 us (6%)
  local copies, waits for them, and re-layouts  12.5 us (6%)
  other arithmetic  8.32 us (4%)
    unnamed x2, waiting for transfers between devices  147 us
    unnamed x12, local copies, waits for them, and re-layouts  9.41 us
    ppermute x2, starting transfers between devices, with_halo(): lax.ppermute(tail, axis, [(i, (i + 1) % count) for i in range(ends)])  6.94 us
    all_to_all x1, waiting for transfers between devices, per_device(): lax.all_to_all(flat_depth.astype(jnp.bfloat16), 'depth', split_axis=1, co...  6.64 us
    all_to_all x1, waiting for transfers between devices, per_device(): lax.all_to_all(prefix.astype(jnp.bfloat16), 'depth', split_axis=0, concat...  6.3 us
    all_to_all x1, starting transfers between devices, per_device(): lax.all_to_all(flat_depth.astype(jnp.bfloat16), 'depth', split_axis=1, co...  5.7 us
  transfers between devices with their start and end apart: 7, of which 4 were waited for; matrix products, arithmetic and copies ran while one was open for 2% of the time, Pallas kernels for 0%

commit v1 on v0

v1 whole, which is shorter than its diff:
```python
import functools

import jax
import jax.numpy as jnp
from jax import lax
from jax.experimental import pallas as pl
from jax.experimental.pallas import tpu as pltpu
from jax.sharding import PartitionSpec as P

LIGHT = (0.36, 0.48, 0.8)
SHADE_GAIN = 1.5
LOG2E = 1.4426950408889634
LANES = 128

MAX_DENSITY = 6.0
MAX_LOOKED = 2.0

COLOUR_STEPS = 2048.0
COLOUR_LOW = -28.0
CODE_MAX = 65535.0


def depth_scale(planes, total_planes):
    return MAX_LOOKED * (1.0 + MAX_DENSITY * MAX_DENSITY) * LOG2E * planes / total_planes


def pairs(count, start):
    swaps = []
    for i in range(start, count - 1, 2):
        swaps += [(i, i + 1), (i + 1, i)]
    return swaps


def exchange(cells, axis, dim):
    count = lax.axis_size(axis)
    odd = lax.axis_index(axis) % 2 == 1
    size = cells.shape[dim]
    head = lax.slice_in_dim(cells, 0, 1, axis=dim)
    tail = lax.slice_in_dim(cells, size - 1, size, axis=dim)
    near = lax.ppermute(jnp.where(odd, head, tail), axis, pairs(count, 0))
    far = lax.ppermute(jnp.where(odd, tail, head), axis, pairs(count, 1))
    return near, far


def tiles_of(value):
    return [value[:, t : t + LANES] for t in range(0, value.shape[1], LANES)]


def lane_next(tiles, lane):
    rolled = [pltpu.roll(v, LANES - 1, 1) for v in tiles] + [0.0]
    return [jnp.where(lane < LANES - 1, rolled[t], rolled[t + 1]) for t in range(len(tiles))]


def lane_previous(tiles, lane):
    rolled = [0.0] + [pltpu.roll(v, 1, 1) for v in tiles]
    return [jnp.where(lane > 0, rolled[t + 1], rolled[t]) for t in range(len(tiles))]


def lane_shift(tiles, lane, shift):
    amount = (LANES - shift) % LANES
    rolled = [pltpu.roll(v, amount, 1) for v in tiles] + [0.0]
    return [jnp.where(lane < LANES - shift, rolled[t], rolled[t + 1]) for t in range(len(tiles))]


def brick_kernel(
    bricks, density_ref, bins_ref, table_ref, plane_near, plane_far, row_near, row_far, out_ref
):
    planes, height, across = density_ref.shape
    total_planes = planes * bricks
    brick = lax.axis_index("depth")
    odd_brick = brick % 2 == 1
    odd_strip = lax.axis_index("strip") % 2 == 1
    count = across // LANES
    lane = lax.broadcasted_iota(jnp.int32, (height, LANES), 1)
    row = lax.broadcasted_iota(jnp.int32, (height, LANES), 0)
    f32 = jnp.float32

    near, far = plane_near[0].astype(f32), plane_far[0].astype(f32)
    beneath = tiles_of(jnp.where(odd_brick, near, far))
    overhead = tiles_of(jnp.where(odd_brick, far, near))
    near, far = row_near[:, 0, :].astype(f32), row_far[:, 0, :].astype(f32)
    above = jnp.where(odd_strip, near, far)
    below = jnp.where(odd_strip, far, near)
    stack = [beneath]
    stack += [tiles_of(density_ref[p].astype(f32)) for p in range(planes)]
    stack += [overhead]
    table = [
        jnp.broadcast_to(table_ref[c : c + 1, :], (height, LANES)) for c in range(4)
    ]
    table[0] = table[0] * (LOG2E / total_planes)

    depth = [jnp.zeros((height, LANES), f32)] * count
    colour = [[jnp.zeros((height, LANES), f32)] * count for _ in range(3)]
    for p in range(planes):
        plane_index = brick * planes + p
        shift = (3 * plane_index) // 8
        fraction = ((3 * plane_index) % 8).astype(f32) / 8.0
        centre = stack[p + 1]
        ahead, behind = lane_next(centre, lane), lane_previous(centre, lane)
        fields = [[], [], [], []]
        for t in range(count):
            cols = slice(t * LANES, (t + 1) * LANES)
            v = centre[t]
            up = jnp.where(row == 0, above[p : p + 1, cols], pltpu.roll(v, 1, 0))
            down = jnp.where(
                row == height - 1, below[p : p + 1, cols], pltpu.roll(v, height - 1, 0)
            )
            dx = ahead[t] - behind[t]
            dy = down - up
            dz = stack[p + 2][t] - stack[p][t]
            gain = SHADE_GAIN * LOG2E
            lit = (LIGHT[0] * gain) * dx + (LIGHT[1] * gain) * dy + (LIGHT[2] * gain) * dz
            shade = jnp.exp2(lit * lax.rsqrt(4.0 + dx * dx + dy * dy + dz * dz))
            bins = bins_ref[p, :, cols]
            looked = [
                jnp.take_along_axis(entry, bins, axis=1, mode="promise_in_bounds")
                for entry in table
            ]
            extinction = looked[0] * (1.0 + v * v)
            strength = (1.0 - jnp.exp2(-extinction)) * shade
            fields[0].append(extinction)
            for c in range(3):
                fields[c + 1].append(looked[c + 1] * strength)
        sheared = []
        for field in fields:
            first = lane_shift(field, lane, shift)
            second = lane_next(first, lane)
            sheared.append([a + fraction * (b - a) for a, b in zip(first, second)])
        for t in range(count):
            through = jnp.exp2(-depth[t])
            for c in range(3):
                colour[c][t] = colour[c][t] + through * sheared[c + 1][t]
            depth[t] = depth[t] + sheared[0][t]

    depth_factor = CODE_MAX / depth_scale(planes, total_planes)
    words = [[], []]
    for t in range(count):
        codes = [jnp.minimum(depth[t] * depth_factor, CODE_MAX)]
        for c in range(3):
            code = jnp.log2(colour[c][t]) * COLOUR_STEPS - COLOUR_LOW * COLOUR_STEPS
            codes.append(jnp.minimum(jnp.maximum(code, 0.0), CODE_MAX))
        codes = [(code + 0.5).astype(jnp.int32) for code in codes]
        words[0].append(codes[0] | (codes[1] << 16))
        words[1].append(codes[2] | (codes[3] << 16))
    owned = height * across // bricks
    tall, wide = max(owned // across, 1), min(owned, across)
    for owner in range(bricks):
        top, left = owner * owned // across, owner * owned % across
        for w in range(2):
            for t in range(wide // LANES):
                out_ref[owner, w, t * tall : (t + 1) * tall, :] = words[w][left // LANES + t][
                    top : top + tall, :
                ]


def merge_kernel(planes, tall, order_ref, words_ref, out_ref):
    bricks, _, rows, _ = words_ref.shape
    f32 = jnp.float32
    depth_unit = depth_scale(planes, planes * bricks) / CODE_MAX
    passed = jnp.zeros((rows, LANES), f32)
    colour = [jnp.zeros((rows, LANES), f32)] * 3
    for k in range(bricks):
        brick = order_ref[0, k]
        words = [words_ref[brick, 0], words_ref[brick, 1]]
        codes = []
        for word in words:
            codes += [word & 0xFFFF, lax.shift_right_logical(word, 16)]
        base = COLOUR_LOW - passed
        for c in range(3):
            code = codes[c + 1]
            term = jnp.exp2(code.astype(f32) * (1.0 / COLOUR_STEPS) + base)
            colour[c] = colour[c] + jnp.where(code > 0, term, 0.0)
        passed = passed + codes[0].astype(f32) * depth_unit
    image = colour + [jnp.exp2(-passed)]
    wide = rows // tall
    for c in range(4):
        for r in range(tall):
            for t in range(wide):
                at = (r * wide + t) * LANES
                out_ref[c : c + 1, at : at + LANES] = image[c][t * tall + r : t * tall + r + 1, :]


def per_device(density, tf_bins, tf_table, brick_order):
    planes, height, across = density.shape
    bricks = lax.axis_size("depth")
    plane_near, plane_far = exchange(density, "depth", 0)
    row_near, row_far = exchange(density, "strip", 1)
    owned = height * across // bricks
    table = jnp.pad(tf_table, ((0, 0), (0, LANES - tf_table.shape[1])))
    vmem = pl.BlockSpec(memory_space=pltpu.VMEM)
    words = pl.pallas_call(
        functools.partial(brick_kernel, bricks),
        out_shape=jax.ShapeDtypeStruct((bricks, 2, owned // LANES, LANES), jnp.int32),
        in_specs=[vmem] * 7,
        out_specs=vmem,
    )(density, tf_bins, table, plane_near, plane_far, row_near, row_far)
    words = lax.all_to_all(words, "depth", 0, 0, tiled=True)
    return pl.pallas_call(
        functools.partial(merge_kernel, planes, max(owned // across, 1)),
        out_shape=jax.ShapeDtypeStruct((4, owned), jnp.float32),
        in_specs=[pl.BlockSpec(memory_space=pltpu.SMEM), vmem],
        out_specs=vmem,
    )(brick_order, words)


def solution(mesh):
    in_specs = (P("depth", "strip", None), P("depth", "strip", None), P(), P("strip", None))
    out_specs = P(None, ("strip", "depth"))
    return jax.shard_map(
        per_device, mesh=mesh, in_specs=in_specs, out_specs=out_specs, check_vma=False
    )
```

time: 219 us -> 32.1 us (0.15)
  waiting for transfers between devices: 164 us -> 0.26 us
  between operations: 14.1 us -> 0.04 us
  blocking collectives: 0 us -> 12.4 us
  local copies, waits for them, and re-layouts: 12.5 us -> 1.82 us
  starting transfers between devices: 18.6 us -> 10.1 us
  other arithmetic: 8.32 us -> 1.69 us
  Pallas kernels: 0 us -> 5.41 us
    unnamed x2 -> x0, waiting for transfers between devices: 147 us -> none
    all_to_all x2 -> x0, waiting for transfers between devices: 12.9 us -> none  [the longest x1 6.64 us: per_device(): lax.all_to_all(flat_depth.astype(jnp.bfloat16), 'depth', split_axis=1, co...]
    all_to_all x0 -> x1, blocking collectives: none -> 12.4 us  [per_device(): words = lax.all_to_all(words, 'depth', 0, 0, tiled=True)]
    all_to_all x2 -> x0, starting transfers between devices: 9.04 us -> none  [the longest x1 5.7 us: per_device(): lax.all_to_all(flat_depth.astype(jnp.bfloat16), 'depth', split_axis=1, co...]
    unnamed x12 -> x10, local copies, waits for them, and re-layouts: 9.41 us -> 1.24 us
    pallas_call x0 -> x2, Pallas kernels: none -> 5.41 us  [the longest x1 3.8 us: per_device(): pl.pallas_call(functools.partial(brick_kernel, bricks), out_shape=jax.Sha...]
    ppermute x4, waiting for transfers between devices: 3.25 us -> 0.26 us  [the longest x2 0.25 us: exchange(): near = lax.ppermute(jnp.where(odd, head, tail), axis, pairs(count, 0))]
    add x5 -> x0, other arithmetic: 2.2 us -> none  [the longest x4 1.87 us: shear_plane(): return (1.0 - fraction) * first + fraction * second]
  transfers between devices with their start and end apart: 7 -> 4, of which waited for: 4 -> 1; matrix products, arithmetic and copies ran while one was open for 2% -> 5% of each run, Pallas kernels for 0% -> 0%
where the time goes in v1:
time: 32.1 us; the launch traced here: 31.7 us
  blocking collectives  12.4 us (39%)
  starting transfers between devices  10.1 us (31%)
  Pallas kernels  5.41 us (17%)
  local copies, waits for them, and re-layouts  1.82 us (6%)
  other arithmetic  1.69 us (5%)
    all_to_all x1, blocking collectives, per_device(): words = lax.all_to_all(words, 'depth', 0, 0, tiled=True)  12.4 us
    ppermute x2, starting transfers between devices, exchange(): near = lax.ppermute(jnp.where(odd, head, tail), axis, pairs(count, 0))  8.74 us
    pallas_call x1, Pallas kernels, per_device(): pl.pallas_call(functools.partial(brick_kernel, bricks), out_shape=jax.Sha...  3.8 us
    select_n x2, other arithmetic, exchange(): far = lax.ppermute(jnp.where(odd, tail, head), axis, pairs(count, 1))  1.69 us
    pallas_call x1, Pallas kernels, per_device(): pl.pallas_call(functools.partial(merge_kernel, planes, max(owned // acros...  1.61 us
    ppermute x2, starting transfers between devices, exchange(): far = lax.ppermute(jnp.where(odd, tail, head), axis, pairs(count, 1))  1.32 us
    unnamed x10, local copies, waits for them, and re-layouts  1.24 us
  transfers between devices with their start and end apart: 4, of which 1 were waited for; matrix products, arithmetic and copies ran while one was open for 5% of the time, Pallas kernels for 0%

profile of v1, /device:TPU:0, one launch (start us, length us, event | category | flops | bytes accessed | tf_op | source)
XLA Modules:
  0.0 31.7 jit_solution(3946384580993777489)
XLA Ops:
  0.0 0.8 %broadcast_select_fusion.2 = (bf16[1,16,1024]{2,1,0:T(8,128)(2,1)S(1)}, bf16[1,16,1024]{2,1,0:T(8,128)(2,1)S(1)}) fusion(pred[]{:T(512)S(6)} %eq.9, bf16[4,16,1024]{2,1,0:T(8,128)(2,1)} %density_ref.1), kind=kLoop, calls=%fused_computation.2 | loop fusion | flops 32768 | bytes 131073 | tf_op jit(solution)/shard_map/jit(_where)/select_n | solution.py:41
  0.8 0.7 %collective-permute-start.1 = (bf16[1,16,1024]{2,1,0:T(8,128)(2,1)S(1)}, bf16[1,16,1024]{2,1,0:T(8,128)(2,1)S(1)}, u32[]{:S(2)}, u32[]{:S(2)}) collective-permute-start(bf16[1,16,1024]{2,1,0:T(8,128)(2,1)S(1)} %get-tuple-element.7), channel_id=1, source_target_pairs={{4,8},{8,4},{12,16},{16,12},{20,24},{24,20},{5,9},{9,5},{13,17},{1... | collective-permute-start | bytes 98312 | tf_op jit(solution)/shard_map/ppermute | solution.py:41
  1.4 5.8 %collective-permute-start = (bf16[1,16,1024]{2,1,0:T(8,128)(2,1)S(1)}, bf16[1,16,1024]{2,1,0:T(8,128)(2,1)S(1)}, u32[]{:S(2)}, u32[]{:S(2)}) collective-permute-start(bf16[1,16,1024]{2,1,0:T(8,128)(2,1)S(1)} %get-tuple-element.8), channel_id=1, source_target_pairs={{0,4},{4,0},{8,12},{12,8},{16,20},{20,16},{24,28},{28,24},{1,5},{5... | collective-permute-start | bytes 98312 | tf_op jit(solution)/shard_map/ppermute | solution.py:40
  7.2 0.9 %broadcast_select_fusion = (bf16[4,1,1024]{2,1,0:T(2,128)(2,1)S(1)}, bf16[4,1,1024]{2,1,0:T(2,128)(2,1)S(1)}) fusion(pred[]{:T(512)S(6)} %eq.10, bf16[4,16,1024]{2,1,0:T(8,128)(2,1)} %density_ref.1), kind=kLoop, calls=%fused_computation | loop fusion | flops 8192 | bytes 32769 | tf_op jit(solution)/shard_map/jit(_where)/select_n | solution.py:41
  8.2 0.0 copy-start.4
  8.2 0.7 %collective-permute-start.3 = (bf16[4,1,1024]{2,1,0:T(2,128)(2,1)S(1)}, bf16[4,1,1024]{2,1,0:T(2,128)(2,1)S(1)}, u32[]{:S(2)}, u32[]{:S(2)}) collective-permute-start(bf16[4,1,1024]{2,1,0:T(2,128)(2,1)S(1)} %get-tuple-element.5), channel_id=1, source_target_pairs={{1,2},{2,1},{5,6},{6,5},{9,10},{10,9},{13,14},{14,13},{17,18},{18,... | collective-permute-start | bytes 24584 | tf_op jit(solution)/shard_map/ppermute | solution.py:41
  8.8 2.9 %collective-permute-start.2 = (bf16[4,1,1024]{2,1,0:T(2,128)(2,1)S(1)}, bf16[4,1,1024]{2,1,0:T(2,128)(2,1)S(1)}, u32[]{:S(2)}, u32[]{:S(2)}) collective-permute-start(bf16[4,1,1024]{2,1,0:T(2,128)(2,1)S(1)} %get-tuple-element.6), channel_id=1, source_target_pairs={{0,1},{1,0},{2,3},{3,2},{4,5},{5,4},{6,7},{7,6},{8,9},{9,8},{10,11... | collective-permute-start | bytes 24584 | tf_op jit(solution)/shard_map/ppermute | solution.py:40
  11.8 0.0 copy-done.4
  11.8 0.6 %pad.4.table_ref = f32[4,128]{1,0:T(4,128)} pad(f32[4,16]{1,0:T(4,128)S(1)} %copy-done.4, f32[]{:T(128)} %constant.23.clone.1), padding=0_0x0_112 | pad | bytes 2308 | tf_op jit(solution)/shard_map/jit(_pad)/pad | solution.py:189
  12.4 0.0 collective-permute-done.3.row_far
  12.4 0.0 copy-start.2
  12.4 0.3 collective-permute-done.2.row_near
  12.6 0.0 copy-start.3
  12.6 0.0 collective-permute-done.1.plane_far
  12.6 0.0 copy-start
  12.6 0.0 collective-permute-done.plane_near
  12.6 0.3 %copy-done.2 = bf16[4,1,1024]{2,1,0:T(2,128)(2,1)} copy-done((bf16[4,1,1024]{2,1,0:T(2,128)(2,1)}, bf16[4,1,1024]{2,1,0:T(2,128)(2,1)S(1)}, u32[]{:S(2)}) %copy-start.2) | copy-done | bytes 8216
  13.0 0.2 copy-done.3
  13.2 0.0 copy-done
  13.3 0.0 copy-start.1
  13.3 0.6 %copy-done.1 = bf16[1,16,1024]{2,1,0:T(8,128)(2,1)} copy-done((bf16[1,16,1024]{2,1,0:T(8,128)(2,1)}, bf16[1,16,1024]{2,1,0:T(8,128)(2,1)S(1)}, u32[]{:S(2)}) %copy-start.1) | copy-done | bytes 32792
  13.9 3.8 %shard_map.46 = s32[8,2,16,128]{3,2,1,0:T(8,128)} custom-call(bf16[4,16,1024]{2,1,0:T(8,128)(2,1)} %density_ref.1, s32[4,16,1024]{2,1,0:T(8,128)} %bins_ref.1, f32[4,128]{1,0:T(4,128)} %pad.4.table_ref, bf16[1,16,1024]{2,1,0:T(8,128)(2,1)} %copy-done.1, bf16[1,16,1024]{2,1,0:T(8,128)(2,1)} %copy-done, bf16[4,1,1024]{2,1,0:T(2,128)(2,1)} %copy-done.3, ...), custom_call_target="tpu_custom_call" | custom-call | tf_op jit(solution)/shard_map/pallas_call | solution.py:191
  17.7 12.4 %all_to_all.5.words_ref = s32[8,2,16,128]{3,2,1,0:T(8,128)} all-to-all(s32[8,2,16,128]{3,2,1,0:T(8,128)} %shard_map.46), channel_id=1, replica_groups=mesh['depth'=8,'strip'=4] {'depth'}, dimensions={0} | all-to-all | bytes 262144 | tf_op jit(solution)/shard_map/all_to_all | solution.py:197
  30.1 1.6 %shard_map.47 = f32[4,2048]{1,0:T(4,128)} custom-call(s32[1,8]{1,0:T(1,128)} %order_ref.1, s32[8,2,16,128]{3,2,1,0:T(8,128)} %all_to_all.5.words_ref), custom_call_target="tpu_custom_call" | custom-call | tf_op jit(solution)/shard_map/pallas_call | solution.py:198
Async XLA Ops:
  0.8 11.8 %collective-permute-start.1 = (bf16[1,16,1024]{2,1,0:T(8,128)(2,1)S(1)}, bf16[1,16,1024]{2,1,0:T(8,128)(2,1)S(1)}, u32[]{:S(2)}, u32[]{:S(2)}) collective-permute-start(bf16[1,16,1024]{2,1,0:T(8,128)(2,1)S(1)} %get-tuple-element.7), channel_id=1, source_target_pairs={{4,8},{8,4},{12,16},{16,12},{20,24},{24,20},{5,9},{9,5},{13,17},{1... | collective-permute-start | bytes 98312 | tf_op jit(solution)/shard_map/ppermute | solution.py:41
  1.4 11.2 %collective-permute-start = (bf16[1,16,1024]{2,1,0:T(8,128)(2,1)S(1)}, bf16[1,16,1024]{2,1,0:T(8,128)(2,1)S(1)}, u32[]{:S(2)}, u32[]{:S(2)}) collective-permute-start(bf16[1,16,1024]{2,1,0:T(8,128)(2,1)S(1)} %get-tuple-element.8), channel_id=1, source_target_pairs={{0,4},{4,0},{8,12},{12,8},{16,20},{20,16},{24,28},{28,24},{1,5},{5... | collective-permute-start | bytes 98312 | tf_op jit(solution)/shard_map/ppermute | solution.py:40
  8.2 3.6 %copy-start.4 = (f32[4,16]{1,0:T(4,128)S(1)}, f32[4,16]{1,0:T(4,128)}, u32[]{:S(2)}) copy-start(f32[4,16]{1,0:T(4,128)} %param.6) | copy-start | bytes 772
  8.2 4.2 %collective-permute-start.3 = (bf16[4,1,1024]{2,1,0:T(2,128)(2,1)S(1)}, bf16[4,1,1024]{2,1,0:T(2,128)(2,1)S(1)}, u32[]{:S(2)}, u32[]{:S(2)}) collective-permute-start(bf16[4,1,1024]{2,1,0:T(2,128)(2,1)S(1)} %get-tuple-element.5), channel_id=1, source_target_pairs={{1,2},{2,1},{5,6},{6,5},{9,10},{10,9},{13,14},{14,13},{17,18},{18,... | collective-permute-start | bytes 24584 | tf_op jit(solution)/shard_map/ppermute | solution.py:41
  8.8 3.8 %collective-permute-start.2 = (bf16[4,1,1024]{2,1,0:T(2,128)(2,1)S(1)}, bf16[4,1,1024]{2,1,0:T(2,128)(2,1)S(1)}, u32[]{:S(2)}, u32[]{:S(2)}) collective-permute-start(bf16[4,1,1024]{2,1,0:T(2,128)(2,1)S(1)} %get-tuple-element.6), channel_id=1, source_target_pairs={{0,1},{1,0},{2,3},{3,2},{4,5},{5,4},{6,7},{7,6},{8,9},{9,8},{10,11... | collective-permute-start | bytes 24584 | tf_op jit(solution)/shard_map/ppermute | solution.py:40
  12.4 0.6 %copy-start.2 = (bf16[4,1,1024]{2,1,0:T(2,128)(2,1)}, bf16[4,1,1024]{2,1,0:T(2,128)(2,1)S(1)}, u32[]{:S(2)}) copy-start(bf16[4,1,1024]{2,1,0:T(2,128)(2,1)S(1)} %collective-permute-done.3.row_far) | copy-start | bytes 24580
  12.6 0.6 %copy-start.3 = (bf16[4,1,1024]{2,1,0:T(2,128)(2,1)}, bf16[4,1,1024]{2,1,0:T(2,128)(2,1)S(1)}, u32[]{:S(2)}) copy-start(bf16[4,1,1024]{2,1,0:T(2,128)(2,1)S(1)} %collective-permute-done.2.row_near) | copy-start | bytes 24580
  12.6 0.6 %copy-start = (bf16[1,16,1024]{2,1,0:T(8,128)(2,1)}, bf16[1,16,1024]{2,1,0:T(8,128)(2,1)S(1)}, u32[]{:S(2)}) copy-start(bf16[1,16,1024]{2,1,0:T(8,128)(2,1)S(1)} %collective-permute-done.1.plane_far) | copy-start | bytes 98308
  13.3 0.6 %copy-start.1 = (bf16[1,16,1024]{2,1,0:T(8,128)(2,1)}, bf16[1,16,1024]{2,1,0:T(8,128)(2,1)S(1)}, u32[]{:S(2)}) copy-start(bf16[1,16,1024]{2,1,0:T(8,128)(2,1)S(1)} %collective-permute-done.plane_near) | copy-start | bytes 98308

commit v2 on v1

--- a/solution.py
+++ b/solution.py
@@ -11,6 +11,7 @@
 SHADE_GAIN = 1.5
 LOG2E = 1.4426950408889634
 LANES = 128
+VMEM_BYTES = 8 * 1024 * 1024
 
 MAX_DENSITY = 6.0
 MAX_LOOKED = 2.0
@@ -193,6 +194,7 @@
         out_shape=jax.ShapeDtypeStruct((bricks, 2, owned // LANES, LANES), jnp.int32),
         in_specs=[vmem] * 7,
         out_specs=vmem,
+        compiler_params=pltpu.CompilerParams(vmem_limit_bytes=VMEM_BYTES),
     )(density, tf_bins, table, plane_near, plane_far, row_near, row_far)
     words = lax.all_to_all(words, "depth", 0, 0, tiled=True)
     return pl.pallas_call(
@@ -200,6 +202,7 @@
         out_shape=jax.ShapeDtypeStruct((4, owned), jnp.float32),
         in_specs=[pl.BlockSpec(memory_space=pltpu.SMEM), vmem],
         out_specs=vmem,
+        compiler_params=pltpu.CompilerParams(vmem_limit_bytes=VMEM_BYTES),
     )(brick_order, words)
 
 

time: 32.1 us -> 28.5 us (0.89)
  Pallas kernels: 5.41 us -> 3.37 us
  local copies, waits for them, and re-layouts: 1.82 us -> 0.97 us
  other arithmetic: 1.69 us -> 0.88 us
  waiting for transfers between devices: 0.26 us -> 0.83 us
    pallas_call x1, Pallas kernels: 3.8 us -> 2.14 us  [per_device(): pl.pallas_call(functools.partial(brick_kernel, bricks), out_shape=jax.Sha...]
    select_n x2, other arithmetic: 1.69 us -> 0.88 us  [exchange(): far = lax.ppermute(jnp.where(odd, tail, head), axis, pairs(count, 1))]
    ppermute x2, waiting for transfers between devices: 0.25 us -> 0.83 us  [exchange(): near = lax.ppermute(jnp.where(odd, head, tail), axis, pairs(count, 0))]
    pad x1, local copies, waits for them, and re-layouts: 0.58 us -> 0.01 us  [per_device(): table = jnp.pad(tf_table, ((0, 0), (0, LANES - tf_table.shape[1])))]
    pallas_call x1, Pallas kernels: 1.61 us -> 1.24 us  [per_device(): pl.pallas_call(functools.partial(merge_kernel, planes, max(owned // acros...]
    unnamed x10 -> x8, local copies, waits for them, and re-layouts: 1.24 us -> 0.97 us
  transfers between devices with their start and end apart: 4 -> 4, of which waited for: 1 -> 1; matrix products, arithmetic and copies ran while one was open for 5% -> 0% of each run, Pallas kernels for 0% -> 0%
where the time goes in v2:
time: 28.5 us; the launch traced here: 28.3 us
  blocking collectives  12.1 us (42%)
  starting transfers between devices  10.1 us (35%)
  Pallas kernels  3.37 us (12%)
  local copies, waits for them, and re-layouts  0.97 us (3%)
  other arithmetic  0.88 us (3%)
  waiting for transfers between devices  0.83 us (3%)
    all_to_all x1, blocking collectives, per_device(): words = lax.all_to_all(words, 'depth', 0, 0, tiled=True)  12.1 us
    ppermute x2, starting transfers between devices, exchange(): near = lax.ppermute(jnp.where(odd, head, tail), axis, pairs(count, 0))  8.74 us
    pallas_call x1, Pallas kernels, per_device(): pl.pallas_call(functools.partial(brick_kernel, bricks), out_shape=jax.Sha...  2.14 us
    ppermute x2, starting transfers between devices, exchange(): far = lax.ppermute(jnp.where(odd, tail, head), axis, pairs(count, 1))  1.33 us
    pallas_call x1, Pallas kernels, per_device(): pl.pallas_call(functools.partial(merge_kernel, planes, max(owned // acros...  1.24 us
    unnamed x8, local copies, waits for them, and re-layouts  0.97 us
    select_n x2, other arithmetic, exchange(): far = lax.ppermute(jnp.where(odd, tail, head), axis, pairs(count, 1))  0.88 us
    ppermute x2, waiting for transfers between devices, exchange(): near = lax.ppermute(jnp.where(odd, head, tail), axis, pairs(count, 0))  0.83 us
  transfers between devices with their start and end apart: 4, of which 1 were waited for; matrix products, arithmetic and copies ran while one was open for 0% of the time, Pallas kernels for 0%

profile of v2, /device:TPU:0, one launch (start us, length us, event | category | flops | bytes accessed | tf_op | source)
XLA Modules:
  0.0 28.3 jit_solution(16251682404508656108)
XLA Ops:
  0.0 0.0 copy-start
  0.0 0.8 %broadcast_select_fusion.2 = (bf16[1,16,1024]{2,1,0:T(8,128)(2,1)S(1)}, bf16[1,16,1024]{2,1,0:T(8,128)(2,1)S(1)}) fusion(pred[]{:T(512)S(6)} %eq.9, bf16[4,16,1024]{2,1,0:T(8,128)(2,1)} %density_ref.1), kind=kLoop, calls=%fused_computation.2 | loop fusion | flops 32768 | bytes 131073 | tf_op jit(solution)/shard_map/jit(_where)/select_n | solution.py:42
  0.8 0.7 %collective-permute-start.1 = (bf16[1,16,1024]{2,1,0:T(8,128)(2,1)S(1)}, bf16[1,16,1024]{2,1,0:T(8,128)(2,1)S(1)}, u32[]{:S(2)}, u32[]{:S(2)}) collective-permute-start(bf16[1,16,1024]{2,1,0:T(8,128)(2,1)S(1)} %get-tuple-element.7), channel_id=1, source_target_pairs={{4,8},{8,4},{12,16},{16,12},{20,24},{24,20},{5,9},{9,5},{13,17},{1... | collective-permute-start | bytes 98312 | tf_op jit(solution)/shard_map/ppermute | solution.py:42
  1.5 5.8 %collective-permute-start = (bf16[1,16,1024]{2,1,0:T(8,128)(2,1)S(1)}, bf16[1,16,1024]{2,1,0:T(8,128)(2,1)S(1)}, u32[]{:S(2)}, u32[]{:S(2)}) collective-permute-start(bf16[1,16,1024]{2,1,0:T(8,128)(2,1)S(1)} %get-tuple-element.8), channel_id=1, source_target_pairs={{0,4},{4,0},{8,12},{12,8},{16,20},{20,16},{24,28},{28,24},{1,5},{5... | collective-permute-start | bytes 98312 | tf_op jit(solution)/shard_map/ppermute | solution.py:41
  7.3 0.0 copy-done
  7.4 0.0 copy-start.3
  7.4 0.7 %collective-permute-start.3 = (bf16[4,1,1024]{2,1,0:T(2,128)(2,1)S(1)}, bf16[4,1,1024]{2,1,0:T(2,128)(2,1)S(1)}, u32[]{:S(2)}, u32[]{:S(2)}) collective-permute-start(bf16[4,1,1024]{2,1,0:T(2,128)(2,1)S(1)} %get-tuple-element.5), channel_id=1, source_target_pairs={{1,2},{2,1},{5,6},{6,5},{9,10},{10,9},{13,14},{14,13},{17,18},{18,... | collective-permute-start | bytes 24584 | tf_op jit(solution)/shard_map/ppermute | solution.py:42
  8.0 2.9 %collective-permute-start.2 = (bf16[4,1,1024]{2,1,0:T(2,128)(2,1)S(1)}, bf16[4,1,1024]{2,1,0:T(2,128)(2,1)S(1)}, u32[]{:S(2)}, u32[]{:S(2)}) collective-permute-start(bf16[4,1,1024]{2,1,0:T(2,128)(2,1)S(1)} %get-tuple-element.6), channel_id=1, source_target_pairs={{0,1},{1,0},{2,3},{3,2},{4,5},{5,4},{6,7},{7,6},{8,9},{9,8},{10,11... | collective-permute-start | bytes 24584 | tf_op jit(solution)/shard_map/ppermute | solution.py:41
  11.0 0.0 copy-done.3
  11.0 0.0 collective-permute-done.3.row_far
  11.0 0.8 %collective-permute-done.2.row_near = bf16[4,1,1024]{2,1,0:T(2,128)(2,1)S(1)} collective-permute-done((bf16[4,1,1024]{2,1,0:T(2,128)(2,1)S(1)}, bf16[4,1,1024]{2,1,0:T(2,128)(2,1)S(1)}, u32[]{:S(2)}, u32[]{:S(2)}) %collective-permute-start.2) | collective-permute-done | bytes 8224 | tf_op jit(solution)/shard_map/ppermute | solution.py:41
  11.8 0.0 collective-permute-done.1.plane_far
  11.8 0.0 collective-permute-done.plane_near
  11.8 0.0 copy-start.1
  11.8 0.9 %copy-done.1 = s32[4,16,1024]{2,1,0:T(8,128)S(1)} copy-done((s32[4,16,1024]{2,1,0:T(8,128)S(1)}, s32[4,16,1024]{2,1,0:T(8,128)}, u32[]{:S(2)}) %copy-start.1) | copy-done | bytes 262168
  12.8 2.1 %shard_map.46 = s32[8,2,16,128]{3,2,1,0:T(8,128)S(1)} custom-call(bf16[4,16,1024]{2,1,0:T(8,128)(2,1)S(1)} %copy-done, s32[4,16,1024]{2,1,0:T(8,128)S(1)} %copy-done.1, f32[4,128]{1,0:T(4,128)S(1)} %pad.4.table_ref, bf16[1,16,1024]{2,1,0:T(8,128)(2,1)S(1)} %collective-permute-done.plane_near, bf16[1,16,1024]{2,1,0:T(8,128)(2,1)S(1)} %collective-permute-done.1.plane_far, ...), custom_call_target="tpu_custom_call" | custom-call | tf_op jit(solution)/shard_map/pallas_call | solution.py:192
  14.9 0.0 copy-start.2
  14.9 12.1 %all_to_all.5.words_ref = s32[8,2,16,128]{3,2,1,0:T(8,128)S(1)} all-to-all(s32[8,2,16,128]{3,2,1,0:T(8,128)S(1)} %shard_map.46), channel_id=1, replica_groups=mesh['depth'=8,'strip'=4] {'depth'}, dimensions={0} | all-to-all | bytes 262144 | tf_op jit(solution)/shard_map/all_to_all | solution.py:199
  27.1 0.0 copy-done.2
  27.1 1.2 %shard_map.47 = f32[4,2048]{1,0:T(4,128)} custom-call(s32[1,8]{1,0:T(1,128)S(1)} %copy-done.2, s32[8,2,16,128]{3,2,1,0:T(8,128)S(1)} %all_to_all.5.words_ref), custom_call_target="tpu_custom_call" | custom-call | tf_op jit(solution)/shard_map/pallas_call | solution.py:200
  (2 shorter events, 0.0 us)
Async XLA Ops:
  0.0 7.3 %copy-start = (bf16[4,16,1024]{2,1,0:T(8,128)(2,1)S(1)}, bf16[4,16,1024]{2,1,0:T(8,128)(2,1)}, u32[]{:S(2)}) copy-start(bf16[4,16,1024]{2,1,0:T(8,128)(2,1)} %density_ref.1) | copy-start | bytes 393220
  0.8 11.0 %collective-permute-start.1 = (bf16[1,16,1024]{2,1,0:T(8,128)(2,1)S(1)}, bf16[1,16,1024]{2,1,0:T(8,128)(2,1)S(1)}, u32[]{:S(2)}, u32[]{:S(2)}) collective-permute-start(bf16[1,16,1024]{2,1,0:T(8,128)(2,1)S(1)} %get-tuple-element.7), channel_id=1, source_target_pairs={{4,8},{8,4},{12,16},{16,12},{20,24},{24,20},{5,9},{9,5},{13,17},{1... | collective-permute-start | bytes 98312 | tf_op jit(solution)/shard_map/ppermute | solution.py:42
  1.5 10.3 %collective-permute-start = (bf16[1,16,1024]{2,1,0:T(8,128)(2,1)S(1)}, bf16[1,16,1024]{2,1,0:T(8,128)(2,1)S(1)}, u32[]{:S(2)}, u32[]{:S(2)}) collective-permute-start(bf16[1,16,1024]{2,1,0:T(8,128)(2,1)S(1)} %get-tuple-element.8), channel_id=1, source_target_pairs={{0,4},{4,0},{8,12},{12,8},{16,20},{20,16},{24,28},{28,24},{1,5},{5... | collective-permute-start | bytes 98312 | tf_op jit(solution)/shard_map/ppermute | solution.py:41
  7.4 3.6 %copy-start.3 = (f32[4,16]{1,0:T(4,128)S(1)}, f32[4,16]{1,0:T(4,128)}, u32[]{:S(2)}) copy-start(f32[4,16]{1,0:T(4,128)} %param.6) | copy-start | bytes 772
  7.4 3.6 %collective-permute-start.3 = (bf16[4,1,1024]{2,1,0:T(2,128)(2,1)S(1)}, bf16[4,1,1024]{2,1,0:T(2,128)(2,1)S(1)}, u32[]{:S(2)}, u32[]{:S(2)}) collective-permute-start(bf16[4,1,1024]{2,1,0:T(2,128)(2,1)S(1)} %get-tuple-element.5), channel_id=1, source_target_pairs={{1,2},{2,1},{5,6},{6,5},{9,10},{10,9},{13,14},{14,13},{17,18},{18,... | collective-permute-start | bytes 24584 | tf_op jit(solution)/shard_map/ppermute | solution.py:42
  8.0 3.8 %collective-permute-start.2 = (bf16[4,1,1024]{2,1,0:T(2,128)(2,1)S(1)}, bf16[4,1,1024]{2,1,0:T(2,128)(2,1)S(1)}, u32[]{:S(2)}, u32[]{:S(2)}) collective-permute-start(bf16[4,1,1024]{2,1,0:T(2,128)(2,1)S(1)} %get-tuple-element.6), channel_id=1, source_target_pairs={{0,1},{1,0},{2,3},{3,2},{4,5},{5,4},{6,7},{7,6},{8,9},{9,8},{10,11... | collective-permute-start | bytes 24584 | tf_op jit(solution)/shard_map/ppermute | solution.py:41
  11.8 1.0 %copy-start.1 = (s32[4,16,1024]{2,1,0:T(8,128)S(1)}, s32[4,16,1024]{2,1,0:T(8,128)}, u32[]{:S(2)}) copy-start(s32[4,16,1024]{2,1,0:T(8,128)} %bins_ref.1) | copy-start | bytes 786436
  14.9 12.1 %copy-start.2 = (s32[1,8]{1,0:T(1,128)S(1)}, s32[1,8]{1,0:T(1,128)}, u32[]{:S(2)}) copy-start(s32[1,8]{1,0:T(1,128)} %order_ref.1) | copy-start | bytes 100

commit v3 on v1

v3 whole, which is shorter than its diff:
```python
import functools

import jax
import jax.numpy as jnp
from jax import lax
from jax.experimental import pallas as pl
from jax.experimental.pallas import tpu as pltpu
from jax.sharding import PartitionSpec as P

LIGHT = (0.36, 0.48, 0.8)
SHADE_GAIN = 1.5
LOG2E = 1.4426950408889634
LANES = 128
VMEM_BYTES = 8 * 1024 * 1024

MAX_DENSITY = 6.0
MAX_LOOKED = 2.0

COLOUR_STEPS = 2048.0
COLOUR_LOW = -28.0
CODE_MAX = 65535.0


def depth_scale(planes, total_planes):
    return MAX_LOOKED * (1.0 + MAX_DENSITY * MAX_DENSITY) * LOG2E * planes / total_planes


def pairs(count, start):
    swaps = []
    for i in range(start, count - 1, 2):
        swaps += [(i, i + 1), (i + 1, i)]
    return swaps


def edges_kernel(density_ref, plane_near, plane_far, row_near, row_far):
    planes, height, _ = density_ref.shape
    odd_brick = lax.axis_index("depth") % 2
    odd_strip = lax.axis_index("strip") % 2 == 1
    plane_near[...] = density_ref[pl.ds((1 - odd_brick) * (planes - 1), 1)]
    plane_far[...] = density_ref[pl.ds(odd_brick * (planes - 1), 1)]
    head, tail = density_ref[:, 0, :], density_ref[:, height - 1, :]
    row_near[:, 0, :] = jnp.where(odd_strip, head, tail)
    row_far[:, 0, :] = jnp.where(odd_strip, tail, head)


def swap(cells, axis, start):
    return lax.ppermute(cells, axis, pairs(lax.axis_size(axis), start))


def tiles_of(value):
    return [value[:, t : t + LANES] for t in range(0, value.shape[1], LANES)]


def lane_next(tiles, lane):
    rolled = [pltpu.roll(v, LANES - 1, 1) for v in tiles] + [0.0]
    return [jnp.where(lane < LANES - 1, rolled[t], rolled[t + 1]) for t in range(len(tiles))]


def lane_previous(tiles, lane):
    rolled = [0.0] + [pltpu.roll(v, 1, 1) for v in tiles]
    return [jnp.where(lane > 0, rolled[t + 1], rolled[t]) for t in range(len(tiles))]


def lane_shift(tiles, lane, shift, beyond):
    amount = (LANES - shift) % LANES
    rolled = [pltpu.roll(v, amount, 1) for v in tiles] + [beyond]
    return [jnp.where(lane < LANES - shift, rolled[t], rolled[t + 1]) for t in range(len(tiles))]


def light_kernel(
    bricks,
    density_ref,
    bins_ref,
    table_ref,
    order_ref,
    first_ref,
    second_ref,
    depth_ref,
    before_ref,
):
    planes, height, across = density_ref.shape
    total_planes = planes * bricks
    count = across // LANES
    f32 = jnp.float32
    lane = lax.broadcasted_iota(jnp.int32, (height, LANES), 1)
    table = [jnp.broadcast_to(table_ref[c : c + 1, :], (height, LANES)) for c in range(4)]
    table[0] = table[0] * (LOG2E / total_planes)
    depth = [jnp.zeros((height, LANES), f32)] * count
    for p in range(planes):
        plane_index = lax.axis_index("depth") * planes + p
        shift = (3 * plane_index) // 8
        fraction = ((3 * plane_index) % 8).astype(f32) / 8.0
        cells = lane_shift(tiles_of(density_ref[p].astype(f32)), lane, shift, 0.0)
        bins = lane_shift(tiles_of(bins_ref[p]), lane, shift, LANES - 1)
        fields = [[], [], [], []]
        for t in range(count):
            looked = [
                jnp.take_along_axis(entry, bins[t], axis=1, mode="promise_in_bounds")
                for entry in table
            ]
            extinction = looked[0] * (1.0 + cells[t] * cells[t])
            opacity = 1.0 - jnp.exp2(-extinction)
            fields[0].append(extinction)
            for c in range(3):
                fields[c + 1].append(looked[c + 1] * opacity)
        after = [lane_next(field, lane) for field in fields]
        for t in range(count):
            cols = slice(t * LANES, (t + 1) * LANES)
            through = jnp.exp2(-depth[t])
            through_second = through * fraction
            through_first = through - through_second
            for c in range(3):
                first_ref[p, c, :, cols] = through_first * fields[c + 1][t]
                second_ref[p, c, :, cols] = through_second * after[c + 1][t]
            depth[t] = depth[t] + (
                fields[0][t] + fraction * (after[0][t] - fields[0][t])
            )
    depth_factor = CODE_MAX / depth_scale(planes, total_planes)
    for t in range(count):
        code = jnp.minimum(depth[t] * depth_factor, CODE_MAX)
        depth_ref[:, t * LANES : (t + 1) * LANES] = (code + 0.5).astype(jnp.int32)
    slot = lax.broadcasted_iota(jnp.int32, (bricks, LANES), 0)
    place = jnp.zeros((bricks, LANES), jnp.int32)
    for k in range(bricks):
        place = jnp.where(slot == order_ref[0, k], k, place)
    for b in range(bricks):
        before_ref[b] = (place < place[b : b + 1, :]).astype(f32)


def shade_kernel(
    bricks,
    plane_far,
    plane_near,
    row_near,
    row_far,
    density_ref,
    first_ref,
    second_ref,
    depth_ref,
    out_ref,
):
    planes, height, across = density_ref.shape
    count = across // LANES
    f32 = jnp.float32
    odd_brick = lax.axis_index("depth") % 2 == 1
    odd_strip = lax.axis_index("strip") % 2 == 1
    lane = lax.broadcasted_iota(jnp.int32, (height, LANES), 1)
    row = lax.broadcasted_iota(jnp.int32, (height, LANES), 0)
    near, far = plane_near[0].astype(f32), plane_far[0].astype(f32)
    beneath = tiles_of(jnp.where(odd_brick, near, far))
    overhead = tiles_of(jnp.where(odd_brick, far, near))
    near, far = row_near[:, 0, :].astype(f32), row_far[:, 0, :].astype(f32)
    above = jnp.where(odd_strip, near, far)
    below = jnp.where(odd_strip, far, near)
    stack = [beneath]
    stack += [tiles_of(density_ref[p].astype(f32)) for p in range(planes)]
    stack += [overhead]
    gain = SHADE_GAIN * LOG2E
    colour = [[None] * count for _ in range(3)]
    for p in range(planes):
        shift = (3 * (lax.axis_index("depth") * planes + p)) // 8
        centre = stack[p + 1]
        ahead, behind = lane_next(centre, lane), lane_previous(centre, lane)
        shade = []
        for t in range(count):
            cols = slice(t * LANES, (t + 1) * LANES)
            v = centre[t]
            up = jnp.where(row == 0, above[p : p + 1, cols], pltpu.roll(v, 1, 0))
            down = jnp.where(
                row == height - 1, below[p : p + 1, cols], pltpu.roll(v, height - 1, 0)
            )
            dx = ahead[t] - behind[t]
            dy = down - up
            dz = stack[p + 2][t] - stack[p][t]
            lit = (LIGHT[0] * gain) * dx + (LIGHT[1] * gain) * dy + (LIGHT[2] * gain) * dz
            shade.append(jnp.exp2(lit * lax.rsqrt(4.0 + dx * dx + dy * dy + dz * dz)))
        shade = lane_shift(shade, lane, shift, 0.0)
        after = lane_next(shade, lane)
        for t in range(count):
            cols = slice(t * LANES, (t + 1) * LANES)
            for c in range(3):
                term = first_ref[p, c, :, cols] * shade[t] + second_ref[p, c, :, cols] * after[t]
                colour[c][t] = term if p == 0 else colour[c][t] + term

    words = [[], []]
    for t in range(count):
        codes = [depth_ref[:, t * LANES : (t + 1) * LANES]]
        for c in range(3):
            code = jnp.log2(colour[c][t]) * COLOUR_STEPS + (0.5 - COLOUR_LOW * COLOUR_STEPS)
            codes.append(jnp.minimum(jnp.maximum(code, 0.0), CODE_MAX).astype(jnp.int32))
        words[0].append(codes[0] | (codes[1] << 16))
        words[1].append(codes[2] | (codes[3] << 16))
    owned = height * across // bricks
    tall, wide = max(owned // across, 1), min(owned, across)
    for owner in range(bricks):
        top, left = owner * owned // across, owner * owned % across
        for w in range(2):
            for t in range(wide // LANES):
                out_ref[owner, w, t * tall : (t + 1) * tall, :] = words[w][left // LANES + t][
                    top : top + tall, :
                ]


def merge_kernel(planes, tall, before_ref, words_ref, out_ref):
    bricks, _, rows, _ = words_ref.shape
    f32 = jnp.float32
    depth_unit = depth_scale(planes, planes * bricks) / CODE_MAX
    depth, codes = [], []
    for b in range(bricks):
        low, high = words_ref[b, 0], words_ref[b, 1]
        depth.append((low & 0xFFFF).astype(f32) * depth_unit)
        codes.append(
            [lax.shift_right_logical(low, 16), high & 0xFFFF, lax.shift_right_logical(high, 16)]
        )
    colour = [jnp.zeros((rows, LANES), f32)] * 3
    for b in range(bricks):
        base = jnp.full((rows, LANES), COLOUR_LOW, f32)
        for other in range(bricks):
            if other != b:
                base = base - before_ref[b, other : other + 1, :] * depth[other]
        for c in range(3):
            term = jnp.exp2(codes[b][c].astype(f32) * (1.0 / COLOUR_STEPS) + base)
            colour[c] = colour[c] + jnp.where(codes[b][c] > 0, term, 0.0)
    image = colour + [jnp.exp2(-sum(depth))]
    wide = rows // tall
    for c in range(4):
        for r in range(tall):
            for t in range(wide):
                at = (r * wide + t) * LANES
                out_ref[c : c + 1, at : at + LANES] = image[c][t * tall + r : t * tall + r + 1, :]


def call(kernel, out_shape, *operands, scalars=()):
    vmem = pl.BlockSpec(memory_space=pltpu.VMEM)
    smem = pl.BlockSpec(memory_space=pltpu.SMEM)
    return pl.pallas_call(
        kernel,
        out_shape=out_shape,
        in_specs=[smem if i in scalars else vmem for i in range(len(operands))],
        out_specs=jax.tree.map(lambda _: vmem, out_shape),
        compiler_params=pltpu.CompilerParams(vmem_limit_bytes=VMEM_BYTES),
    )(*operands)


def per_device(density, tf_bins, tf_table, brick_order):
    planes, height, across = density.shape
    bricks = lax.axis_size("depth")
    owned = height * across // bricks
    shape = jax.ShapeDtypeStruct
    table = jnp.pad(tf_table, ((0, 0), (0, LANES - tf_table.shape[1])))
    plane = shape((1, height, across), density.dtype)
    rows = shape((planes, 1, across), density.dtype)
    plane_near, plane_far, row_near, row_far = call(
        edges_kernel, [plane, plane, rows, rows], density
    )
    plane_far = swap(plane_far, "depth", 1)
    plane_near = swap(plane_near, "depth", 0)
    row_near = swap(row_near, "strip", 0)
    row_far = swap(row_far, "strip", 1)
    sheared = shape((planes, 3, height, across), jnp.float32)
    first, second, depth, before = call(
        functools.partial(light_kernel, bricks),
        [
            sheared,
            sheared,
            shape((height, across), jnp.int32),
            shape((bricks, bricks, LANES), jnp.float32),
        ],
        density,
        tf_bins,
        table,
        brick_order,
        scalars=(3,),
    )
    words = call(
        functools.partial(shade_kernel, bricks),
        shape((bricks, 2, owned // LANES, LANES), jnp.int32),
        plane_far,
        plane_near,
        row_near,
        row_far,
        density,
        first,
        second,
        depth,
    )
    words = lax.all_to_all(words, "depth", 0, 0, tiled=True)
    return call(
        functools.partial(merge_kernel, planes, max(owned // across, 1)),
        shape((4, owned), jnp.float32),
        before,
        words,
    )


def solution(mesh):
    in_specs = (P("depth", "strip", None), P("depth", "strip", None), P(), P("strip", None))
    out_specs = P(None, ("strip", "depth"))
    return jax.shard_map(
        per_device, mesh=mesh, in_specs=in_specs, out_specs=out_specs, check_vma=False
    )
```

time: 32.1 us -> 25.7 us (0.80)
  the two profiles are of different devices: /device:TPU:0 before, /device:TPU:1 now
where the time goes in v3:
time: 25.7 us; the launch traced here: 25.5 us
  blocking collectives  10.4 us (40%)
  starting transfers between devices  9.8 us (38%)
  Pallas kernels  3.27 us (13%)
  local copies, waits for them, and re-layouts  1.87 us (7%)
    all_to_all x1, blocking collectives, per_device(): words = lax.all_to_all(words, 'depth', 0, 0, tiled=True)  10.4 us
    ppermute x4, starting transfers between devices, swap(): return lax.ppermute(cells, axis, pairs(lax.axis_size(axis), start))  9.8 us
    pallas_call x4, Pallas kernels, call(): pl.pallas_call(kernel, out_shape=out_shape, in_specs=[smem if i in scalar...  3.27 us
    unnamed x10, local copies, waits for them, and re-layouts  1.86 us
  transfers between devices with their start and end apart: 4, of which 0 were waited for; matrix products, arithmetic and copies ran while one was open for 0% of the time, Pallas kernels for 8%

profile of v3, /device:TPU:1, one launch (start us, length us, event | category | flops | bytes accessed | tf_op | source)
XLA Modules:
  0.0 25.5 jit_solution(1991178853151240269)
XLA Ops:
  0.0 0.0 copy-start
  0.0 0.9 %copy-done = bf16[4,16,1024]{2,1,0:T(8,128)(2,1)S(1)} copy-done((bf16[4,16,1024]{2,1,0:T(8,128)(2,1)S(1)}, bf16[4,16,1024]{2,1,0:T(8,128)(2,1)}, u32[]{:S(2)}) %copy-start) | copy-done | bytes 131096
  0.9 0.0 copy-start.1
  0.9 0.8 %collective-permute-start = (bf16[1,16,1024]{2,1,0:T(8,128)(2,1)S(1)}, bf16[1,16,1024]{2,1,0:T(8,128)(2,1)S(1)}, u32[]{:S(2)}, u32[]{:S(2)}) collective-permute-start(bf16[1,16,1024]{2,1,0:T(8,128)(2,1)S(1)} %get-tuple-element.14), channel_id=1, source_target_pairs={{4,8},{8,4},{12,16},{16,12},{20,24},{24,20},{5,9},{9,5},{13,17},{1... | collective-permute-start | bytes 98312 | tf_op jit(solution)/shard_map/ppermute | solution.py:47
  1.8 0.0 copy-start.4
  1.8 4.6 %collective-permute-start.1 = (bf16[1,16,1024]{2,1,0:T(8,128)(2,1)S(1)}, bf16[1,16,1024]{2,1,0:T(8,128)(2,1)S(1)}, u32[]{:S(2)}, u32[]{:S(2)}) collective-permute-start(bf16[1,16,1024]{2,1,0:T(8,128)(2,1)S(1)} %get-tuple-element.15), channel_id=1, source_target_pairs={{0,4},{4,0},{8,12},{12,8},{16,20},{20,16},{24,28},{28,24},{1,5},{5... | collective-permute-start | bytes 98312 | tf_op jit(solution)/shard_map/ppermute | solution.py:47
  6.4 1.2 %collective-permute-start.2 = (bf16[4,1,1024]{2,1,0:T(2,128)(2,1)S(1)}, bf16[4,1,1024]{2,1,0:T(2,128)(2,1)S(1)}, u32[]{:S(2)}, u32[]{:S(2)}) collective-permute-start(bf16[4,1,1024]{2,1,0:T(2,128)(2,1)S(1)} %get-tuple-element.16), channel_id=1, source_target_pairs={{0,1},{1,0},{2,3},{3,2},{4,5},{5,4},{6,7},{7,6},{8,9},{9,8},{10,11... | collective-permute-start | bytes 24584 | tf_op jit(solution)/shard_map/ppermute | solution.py:47
  7.6 0.0 copy-start.3
  7.6 3.2 %collective-permute-start.3 = (bf16[4,1,1024]{2,1,0:T(2,128)(2,1)S(1)}, bf16[4,1,1024]{2,1,0:T(2,128)(2,1)S(1)}, u32[]{:S(2)}, u32[]{:S(2)}) collective-permute-start(bf16[4,1,1024]{2,1,0:T(2,128)(2,1)S(1)} %get-tuple-element.17), channel_id=1, source_target_pairs={{1,2},{2,1},{5,6},{6,5},{9,10},{10,9},{13,14},{14,13},{17,18},{18,... | collective-permute-start | bytes 24584 | tf_op jit(solution)/shard_map/ppermute | solution.py:47
  10.8 0.0 copy-done.4
  10.8 0.0 copy-done.1
  10.8 0.0 copy-done.3
  10.8 0.0 copy-start.2
  10.8 0.9 %copy-done.2 = s32[4,16,1024]{2,1,0:T(8,128)S(1)} copy-done((s32[4,16,1024]{2,1,0:T(8,128)S(1)}, s32[4,16,1024]{2,1,0:T(8,128)}, u32[]{:S(2)}) %copy-start.2) | copy-done | bytes 262168
  11.8 1.9 %shard_map.46 = (f32[4,3,16,1024]{3,2,1,0:T(8,128)S(1)}, f32[4,3,16,1024]{3,2,1,0:T(8,128)S(1)}, s32[16,1024]{1,0:T(8,128)S(1)}, f32[8,8,128]{2,1,0:T(8,128)S(1)}) custom-call(bf16[4,16,1024]{2,1,0:T(8,128)(2,1)S(1)} %copy-done.1, s32[4,16,1024]{2,1,0:T(8,128)S(1)} %copy-done.2, f32[4,128]{1,0:T(4,128)S(1)} %pad.4.table_ref, s32[1,8]{1,0:T(1,128)S(1)} %copy-done.3), custom_call_target="tpu_custom_call" | custom-call | tf_op jit(solution)/shard_map/pallas_call | solution.py:236
  13.7 0.0 collective-permute-done.2.row_near
  13.7 0.0 collective-permute-done.3.row_far
  13.7 0.0 collective-permute-done.plane_far
  13.7 0.0 collective-permute-done.1.plane_near
  13.8 0.6 %shard_map.48 = s32[8,2,16,128]{3,2,1,0:T(8,128)S(1)} custom-call(bf16[1,16,1024]{2,1,0:T(8,128)(2,1)S(1)} %collective-permute-done.plane_far, bf16[1,16,1024]{2,1,0:T(8,128)(2,1)S(1)} %collective-permute-done.1.plane_near, bf16[4,1,1024]{2,1,0:T(2,128)(2,1)S(1)} %collective-permute-done.2.row_near, bf16[4,1,1024]{2,1,0:T(2,128)(2,1)S(1)} %collective-permute-done.3.row_far, ...), custom_call_target="tpu_custom_call" | custom-call | tf_op jit(solution)/shard_map/pallas_call | solution.py:236
  14.3 10.4 %all_to_all.5.words_ref = s32[8,2,16,128]{3,2,1,0:T(8,128)S(1)} all-to-all(s32[8,2,16,128]{3,2,1,0:T(8,128)S(1)} %shard_map.48), channel_id=1, replica_groups=mesh['depth'=8,'strip'=4] {'depth'}, dimensions={0} | all-to-all | bytes 262144 | tf_op jit(solution)/shard_map/all_to_all | solution.py:287
  24.7 0.7 %shard_map.49 = f32[4,2048]{1,0:T(4,128)} custom-call(f32[8,8,128]{2,1,0:T(8,128)S(1)} %get-tuple-element.13.before_ref, s32[8,2,16,128]{3,2,1,0:T(8,128)S(1)} %all_to_all.5.words_ref), custom_call_target="tpu_custom_call" | custom-call | tf_op jit(solution)/shard_map/pallas_call | solution.py:236
  (2 shorter events, 0.0 us)
Async XLA Ops:
  0.0 0.9 %copy-start = (bf16[4,16,1024]{2,1,0:T(8,128)(2,1)S(1)}, bf16[4,16,1024]{2,1,0:T(8,128)(2,1)}, u32[]{:S(2)}) copy-start(bf16[4,16,1024]{2,1,0:T(8,128)(2,1)} %density_ref.5) | copy-start | bytes 393220
  0.9 9.9 %copy-start.1 = (bf16[4,16,1024]{2,1,0:T(8,128)(2,1)S(1)}, bf16[4,16,1024]{2,1,0:T(8,128)(2,1)}, u32[]{:S(2)}) copy-start(bf16[4,16,1024]{2,1,0:T(8,128)(2,1)} %density_ref.5) | copy-start | bytes 393220
  0.9 12.8 %collective-permute-start = (bf16[1,16,1024]{2,1,0:T(8,128)(2,1)S(1)}, bf16[1,16,1024]{2,1,0:T(8,128)(2,1)S(1)}, u32[]{:S(2)}, u32[]{:S(2)}) collective-permute-start(bf16[1,16,1024]{2,1,0:T(8,128)(2,1)S(1)} %get-tuple-element.14), channel_id=1, source_target_pairs={{4,8},{8,4},{12,16},{16,12},{20,24},{24,20},{5,9},{9,5},{13,17},{1... | collective-permute-start | bytes 98312 | tf_op jit(solution)/shard_map/ppermute | solution.py:47
  1.8 9.0 %copy-start.4 = (f32[4,16]{1,0:T(4,128)S(1)}, f32[4,16]{1,0:T(4,128)}, u32[]{:S(2)}) copy-start(f32[4,16]{1,0:T(4,128)} %param.6) | copy-start | bytes 772
  1.8 12.0 %collective-permute-start.1 = (bf16[1,16,1024]{2,1,0:T(8,128)(2,1)S(1)}, bf16[1,16,1024]{2,1,0:T(8,128)(2,1)S(1)}, u32[]{:S(2)}, u32[]{:S(2)}) collective-permute-start(bf16[1,16,1024]{2,1,0:T(8,128)(2,1)S(1)} %get-tuple-element.15), channel_id=1, source_target_pairs={{0,4},{4,0},{8,12},{12,8},{16,20},{20,16},{24,28},{28,24},{1,5},{5... | collective-permute-start | bytes 98312 | tf_op jit(solution)/shard_map/ppermute | solution.py:47
  6.4 7.3 %collective-permute-start.2 = (bf16[4,1,1024]{2,1,0:T(2,128)(2,1)S(1)}, bf16[4,1,1024]{2,1,0:T(2,128)(2,1)S(1)}, u32[]{:S(2)}, u32[]{:S(2)}) collective-permute-start(bf16[4,1,1024]{2,1,0:T(2,128)(2,1)S(1)} %get-tuple-element.16), channel_id=1, source_target_pairs={{0,1},{1,0},{2,3},{3,2},{4,5},{5,4},{6,7},{7,6},{8,9},{9,8},{10,11... | collective-permute-start | bytes 24584 | tf_op jit(solution)/shard_map/ppermute | solution.py:47
  7.6 3.2 %copy-start.3 = (s32[1,8]{1,0:T(1,128)S(1)}, s32[1,8]{1,0:T(1,128)}, u32[]{:S(2)}) copy-start(s32[1,8]{1,0:T(1,128)} %order_ref.1) | copy-start | bytes 100
  7.6 6.1 %collective-permute-start.3 = (bf16[4,1,1024]{2,1,0:T(2,128)(2,1)S(1)}, bf16[4,1,1024]{2,1,0:T(2,128)(2,1)S(1)}, u32[]{:S(2)}, u32[]{:S(2)}) collective-permute-start(bf16[4,1,1024]{2,1,0:T(2,128)(2,1)S(1)} %get-tuple-element.17), channel_id=1, source_target_pairs={{1,2},{2,1},{5,6},{6,5},{9,10},{10,9},{13,14},{14,13},{17,18},{18,... | collective-permute-start | bytes 24584 | tf_op jit(solution)/shard_map/ppermute | solution.py:47
  10.8 1.0 %copy-start.2 = (s32[4,16,1024]{2,1,0:T(8,128)S(1)}, s32[4,16,1024]{2,1,0:T(8,128)}, u32[]{:S(2)}) copy-start(s32[4,16,1024]{2,1,0:T(8,128)} %bins_ref.1) | copy-start | bytes 786436

commit v4 on v3

--- a/solution.py
+++ b/solution.py
@@ -32,15 +32,44 @@
     return swaps
 
 
-def edges_kernel(density_ref, plane_near, plane_far, row_near, row_far):
+def edges_kernel(
+    density_hbm,
+    bins_hbm,
+    table_hbm,
+    order_hbm,
+    density_ref,
+    bins_ref,
+    table_ref,
+    order_ref,
+    plane_near,
+    plane_far,
+    row_near,
+    row_far,
+    small_ref,
+    semaphores,
+):
+    density_copy = pltpu.make_async_copy(density_hbm, density_ref, semaphores.at[0])
+    bins_copy = pltpu.make_async_copy(bins_hbm, bins_ref, semaphores.at[1])
+    density_copy.start()
+    bins_copy.start()
+    table_copy = pltpu.make_async_copy(table_hbm, small_ref, semaphores.at[2])
+    order_copy = pltpu.make_async_copy(order_hbm, order_ref, semaphores.at[3])
+    table_copy.start()
+    order_copy.start()
+    table_ref[...] = jnp.zeros_like(table_ref)
     planes, height, _ = density_ref.shape
     odd_brick = lax.axis_index("depth") % 2
     odd_strip = lax.axis_index("strip") % 2 == 1
+    density_copy.wait()
     plane_near[...] = density_ref[pl.ds((1 - odd_brick) * (planes - 1), 1)]
     plane_far[...] = density_ref[pl.ds(odd_brick * (planes - 1), 1)]
     head, tail = density_ref[:, 0, :], density_ref[:, height - 1, :]
     row_near[:, 0, :] = jnp.where(odd_strip, head, tail)
     row_far[:, 0, :] = jnp.where(odd_strip, tail, head)
+    table_copy.wait()
+    table_ref[:, : small_ref.shape[1]] = small_ref[...]
+    order_copy.wait()
+    bins_copy.wait()
 
 
 def swap(cells, axis, start):
@@ -122,7 +151,8 @@
     slot = lax.broadcasted_iota(jnp.int32, (bricks, LANES), 0)
     place = jnp.zeros((bricks, LANES), jnp.int32)
     for k in range(bricks):
-        place = jnp.where(slot == order_ref[0, k], k, place)
+        brick = jnp.broadcast_to(order_ref[0:1, k : k + 1], (bricks, LANES))
+        place = jnp.where(slot == brick, k, place)
     for b in range(bricks):
         before_ref[b] = (place < place[b : b + 1, :]).astype(f32)
 
@@ -230,14 +260,17 @@
                 out_ref[c : c + 1, at : at + LANES] = image[c][t * tall + r : t * tall + r + 1, :]
 
 
-def call(kernel, out_shape, *operands, scalars=()):
+def call(kernel, out_shape, *operands, spaces=None, scratch=()):
     vmem = pl.BlockSpec(memory_space=pltpu.VMEM)
-    smem = pl.BlockSpec(memory_space=pltpu.SMEM)
+    spaces = spaces or {}
     return pl.pallas_call(
         kernel,
         out_shape=out_shape,
-        in_specs=[smem if i in scalars else vmem for i in range(len(operands))],
+        in_specs=[
+            pl.BlockSpec(memory_space=spaces.get(i, pltpu.VMEM)) for i in range(len(operands))
+        ],
         out_specs=jax.tree.map(lambda _: vmem, out_shape),
+        scratch_shapes=scratch,
         compiler_params=pltpu.CompilerParams(vmem_limit_bytes=VMEM_BYTES),
     )(*operands)
 
@@ -247,11 +280,26 @@
     bricks = lax.axis_size("depth")
     owned = height * across // bricks
     shape = jax.ShapeDtypeStruct
-    table = jnp.pad(tf_table, ((0, 0), (0, LANES - tf_table.shape[1])))
     plane = shape((1, height, across), density.dtype)
     rows = shape((planes, 1, across), density.dtype)
-    plane_near, plane_far, row_near, row_far = call(
-        edges_kernel, [plane, plane, rows, rows], density
+    density, tf_bins, table, order, plane_near, plane_far, row_near, row_far = call(
+        edges_kernel,
+        [
+            shape(density.shape, density.dtype),
+            shape(tf_bins.shape, tf_bins.dtype),
+            shape((tf_table.shape[0], LANES), tf_table.dtype),
+            shape(brick_order.shape, brick_order.dtype),
+            plane,
+            plane,
+            rows,
+            rows,
+        ],
+        *[
+            pltpu.with_memory_space_constraint(argument, pltpu.HBM)
+            for argument in (density, tf_bins, tf_table, brick_order)
+        ],
+        spaces={i: pltpu.HBM for i in range(4)},
+        scratch=[pltpu.VMEM(tf_table.shape, tf_table.dtype), pltpu.SemaphoreType.DMA((4,))],
     )
     plane_far = swap(plane_far, "depth", 1)
     plane_near = swap(plane_near, "depth", 0)
@@ -269,8 +317,7 @@
         density,
         tf_bins,
         table,
-        brick_order,
-        scalars=(3,),
+        order,
     )
     words = call(
         functools.partial(shade_kernel, bricks),

time: 25.7 us -> 24.5 us (0.953)
  local copies, waits for them, and re-layouts: 1.87 us -> 0 us
  waiting for transfers between devices: 0.01 us -> 0.6 us
  Pallas kernels: 3.27 us -> 3.76 us
  starting transfers between devices: 9.8 us -> 9.54 us
    unnamed x10 -> x0, local copies, waits for them, and re-layouts: 1.86 us -> none
    ppermute x4, waiting for transfers between devices: 0.01 us -> 0.6 us  [swap(): return lax.ppermute(cells, axis, pairs(lax.axis_size(axis), start))]
    pallas_call x4, Pallas kernels: 3.27 us -> 3.76 us  [call(): pl.pallas_call(kernel, out_shape=out_shape, in_specs=[pl.BlockSpec(memory...]
    ppermute x4, starting transfers between devices: 9.8 us -> 9.54 us  [swap(): return lax.ppermute(cells, axis, pairs(lax.axis_size(axis), start))]
  transfers between devices with their start and end apart: 4 -> 4, of which waited for: 0 -> 1; matrix products, arithmetic and copies ran while one was open for 0% -> 0% of each run, Pallas kernels for 8% -> 6%
where the time goes in v4:
time: 24.5 us; the launch traced here: 24.3 us
  blocking collectives  10.4 us (42%)
  starting transfers between devices  9.54 us (39%)
  Pallas kernels  3.76 us (15%)
  waiting for transfers between devices  0.6 us (2%)
    all_to_all x1, blocking collectives, per_device(): words = lax.all_to_all(words, 'depth', 0, 0, tiled=True)  10.4 us
    ppermute x4, starting transfers between devices, swap(): return lax.ppermute(cells, axis, pairs(lax.axis_size(axis), start))  9.54 us
    pallas_call x4, Pallas kernels, call(): pl.pallas_call(kernel, out_shape=out_shape, in_specs=[pl.BlockSpec(memory...  3.76 us
    ppermute x4, waiting for transfers between devices, swap(): return lax.ppermute(cells, axis, pairs(lax.axis_size(axis), start))  0.6 us
  transfers between devices with their start and end apart: 4, of which 1 were waited for; matrix products, arithmetic and copies ran while one was open for 0% of the time, Pallas kernels for 6%

profile of v4, /device:TPU:1, one launch (start us, length us, event | category | flops | bytes accessed | tf_op | source)
XLA Modules:
  0.0 24.3 jit_solution(17259813990130794033)
XLA Ops:
  0.0 1.1 %shard_map.46 = (bf16[4,16,1024]{2,1,0:T(8,128)(2,1)S(1)}, s32[4,16,1024]{2,1,0:T(8,128)S(1)}, f32[4,128]{1,0:T(4,128)S(1)}, s32[1,8]{1,0:T(1,128)S(1)}, bf16[1,...) custom-call(bf16[4,16,1024]{2,1,0:T(8,128)(2,1)} %density_hbm.1, ...), custom_call_target="tpu_custom_call" | custom-call | tf_op jit(solution)/shard_map/pallas_call | solution.py:266
  1.1 0.7 %collective-permute-start = (bf16[1,16,1024]{2,1,0:T(8,128)(2,1)S(1)}, bf16[1,16,1024]{2,1,0:T(8,128)(2,1)S(1)}, u32[]{:S(2)}, u32[]{:S(2)}) collective-permute-start(bf16[1,16,1024]{2,1,0:T(8,128)(2,1)S(1)} %get-tuple-element.22), channel_id=1, source_target_pairs={{4,8},{8,4},{12,16},{16,12},{20,24},{24,20},{5,9},{9,5},{13,17},{1... | collective-permute-start | bytes 98312 | tf_op jit(solution)/shard_map/ppermute | solution.py:76
  1.7 4.6 %collective-permute-start.1 = (bf16[1,16,1024]{2,1,0:T(8,128)(2,1)S(1)}, bf16[1,16,1024]{2,1,0:T(8,128)(2,1)S(1)}, u32[]{:S(2)}, u32[]{:S(2)}) collective-permute-start(bf16[1,16,1024]{2,1,0:T(8,128)(2,1)S(1)} %get-tuple-element.23), channel_id=1, source_target_pairs={{0,4},{4,0},{8,12},{12,8},{16,20},{20,16},{24,28},{28,24},{1,5},{5... | collective-permute-start | bytes 98312 | tf_op jit(solution)/shard_map/ppermute | solution.py:76
  6.4 1.2 %collective-permute-start.2 = (bf16[4,1,1024]{2,1,0:T(2,128)(2,1)S(1)}, bf16[4,1,1024]{2,1,0:T(2,128)(2,1)S(1)}, u32[]{:S(2)}, u32[]{:S(2)}) collective-permute-start(bf16[4,1,1024]{2,1,0:T(2,128)(2,1)S(1)} %get-tuple-element.24), channel_id=1, source_target_pairs={{0,1},{1,0},{2,3},{3,2},{4,5},{5,4},{6,7},{7,6},{8,9},{9,8},{10,11... | collective-permute-start | bytes 24584 | tf_op jit(solution)/shard_map/ppermute | solution.py:76
  7.6 3.0 %collective-permute-start.3 = (bf16[4,1,1024]{2,1,0:T(2,128)(2,1)S(1)}, bf16[4,1,1024]{2,1,0:T(2,128)(2,1)S(1)}, u32[]{:S(2)}, u32[]{:S(2)}) collective-permute-start(bf16[4,1,1024]{2,1,0:T(2,128)(2,1)S(1)} %get-tuple-element.25), channel_id=1, source_target_pairs={{1,2},{2,1},{5,6},{6,5},{9,10},{10,9},{13,14},{14,13},{17,18},{18,... | collective-permute-start | bytes 24584 | tf_op jit(solution)/shard_map/ppermute | solution.py:76
  10.6 1.4 %shard_map.47 = (f32[4,3,16,1024]{3,2,1,0:T(8,128)S(1)}, f32[4,3,16,1024]{3,2,1,0:T(8,128)S(1)}, s32[16,1024]{1,0:T(8,128)S(1)}, f32[8,8,128]{2,1,0:T(8,128)S(1)}) custom-call(bf16[4,16,1024]{2,1,0:T(8,128)(2,1)S(1)} %get-tuple-element.17.density_ref, s32[4,16,1024]{2,1,0:T(8,128)S(1)} %get-tuple-element.18.bins_ref, ...), custom_call_target="tpu_custom_call" | custom-call | tf_op jit(solution)/shard_map/pallas_call | solution.py:266
  12.0 0.0 collective-permute-done.2.row_near
  12.0 0.6 %collective-permute-done.3.row_far = bf16[4,1,1024]{2,1,0:T(2,128)(2,1)S(1)} collective-permute-done((bf16[4,1,1024]{2,1,0:T(2,128)(2,1)S(1)}, bf16[4,1,1024]{2,1,0:T(2,128)(2,1)S(1)}, u32[]{:S(2)}, u32[]{:S(2)}) %collective-permute-start.3) | collective-permute-done | bytes 8224 | tf_op jit(solution)/shard_map/ppermute | solution.py:76
  12.6 0.0 collective-permute-done.plane_far
  12.6 0.0 collective-permute-done.1.plane_near
  12.6 0.6 %shard_map.48 = s32[8,2,16,128]{3,2,1,0:T(8,128)S(1)} custom-call(bf16[1,16,1024]{2,1,0:T(8,128)(2,1)S(1)} %collective-permute-done.plane_far, bf16[1,16,1024]{2,1,0:T(8,128)(2,1)S(1)} %collective-permute-done.1.plane_near, bf16[4,1,1024]{2,1,0:T(2,128)(2,1)S(1)} %collective-permute-done.2.row_near, bf16[4,1,1024]{2,1,0:T(2,128)(2,1)S(1)} %collective-permute-done.3.row_far, ...), custom_call_target="tpu_custom_call" | custom-call | tf_op jit(solution)/shard_map/pallas_call | solution.py:266
  13.2 10.4 %all_to_all.5.words_ref = s32[8,2,16,128]{3,2,1,0:T(8,128)S(1)} all-to-all(s32[8,2,16,128]{3,2,1,0:T(8,128)S(1)} %shard_map.48), channel_id=1, replica_groups=mesh['depth'=8,'strip'=4] {'depth'}, dimensions={0} | all-to-all | bytes 262144 | tf_op jit(solution)/shard_map/all_to_all | solution.py:334
  23.6 0.7 %shard_map.49 = f32[4,2048]{1,0:T(4,128)} custom-call(f32[8,8,128]{2,1,0:T(8,128)S(1)} %get-tuple-element.21.before_ref, s32[8,2,16,128]{3,2,1,0:T(8,128)S(1)} %all_to_all.5.words_ref), custom_call_target="tpu_custom_call" | custom-call | tf_op jit(solution)/shard_map/pallas_call | solution.py:266
Async XLA Ops:
  1.1 11.6 %collective-permute-start = (bf16[1,16,1024]{2,1,0:T(8,128)(2,1)S(1)}, bf16[1,16,1024]{2,1,0:T(8,128)(2,1)S(1)}, u32[]{:S(2)}, u32[]{:S(2)}) collective-permute-start(bf16[1,16,1024]{2,1,0:T(8,128)(2,1)S(1)} %get-tuple-element.22), channel_id=1, source_target_pairs={{4,8},{8,4},{12,16},{16,12},{20,24},{24,20},{5,9},{9,5},{13,17},{1... | collective-permute-start | bytes 98312 | tf_op jit(solution)/shard_map/ppermute | solution.py:76
  1.7 10.9 %collective-permute-start.1 = (bf16[1,16,1024]{2,1,0:T(8,128)(2,1)S(1)}, bf16[1,16,1024]{2,1,0:T(8,128)(2,1)S(1)}, u32[]{:S(2)}, u32[]{:S(2)}) collective-permute-start(bf16[1,16,1024]{2,1,0:T(8,128)(2,1)S(1)} %get-tuple-element.23), channel_id=1, source_target_pairs={{0,4},{4,0},{8,12},{12,8},{16,20},{20,16},{24,28},{28,24},{1,5},{5... | collective-permute-start | bytes 98312 | tf_op jit(solution)/shard_map/ppermute | solution.py:76
  6.4 5.7 %collective-permute-start.2 = (bf16[4,1,1024]{2,1,0:T(2,128)(2,1)S(1)}, bf16[4,1,1024]{2,1,0:T(2,128)(2,1)S(1)}, u32[]{:S(2)}, u32[]{:S(2)}) collective-permute-start(bf16[4,1,1024]{2,1,0:T(2,128)(2,1)S(1)} %get-tuple-element.24), channel_id=1, source_target_pairs={{0,1},{1,0},{2,3},{3,2},{4,5},{5,4},{6,7},{7,6},{8,9},{9,8},{10,11... | collective-permute-start | bytes 24584 | tf_op jit(solution)/shard_map/ppermute | solution.py:76
  7.6 5.0 %collective-permute-start.3 = (bf16[4,1,1024]{2,1,0:T(2,128)(2,1)S(1)}, bf16[4,1,1024]{2,1,0:T(2,128)(2,1)S(1)}, u32[]{:S(2)}, u32[]{:S(2)}) collective-permute-start(bf16[4,1,1024]{2,1,0:T(2,128)(2,1)S(1)} %get-tuple-element.25), channel_id=1, source_target_pairs={{1,2},{2,1},{5,6},{6,5},{9,10},{10,9},{13,14},{14,13},{17,18},{18,... | collective-permute-start | bytes 24584 | tf_op jit(solution)/shard_map/ppermute | solution.py:76

commit v5 on v4

--- a/solution.py
+++ b/solution.py
@@ -30,6 +30,11 @@
     for i in range(start, count - 1, 2):
         swaps += [(i, i + 1), (i + 1, i)]
     return swaps
+
+
+def partner_exists(index, count, start):
+    lower = index % 2 == start
+    return jnp.where(lower, index + 1 < count, index > 0)
 
 
 def edges_kernel(
@@ -73,7 +78,25 @@
 
 
 def swap(cells, axis, start):
-    return lax.ppermute(cells, axis, pairs(lax.axis_size(axis), start))
+    bricks, strips = lax.axis_size("depth"), lax.axis_size("strip")
+    count = bricks if axis == "depth" else strips
+    swaps = pairs(count, start)
+    spare = [i for i in range(count) if (i, i + 1) not in swaps and (i, i - 1) not in swaps]
+    if axis == "depth":
+        links = [((a, s), (b, s)) for a, b in swaps for s in range(strips)]
+        if strips % 2 == 0:
+            links += [((a, s), (a, s ^ 1)) for a in spare for s in range(strips)]
+    else:
+        if len(spare) == 2:
+            swaps = swaps + [tuple(spare), tuple(spare[::-1])]
+        links = [((d, a), (d, b)) for a, b in swaps for d in range(bricks)]
+    flat = [(a * strips + s, b * strips + t) for (a, s), (b, t) in links]
+    return lax.ppermute(cells, ("depth", "strip"), flat)
+
+
+def masked(cells, axis, start):
+    exists = partner_exists(lax.axis_index(axis), lax.axis_size(axis), start)
+    return jnp.where(exists, cells, 0.0)
 
 
 def tiles_of(value):
@@ -176,10 +199,12 @@
     odd_strip = lax.axis_index("strip") % 2 == 1
     lane = lax.broadcasted_iota(jnp.int32, (height, LANES), 1)
     row = lax.broadcasted_iota(jnp.int32, (height, LANES), 0)
-    near, far = plane_near[0].astype(f32), plane_far[0].astype(f32)
+    near = masked(plane_near[0].astype(f32), "depth", 0)
+    far = masked(plane_far[0].astype(f32), "depth", 1)
     beneath = tiles_of(jnp.where(odd_brick, near, far))
     overhead = tiles_of(jnp.where(odd_brick, far, near))
-    near, far = row_near[:, 0, :].astype(f32), row_far[:, 0, :].astype(f32)
+    near = masked(row_near[:, 0, :].astype(f32), "strip", 0)
+    far = masked(row_far[:, 0, :].astype(f32), "strip", 1)
     above = jnp.where(odd_strip, near, far)
     below = jnp.where(odd_strip, far, near)
     stack = [beneath]

time: 24.5 us -> 22.4 us (0.914)
  the two profiles are of different devices: /device:TPU:1 before, /device:TPU:0 now
where the time goes in v5:
time: 22.4 us; the launch traced here: 22.2 us
  blocking collectives  12.1 us (54%)
  starting transfers between devices  6.19 us (28%)
  Pallas kernels  3.74 us (17%)
    all_to_all x1, blocking collectives, per_device(): words = lax.all_to_all(words, 'depth', 0, 0, tiled=True)  12.1 us
    ppermute x4, starting transfers between devices, swap(): return lax.ppermute(cells, ('depth', 'strip'), flat)  6.19 us
    pallas_call x4, Pallas kernels, call(): pl.pallas_call(kernel, out_shape=out_shape, in_specs=[pl.BlockSpec(memory...  3.74 us
  transfers between devices with their start and end apart: 4, of which 1 were waited for; matrix products, arithmetic and copies ran while one was open for 0% of the time, Pallas kernels for 6%

profile of v5, /device:TPU:0, one launch (start us, length us, event | category | flops | bytes accessed | tf_op | source)
XLA Modules:
  0.0 22.2 jit_solution(13069457112753022136)
XLA Ops:
  0.0 1.1 %shard_map.46 = (bf16[4,16,1024]{2,1,0:T(8,128)(2,1)S(1)}, s32[4,16,1024]{2,1,0:T(8,128)S(1)}, f32[4,128]{1,0:T(4,128)S(1)}, s32[1,8]{1,0:T(1,128)S(1)}, bf16[1,...) custom-call(bf16[4,16,1024]{2,1,0:T(8,128)(2,1)} %density_hbm.1, ...), custom_call_target="tpu_custom_call" | custom-call | tf_op jit(solution)/shard_map/pallas_call | solution.py:291
  1.1 0.5 %collective-permute-start = (bf16[1,16,1024]{2,1,0:T(8,128)(2,1)S(1)}, bf16[1,16,1024]{2,1,0:T(8,128)(2,1)S(1)}, u32[]{:S(2)}, u32[]{:S(2)}) collective-permute-start(bf16[1,16,1024]{2,1,0:T(8,128)(2,1)S(1)} %get-tuple-element.22), channel_id=1, source_target_pairs={{4,8},{5,9},{6,10},{7,11},{8,4},{9,5},{10,6},{11,7},{12,16},{13,17... | collective-permute-start | bytes 98312 | tf_op jit(solution)/shard_map/ppermute | solution.py:94
  1.6 4.0 %collective-permute-start.1 = (bf16[1,16,1024]{2,1,0:T(8,128)(2,1)S(1)}, bf16[1,16,1024]{2,1,0:T(8,128)(2,1)S(1)}, u32[]{:S(2)}, u32[]{:S(2)}) collective-permute-start(bf16[1,16,1024]{2,1,0:T(8,128)(2,1)S(1)} %get-tuple-element.23), channel_id=1, source_target_pairs={{0,4},{1,5},{2,6},{3,7},{4,0},{5,1},{6,2},{7,3},{8,12},{9,13},{10,... | collective-permute-start | bytes 98312 | tf_op jit(solution)/shard_map/ppermute | solution.py:94
  5.6 0.0 collective-permute-start.2
  5.6 1.6 %collective-permute-start.3 = (bf16[4,1,1024]{2,1,0:T(2,128)(2,1)S(1)}, bf16[4,1,1024]{2,1,0:T(2,128)(2,1)S(1)}, u32[]{:S(2)}, u32[]{:S(2)}) collective-permute-start(bf16[4,1,1024]{2,1,0:T(2,128)(2,1)S(1)} %get-tuple-element.25), channel_id=1, source_target_pairs={{1,2},{5,6},{9,10},{13,14},{17,18},{21,22},{25,26},{29,30},{2,1},{... | collective-permute-start | bytes 24584 | tf_op jit(solution)/shard_map/ppermute | solution.py:94
  7.3 1.4 %shard_map.47 = (f32[4,3,16,1024]{3,2,1,0:T(8,128)S(1)}, f32[4,3,16,1024]{3,2,1,0:T(8,128)S(1)}, s32[16,1024]{1,0:T(8,128)S(1)}, f32[8,8,128]{2,1,0:T(8,128)S(1)}) custom-call(bf16[4,16,1024]{2,1,0:T(8,128)(2,1)S(1)} %get-tuple-element.17.density_ref, s32[4,16,1024]{2,1,0:T(8,128)S(1)} %get-tuple-element.18.bins_ref, ...), custom_call_target="tpu_custom_call" | custom-call | tf_op jit(solution)/shard_map/pallas_call | solution.py:291
  8.6 0.0 collective-permute-done.2.row_near
  8.7 0.1 collective-permute-done.3.row_far
  8.8 0.0 collective-permute-done.plane_far
  8.8 0.0 collective-permute-done.1.plane_near
  8.8 0.6 %shard_map.48 = s32[8,2,16,128]{3,2,1,0:T(8,128)S(1)} custom-call(bf16[1,16,1024]{2,1,0:T(8,128)(2,1)S(1)} %collective-permute-done.plane_far, bf16[1,16,1024]{2,1,0:T(8,128)(2,1)S(1)} %collective-permute-done.1.plane_near, bf16[4,1,1024]{2,1,0:T(2,128)(2,1)S(1)} %collective-permute-done.2.row_near, bf16[4,1,1024]{2,1,0:T(2,128)(2,1)S(1)} %collective-permute-done.3.row_far, ...), custom_call_target="tpu_custom_call" | custom-call | tf_op jit(solution)/shard_map/pallas_call | solution.py:291
  9.4 12.1 %all_to_all.5.words_ref = s32[8,2,16,128]{3,2,1,0:T(8,128)S(1)} all-to-all(s32[8,2,16,128]{3,2,1,0:T(8,128)S(1)} %shard_map.48), channel_id=1, replica_groups=mesh['depth'=8,'strip'=4] {'depth'}, dimensions={0} | all-to-all | bytes 262144 | tf_op jit(solution)/shard_map/all_to_all | solution.py:359
  21.5 0.7 %shard_map.49 = f32[4,2048]{1,0:T(4,128)} custom-call(f32[8,8,128]{2,1,0:T(8,128)S(1)} %get-tuple-element.21.before_ref, s32[8,2,16,128]{3,2,1,0:T(8,128)S(1)} %all_to_all.5.words_ref), custom_call_target="tpu_custom_call" | custom-call | tf_op jit(solution)/shard_map/pallas_call | solution.py:291
Async XLA Ops:
  1.1 7.7 %collective-permute-start = (bf16[1,16,1024]{2,1,0:T(8,128)(2,1)S(1)}, bf16[1,16,1024]{2,1,0:T(8,128)(2,1)S(1)}, u32[]{:S(2)}, u32[]{:S(2)}) collective-permute-start(bf16[1,16,1024]{2,1,0:T(8,128)(2,1)S(1)} %get-tuple-element.22), channel_id=1, source_target_pairs={{4,8},{5,9},{6,10},{7,11},{8,4},{9,5},{10,6},{11,7},{12,16},{13,17... | collective-permute-start | bytes 98312 | tf_op jit(solution)/shard_map/ppermute | solution.py:94
  1.6 7.2 %collective-permute-start.1 = (bf16[1,16,1024]{2,1,0:T(8,128)(2,1)S(1)}, bf16[1,16,1024]{2,1,0:T(8,128)(2,1)S(1)}, u32[]{:S(2)}, u32[]{:S(2)}) collective-permute-start(bf16[1,16,1024]{2,1,0:T(8,128)(2,1)S(1)} %get-tuple-element.23), channel_id=1, source_target_pairs={{0,4},{1,5},{2,6},{3,7},{4,0},{5,1},{6,2},{7,3},{8,12},{9,13},{10,... | collective-permute-start | bytes 98312 | tf_op jit(solution)/shard_map/ppermute | solution.py:94
  5.6 3.0 %collective-permute-start.2 = (bf16[4,1,1024]{2,1,0:T(2,128)(2,1)S(1)}, bf16[4,1,1024]{2,1,0:T(2,128)(2,1)S(1)}, u32[]{:S(2)}, u32[]{:S(2)}) collective-permute-start(bf16[4,1,1024]{2,1,0:T(2,128)(2,1)S(1)} %get-tuple-element.24), channel_id=1, source_target_pairs={{0,1},{4,5},{8,9},{12,13},{16,17},{20,21},{24,25},{28,29},{1,0},{5... | collective-permute-start | bytes 24584 | tf_op jit(solution)/shard_map/ppermute | solution.py:94
  5.6 3.2 %collective-permute-start.3 = (bf16[4,1,1024]{2,1,0:T(2,128)(2,1)S(1)}, bf16[4,1,1024]{2,1,0:T(2,128)(2,1)S(1)}, u32[]{:S(2)}, u32[]{:S(2)}) collective-permute-start(bf16[4,1,1024]{2,1,0:T(2,128)(2,1)S(1)} %get-tuple-element.25), channel_id=1, source_target_pairs={{1,2},{5,6},{9,10},{13,14},{17,18},{21,22},{25,26},{29,30},{2,1},{... | collective-permute-start | bytes 24584 | tf_op jit(solution)/shard_map/ppermute | solution.py:94

commit v6 on v5

--- a/solution.py
+++ b/solution.py
@@ -69,8 +69,8 @@
     plane_near[...] = density_ref[pl.ds((1 - odd_brick) * (planes - 1), 1)]
     plane_far[...] = density_ref[pl.ds(odd_brick * (planes - 1), 1)]
     head, tail = density_ref[:, 0, :], density_ref[:, height - 1, :]
-    row_near[:, 0, :] = jnp.where(odd_strip, head, tail)
-    row_far[:, 0, :] = jnp.where(odd_strip, tail, head)
+    row_near[:, 0, :] = tail
+    row_far[:, 0, :] = head
     table_copy.wait()
     table_ref[:, : small_ref.shape[1]] = small_ref[...]
     order_copy.wait()
@@ -184,8 +184,8 @@
     bricks,
     plane_far,
     plane_near,
+    row_far,
     row_near,
-    row_far,
     density_ref,
     first_ref,
     second_ref,
@@ -203,10 +203,9 @@
     far = masked(plane_far[0].astype(f32), "depth", 1)
     beneath = tiles_of(jnp.where(odd_brick, near, far))
     overhead = tiles_of(jnp.where(odd_brick, far, near))
-    near = masked(row_near[:, 0, :].astype(f32), "strip", 0)
-    far = masked(row_far[:, 0, :].astype(f32), "strip", 1)
-    above = jnp.where(odd_strip, near, far)
-    below = jnp.where(odd_strip, far, near)
+    strip = lax.axis_index("strip")
+    above = jnp.where(strip > 0, row_near[:, 0, :].astype(f32), 0.0)
+    below = jnp.where(strip < lax.axis_size("strip") - 1, row_far[:, 0, :].astype(f32), 0.0)
     stack = [beneath]
     stack += [tiles_of(density_ref[p].astype(f32)) for p in range(planes)]
     stack += [overhead]
@@ -328,8 +327,9 @@
     )
     plane_far = swap(plane_far, "depth", 1)
     plane_near = swap(plane_near, "depth", 0)
-    row_near = swap(row_near, "strip", 0)
-    row_far = swap(row_far, "strip", 1)
+    count = lax.axis_size("strip")
+    row_near = lax.ppermute(row_near, "strip", [(i, (i + 1) % count) for i in range(count)])
+    row_far = lax.ppermute(row_far, "strip", [(i, (i - 1) % count) for i in range(count)])
     sheared = shape((planes, 3, height, across), jnp.float32)
     first, second, depth, before = call(
         functools.partial(light_kernel, bricks),
@@ -349,8 +349,8 @@
         shape((bricks, 2, owned // LANES, LANES), jnp.int32),
         plane_far,
         plane_near,
+        row_far,
         row_near,
-        row_far,
         density,
         first,
         second,

time: 22.4 us -> 22.5 us (level)
  waiting for transfers between devices: 0.14 us -> 1.66 us
  starting transfers between devices: 6.19 us -> 5.06 us
  blocking collectives: 12.1 us -> 11.8 us
    ppermute x0 -> x2, waiting for transfers between devices: none -> 1.65 us  [the longest x1 1.65 us: per_device(): lax.ppermute(row_near, 'strip', [(i, (i + 1) % count) for i in range(coun...]
    ppermute x4 -> x2, starting transfers between devices: 6.19 us -> 4.55 us  [swap(): return lax.ppermute(cells, ('depth', 'strip'), flat)]
    ppermute x0 -> x2, starting transfers between devices: none -> 0.51 us  [the longest x1 0.4 us: per_device(): lax.ppermute(row_far, 'strip', [(i, (i - 1) % count) for i in range(count)])]
    all_to_all x1, blocking collectives: 12.1 us -> 11.8 us  [per_device(): words = lax.all_to_all(words, 'depth', 0, 0, tiled=True)]
where the time goes in v6:
time: 22.5 us; the launch traced here: 22.3 us
  blocking collectives  11.8 us (52%)
  starting transfers between devices  5.06 us (22%)
  Pallas kernels  3.74 us (17%)
  waiting for transfers between devices  1.66 us (7%)
    all_to_all x1, blocking collectives, per_device(): words = lax.all_to_all(words, 'depth', 0, 0, tiled=True)  11.8 us
    ppermute x2, starting transfers between devices, swap(): return lax.ppermute(cells, ('depth', 'strip'), flat)  4.55 us
    pallas_call x4, Pallas kernels, call(): pl.pallas_call(kernel, out_shape=out_shape, in_specs=[pl.BlockSpec(memory...  3.74 us
    ppermute x1, waiting for transfers between devices, per_device(): lax.ppermute(row_near, 'strip', [(i, (i + 1) % count) for i in range(coun...  1.65 us
  transfers between devices with their start and end apart: 4, of which 1 were waited for; matrix products, arithmetic and copies ran while one was open for 0% of the time, Pallas kernels for 6%

profile of v6, /device:TPU:0, one launch (start us, length us, event | category | flops | bytes accessed | tf_op | source)
XLA Modules:
  0.0 22.3 jit_solution(2065288639523397712)
XLA Ops:
  0.0 1.1 %shard_map.46 = (bf16[4,16,1024]{2,1,0:T(8,128)(2,1)S(1)}, s32[4,16,1024]{2,1,0:T(8,128)S(1)}, f32[4,128]{1,0:T(4,128)S(1)}, s32[1,8]{1,0:T(1,128)S(1)}, bf16[1,...) custom-call(bf16[4,16,1024]{2,1,0:T(8,128)(2,1)} %density_hbm.1, ...), custom_call_target="tpu_custom_call" | custom-call | tf_op jit(solution)/shard_map/pallas_call | solution.py:290
  1.1 0.5 %collective-permute-start = (bf16[1,16,1024]{2,1,0:T(8,128)(2,1)S(1)}, bf16[1,16,1024]{2,1,0:T(8,128)(2,1)S(1)}, u32[]{:S(2)}, u32[]{:S(2)}) collective-permute-start(bf16[1,16,1024]{2,1,0:T(8,128)(2,1)S(1)} %get-tuple-element.22), channel_id=1, source_target_pairs={{4,8},{5,9},{6,10},{7,11},{8,4},{9,5},{10,6},{11,7},{12,16},{13,17... | collective-permute-start | bytes 98312 | tf_op jit(solution)/shard_map/ppermute | solution.py:94
  1.6 4.0 %collective-permute-start.1 = (bf16[1,16,1024]{2,1,0:T(8,128)(2,1)S(1)}, bf16[1,16,1024]{2,1,0:T(8,128)(2,1)S(1)}, u32[]{:S(2)}, u32[]{:S(2)}) collective-permute-start(bf16[1,16,1024]{2,1,0:T(8,128)(2,1)S(1)} %get-tuple-element.23), channel_id=1, source_target_pairs={{0,4},{1,5},{2,6},{3,7},{4,0},{5,1},{6,2},{7,3},{8,12},{9,13},{10,... | collective-permute-start | bytes 98312 | tf_op jit(solution)/shard_map/ppermute | solution.py:94
  5.6 0.4 %collective-permute-start.2 = (bf16[4,1,1024]{2,1,0:T(2,128)(2,1)S(1)}, bf16[4,1,1024]{2,1,0:T(2,128)(2,1)S(1)}, u32[]{:S(2)}, u32[]{:S(2)}) collective-permute-start(bf16[4,1,1024]{2,1,0:T(2,128)(2,1)S(1)} %get-tuple-element.24), channel_id=1, source_target_pairs={{0,3},{1,0},{2,1},{3,2},{4,7},{5,4},{6,5},{7,6},{8,11},{9,8},{10,9... | collective-permute-start | bytes 24584 | tf_op jit(solution)/shard_map/ppermute | solution.py:332
  6.0 0.1 collective-permute-start.3
  6.1 1.4 %shard_map.47 = (f32[4,3,16,1024]{3,2,1,0:T(8,128)S(1)}, f32[4,3,16,1024]{3,2,1,0:T(8,128)S(1)}, s32[16,1024]{1,0:T(8,128)S(1)}, f32[8,8,128]{2,1,0:T(8,128)S(1)}) custom-call(bf16[4,16,1024]{2,1,0:T(8,128)(2,1)S(1)} %get-tuple-element.17.density_ref, s32[4,16,1024]{2,1,0:T(8,128)S(1)} %get-tuple-element.18.bins_ref, ...), custom_call_target="tpu_custom_call" | custom-call | tf_op jit(solution)/shard_map/pallas_call | solution.py:290
  7.5 0.0 collective-permute-done.2.row_far
  7.5 1.7 %collective-permute-done.3.row_near = bf16[4,1,1024]{2,1,0:T(2,128)(2,1)S(1)} collective-permute-done((bf16[4,1,1024]{2,1,0:T(2,128)(2,1)S(1)}, bf16[4,1,1024]{2,1,0:T(2,128)(2,1)S(1)}, u32[]{:S(2)}, u32[]{:S(2)}) %collective-permute-start.3) | collective-permute-done | bytes 8224 | tf_op jit(solution)/shard_map/ppermute | solution.py:331
  9.2 0.0 collective-permute-done.plane_far
  9.2 0.0 collective-permute-done.1.plane_near
  9.2 0.6 %shard_map.48 = s32[8,2,16,128]{3,2,1,0:T(8,128)S(1)} custom-call(bf16[1,16,1024]{2,1,0:T(8,128)(2,1)S(1)} %collective-permute-done.plane_far, bf16[1,16,1024]{2,1,0:T(8,128)(2,1)S(1)} %collective-permute-done.1.plane_near, bf16[4,1,1024]{2,1,0:T(2,128)(2,1)S(1)} %collective-permute-done.2.row_far, bf16[4,1,1024]{2,1,0:T(2,128)(2,1)S(1)} %collective-permute-done.3.row_near, ...), custom_call_target="tpu_custom_call" | custom-call | tf_op jit(solution)/shard_map/pallas_call | solution.py:290
  9.8 11.8 %all_to_all.5.words_ref = s32[8,2,16,128]{3,2,1,0:T(8,128)S(1)} all-to-all(s32[8,2,16,128]{3,2,1,0:T(8,128)S(1)} %shard_map.48), channel_id=1, replica_groups=mesh['depth'=8,'strip'=4] {'depth'}, dimensions={0} | all-to-all | bytes 262144 | tf_op jit(solution)/shard_map/all_to_all | solution.py:359
  21.6 0.7 %shard_map.49 = f32[4,2048]{1,0:T(4,128)} custom-call(f32[8,8,128]{2,1,0:T(8,128)S(1)} %get-tuple-element.21.before_ref, s32[8,2,16,128]{3,2,1,0:T(8,128)S(1)} %all_to_all.5.words_ref), custom_call_target="tpu_custom_call" | custom-call | tf_op jit(solution)/shard_map/pallas_call | solution.py:290
Async XLA Ops:
  1.1 8.1 %collective-permute-start = (bf16[1,16,1024]{2,1,0:T(8,128)(2,1)S(1)}, bf16[1,16,1024]{2,1,0:T(8,128)(2,1)S(1)}, u32[]{:S(2)}, u32[]{:S(2)}) collective-permute-start(bf16[1,16,1024]{2,1,0:T(8,128)(2,1)S(1)} %get-tuple-element.22), channel_id=1, source_target_pairs={{4,8},{5,9},{6,10},{7,11},{8,4},{9,5},{10,6},{11,7},{12,16},{13,17... | collective-permute-start | bytes 98312 | tf_op jit(solution)/shard_map/ppermute | solution.py:94
  1.6 7.6 %collective-permute-start.1 = (bf16[1,16,1024]{2,1,0:T(8,128)(2,1)S(1)}, bf16[1,16,1024]{2,1,0:T(8,128)(2,1)S(1)}, u32[]{:S(2)}, u32[]{:S(2)}) collective-permute-start(bf16[1,16,1024]{2,1,0:T(8,128)(2,1)S(1)} %get-tuple-element.23), channel_id=1, source_target_pairs={{0,4},{1,5},{2,6},{3,7},{4,0},{5,1},{6,2},{7,3},{8,12},{9,13},{10,... | collective-permute-start | bytes 98312 | tf_op jit(solution)/shard_map/ppermute | solution.py:94
  5.6 1.9 %collective-permute-start.2 = (bf16[4,1,1024]{2,1,0:T(2,128)(2,1)S(1)}, bf16[4,1,1024]{2,1,0:T(2,128)(2,1)S(1)}, u32[]{:S(2)}, u32[]{:S(2)}) collective-permute-start(bf16[4,1,1024]{2,1,0:T(2,128)(2,1)S(1)} %get-tuple-element.24), channel_id=1, source_target_pairs={{0,3},{1,0},{2,1},{3,2},{4,7},{5,4},{6,5},{7,6},{8,11},{9,8},{10,9... | collective-permute-start | bytes 24584 | tf_op jit(solution)/shard_map/ppermute | solution.py:332
  6.0 3.2 %collective-permute-start.3 = (bf16[4,1,1024]{2,1,0:T(2,128)(2,1)S(1)}, bf16[4,1,1024]{2,1,0:T(2,128)(2,1)S(1)}, u32[]{:S(2)}, u32[]{:S(2)}) collective-permute-start(bf16[4,1,1024]{2,1,0:T(2,128)(2,1)S(1)} %get-tuple-element.25), channel_id=1, source_target_pairs={{0,1},{1,2},{2,3},{3,0},{4,5},{5,6},{6,7},{7,4},{8,9},{9,10},{10,1... | collective-permute-start | bytes 24584 | tf_op jit(solution)/shard_map/ppermute | solution.py:331

commit v7 on v6

--- a/solution.py
+++ b/solution.py
@@ -48,8 +48,8 @@
     order_ref,
     plane_near,
     plane_far,
-    row_near,
-    row_far,
+    row_tail,
+    row_head,
     small_ref,
     semaphores,
 ):
@@ -64,34 +64,32 @@
     table_ref[...] = jnp.zeros_like(table_ref)
     planes, height, _ = density_ref.shape
     odd_brick = lax.axis_index("depth") % 2
-    odd_strip = lax.axis_index("strip") % 2 == 1
     density_copy.wait()
     plane_near[...] = density_ref[pl.ds((1 - odd_brick) * (planes - 1), 1)]
     plane_far[...] = density_ref[pl.ds(odd_brick * (planes - 1), 1)]
     head, tail = density_ref[:, 0, :], density_ref[:, height - 1, :]
-    row_near[:, 0, :] = tail
-    row_far[:, 0, :] = head
+    row_tail[:, 0, :] = tail
+    row_head[:, 0, :] = head
     table_copy.wait()
     table_ref[:, : small_ref.shape[1]] = small_ref[...]
     order_copy.wait()
     bins_copy.wait()
 
 
-def swap(cells, axis, start):
+def swap_planes(cells, start):
     bricks, strips = lax.axis_size("depth"), lax.axis_size("strip")
-    count = bricks if axis == "depth" else strips
-    swaps = pairs(count, start)
-    spare = [i for i in range(count) if (i, i + 1) not in swaps and (i, i - 1) not in swaps]
-    if axis == "depth":
-        links = [((a, s), (b, s)) for a, b in swaps for s in range(strips)]
-        if strips % 2 == 0:
-            links += [((a, s), (a, s ^ 1)) for a in spare for s in range(strips)]
-    else:
-        if len(spare) == 2:
-            swaps = swaps + [tuple(spare), tuple(spare[::-1])]
-        links = [((d, a), (d, b)) for a, b in swaps for d in range(bricks)]
+    swaps = pairs(bricks, start)
+    links = [((a, s), (b, s)) for a, b in swaps for s in range(strips)]
+    if strips % 2 == 0:
+        spare = [i for i in range(bricks) if i not in dict(swaps)]
+        links += [((a, s), (a, s ^ 1)) for a in spare for s in range(strips)]
     flat = [(a * strips + s, b * strips + t) for (a, s), (b, t) in links]
     return lax.ppermute(cells, ("depth", "strip"), flat)
+
+
+def rotate_rows(cells, step):
+    strips = lax.axis_size("strip")
+    return lax.ppermute(cells, "strip", [(i, (i + step) % strips) for i in range(strips)])
 
 
 def masked(cells, axis, start):
@@ -180,12 +178,12 @@
         before_ref[b] = (place < place[b : b + 1, :]).astype(f32)
 
 
-def shade_kernel(
+def shade(
     bricks,
+    above,
     plane_far,
     plane_near,
-    row_far,
-    row_near,
+    row_below,
     density_ref,
     first_ref,
     second_ref,
@@ -196,7 +194,6 @@
     count = across // LANES
     f32 = jnp.float32
     odd_brick = lax.axis_index("depth") % 2 == 1
-    odd_strip = lax.axis_index("strip") % 2 == 1
     lane = lax.broadcasted_iota(jnp.int32, (height, LANES), 1)
     row = lax.broadcasted_iota(jnp.int32, (height, LANES), 0)
     near = masked(plane_near[0].astype(f32), "depth", 0)
@@ -204,8 +201,7 @@
     beneath = tiles_of(jnp.where(odd_brick, near, far))
     overhead = tiles_of(jnp.where(odd_brick, far, near))
     strip = lax.axis_index("strip")
-    above = jnp.where(strip > 0, row_near[:, 0, :].astype(f32), 0.0)
-    below = jnp.where(strip < lax.axis_size("strip") - 1, row_far[:, 0, :].astype(f32), 0.0)
+    below = jnp.where(strip < lax.axis_size("strip") - 1, row_below[:, 0, :].astype(f32), 0.0)
     stack = [beneath]
     stack += [tiles_of(density_ref[p].astype(f32)) for p in range(planes)]
     stack += [overhead]
@@ -255,6 +251,26 @@
                 ]
 
 
+def top_strip_kernel(bricks, *refs):
+    planes, _, across = refs[3].shape
+
+    @pl.when(lax.axis_index("strip") == 0)
+    def _():
+        shade(bricks, jnp.zeros((planes, across), jnp.float32), *refs)
+
+
+def other_strips_kernel(bricks, *refs):
+    *refs, row_above, top_words_ref, out_ref = refs
+
+    @pl.when(lax.axis_index("strip") == 0)
+    def _():
+        out_ref[...] = top_words_ref[...]
+
+    @pl.when(lax.axis_index("strip") > 0)
+    def _():
+        shade(bricks, row_above[:, 0, :].astype(jnp.float32), *refs, out_ref)
+
+
 def merge_kernel(planes, tall, before_ref, words_ref, out_ref):
     bricks, _, rows, _ = words_ref.shape
     f32 = jnp.float32
@@ -306,7 +322,7 @@
     shape = jax.ShapeDtypeStruct
     plane = shape((1, height, across), density.dtype)
     rows = shape((planes, 1, across), density.dtype)
-    density, tf_bins, table, order, plane_near, plane_far, row_near, row_far = call(
+    density, tf_bins, table, order, plane_near, plane_far, row_tail, row_head = call(
         edges_kernel,
         [
             shape(density.shape, density.dtype),
@@ -325,11 +341,10 @@
         spaces={i: pltpu.HBM for i in range(4)},
         scratch=[pltpu.VMEM(tf_table.shape, tf_table.dtype), pltpu.SemaphoreType.DMA((4,))],
     )
-    plane_far = swap(plane_far, "depth", 1)
-    plane_near = swap(plane_near, "depth", 0)
-    count = lax.axis_size("strip")
-    row_near = lax.ppermute(row_near, "strip", [(i, (i + 1) % count) for i in range(count)])
-    row_far = lax.ppermute(row_far, "strip", [(i, (i - 1) % count) for i in range(count)])
+    plane_far = swap_planes(plane_far, 1)
+    plane_near = swap_planes(plane_near, 0)
+    row_below = rotate_rows(row_head, -1)
+    row_above = rotate_rows(row_tail, 1)
     sheared = shape((planes, 3, height, across), jnp.float32)
     first, second, depth, before = call(
         functools.partial(light_kernel, bricks),
@@ -344,17 +359,11 @@
         table,
         order,
     )
+    words_shape = shape((bricks, 2, owned // LANES, LANES), jnp.int32)
+    operands = (plane_far, plane_near, row_below, density, first, second, depth)
+    words = call(functools.partial(top_strip_kernel, bricks), words_shape, *operands)
     words = call(
-        functools.partial(shade_kernel, bricks),
-        shape((bricks, 2, owned // LANES, LANES), jnp.int32),
-        plane_far,
-        plane_near,
-        row_far,
-        row_near,
-        density,
-        first,
-        second,
-        depth,
+        functools.partial(other_strips_kernel, bricks), words_shape, *operands, row_above, words
     )
     words = lax.all_to_all(words, "depth", 0, 0, tiled=True)
     return call(

time: 22.5 us -> 21.9 us (0.973)
  waiting for transfers between devices: 1.66 us -> 1.09 us
    ppermute x4, waiting for transfers between devices: 1.66 us -> 1.09 us  [the longest x2 1.08 us: rotate_rows(): lax.ppermute(cells, 'strip', [(i, (i + step) % strips) for i in range(str...]
    pallas_call x4 -> x5, Pallas kernels: 3.74 us -> 3.73 us  [call(): pl.pallas_call(kernel, out_shape=out_shape, in_specs=[pl.BlockSpec(memory...]
  transfers between devices with their start and end apart: 4 -> 4, of which waited for: 1 -> 1; matrix products, arithmetic and copies ran while one was open for 0% -> 0% of each run, Pallas kernels for 6% -> 9%
where the time goes in v7:
time: 21.9 us; the launch traced here: 21.8 us
  blocking collectives  11.8 us (54%)
  starting transfers between devices  5.06 us (23%)
  Pallas kernels  3.73 us (17%)
  waiting for transfers between devices  1.09 us (5%)
    all_to_all x1, blocking collectives, per_device(): words = lax.all_to_all(words, 'depth', 0, 0, tiled=True)  11.8 us
    ppermute x2, starting transfers between devices, swap_planes(): return lax.ppermute(cells, ('depth', 'strip'), flat)  4.55 us
    pallas_call x5, Pallas kernels, call(): pl.pallas_call(kernel, out_shape=out_shape, in_specs=[pl.BlockSpec(memory...  3.73 us
    ppermute x2, waiting for transfers between devices, rotate_rows(): lax.ppermute(cells, 'strip', [(i, (i + step) % strips) for i in range(str...  1.08 us
    ppermute x2, starting transfers between devices, rotate_rows(): lax.ppermute(cells, 'strip', [(i, (i + step) % strips) for i in range(str...  0.51 us
  transfers between devices with their start and end apart: 4, of which 1 were waited for; matrix products, arithmetic and copies ran while one was open for 0% of the time, Pallas kernels for 9%

profile of v7, /device:TPU:0, one launch (start us, length us, event | category | flops | bytes accessed | tf_op | source)
XLA Modules:
  0.0 21.8 jit_solution(5158155474615735943)
XLA Ops:
  0.0 1.1 %shard_map.46 = (bf16[4,16,1024]{2,1,0:T(8,128)(2,1)S(1)}, s32[4,16,1024]{2,1,0:T(8,128)S(1)}, f32[4,128]{1,0:T(4,128)S(1)}, s32[1,8]{1,0:T(1,128)S(1)}, bf16[1,...) custom-call(bf16[4,16,1024]{2,1,0:T(8,128)(2,1)} %density_hbm.1, ...), custom_call_target="tpu_custom_call" | custom-call | tf_op jit(solution)/shard_map/pallas_call | solution.py:306
  1.1 0.5 %collective-permute-start = (bf16[1,16,1024]{2,1,0:T(8,128)(2,1)S(1)}, bf16[1,16,1024]{2,1,0:T(8,128)(2,1)S(1)}, u32[]{:S(2)}, u32[]{:S(2)}) collective-permute-start(bf16[1,16,1024]{2,1,0:T(8,128)(2,1)S(1)} %get-tuple-element.22), channel_id=1, source_target_pairs={{4,8},{5,9},{6,10},{7,11},{8,4},{9,5},{10,6},{11,7},{12,16},{13,17... | collective-permute-start | bytes 98312 | tf_op jit(solution)/shard_map/ppermute | solution.py:87
  1.6 4.0 %collective-permute-start.1 = (bf16[1,16,1024]{2,1,0:T(8,128)(2,1)S(1)}, bf16[1,16,1024]{2,1,0:T(8,128)(2,1)S(1)}, u32[]{:S(2)}, u32[]{:S(2)}) collective-permute-start(bf16[1,16,1024]{2,1,0:T(8,128)(2,1)S(1)} %get-tuple-element.23), channel_id=1, source_target_pairs={{0,4},{1,5},{2,6},{3,7},{4,0},{5,1},{6,2},{7,3},{8,12},{9,13},{10,... | collective-permute-start | bytes 98312 | tf_op jit(solution)/shard_map/ppermute | solution.py:87
  5.6 0.4 %collective-permute-start.2 = (bf16[4,1,1024]{2,1,0:T(2,128)(2,1)S(1)}, bf16[4,1,1024]{2,1,0:T(2,128)(2,1)S(1)}, u32[]{:S(2)}, u32[]{:S(2)}) collective-permute-start(bf16[4,1,1024]{2,1,0:T(2,128)(2,1)S(1)} %get-tuple-element.24), channel_id=1, source_target_pairs={{0,3},{1,0},{2,1},{3,2},{4,7},{5,4},{6,5},{7,6},{8,11},{9,8},{10,9... | collective-permute-start | bytes 24584 | tf_op jit(solution)/shard_map/ppermute | solution.py:92
  6.0 0.1 collective-permute-start.3
  6.1 1.4 %shard_map.47 = (f32[4,3,16,1024]{3,2,1,0:T(8,128)S(1)}, f32[4,3,16,1024]{3,2,1,0:T(8,128)S(1)}, s32[16,1024]{1,0:T(8,128)S(1)}, f32[8,8,128]{2,1,0:T(8,128)S(1)}) custom-call(bf16[4,16,1024]{2,1,0:T(8,128)(2,1)S(1)} %get-tuple-element.17.density_ref.refs_3_, s32[4,16,1024]{2,1,0:T(8,128)S(1)} %get-tuple-element.18.bins_ref, ...), custom_call_target="tpu_custom_call" | custom-call | tf_op jit(solution)/shard_map/pallas_call | solution.py:306
  7.5 0.0 collective-permute-done.2.refs_2_
  7.5 0.0 collective-permute-done.refs_0_
  7.5 0.0 collective-permute-done.1.refs_1_
  7.5 0.5 %shard_map.48.refs_8_ = s32[8,2,16,128]{3,2,1,0:T(8,128)S(1)} custom-call(bf16[1,16,1024]{2,1,0:T(8,128)(2,1)S(1)} %collective-permute-done.refs_0_, bf16[1,16,1024]{2,1,0:T(8,128)(2,1)S(1)} %collective-permute-done.1.refs_1_, bf16[4,1,1024]{2,1,0:T(2,128)(2,1)S(1)} %collective-permute-done.2.refs_2_, ...), custom_call_target="tpu_custom_call" | custom-call | tf_op jit(solution)/shard_map/pallas_call | solution.py:306
  8.1 1.1 %collective-permute-done.3.refs_7_ = bf16[4,1,1024]{2,1,0:T(2,128)(2,1)S(1)} collective-permute-done((bf16[4,1,1024]{2,1,0:T(2,128)(2,1)S(1)}, bf16[4,1,1024]{2,1,0:T(2,128)(2,1)S(1)}, u32[]{:S(2)}, u32[]{:S(2)}) %collective-permute-start.3) | collective-permute-done | bytes 8224 | tf_op jit(solution)/shard_map/ppermute | solution.py:92
  9.2 11.8 %all_to_all.5.words_ref = s32[8,2,16,128]{3,2,1,0:T(8,128)S(1)} all-to-all(s32[8,2,16,128]{3,2,1,0:T(8,128)S(1)} %shard_map.49), channel_id=1, replica_groups=mesh['depth'=8,'strip'=4] {'depth'}, dimensions={0} | all-to-all | bytes 262144 | tf_op jit(solution)/shard_map/all_to_all | solution.py:368
  21.0 0.7 %shard_map.50 = f32[4,2048]{1,0:T(4,128)} custom-call(f32[8,8,128]{2,1,0:T(8,128)S(1)} %get-tuple-element.21.before_ref, s32[8,2,16,128]{3,2,1,0:T(8,128)S(1)} %all_to_all.5.words_ref), custom_call_target="tpu_custom_call" | custom-call | tf_op jit(solution)/shard_map/pallas_call | solution.py:306
  (1 shorter events, 0.0 us)
Async XLA Ops:
  1.1 6.5 %collective-permute-start = (bf16[1,16,1024]{2,1,0:T(8,128)(2,1)S(1)}, bf16[1,16,1024]{2,1,0:T(8,128)(2,1)S(1)}, u32[]{:S(2)}, u32[]{:S(2)}) collective-permute-start(bf16[1,16,1024]{2,1,0:T(8,128)(2,1)S(1)} %get-tuple-element.22), channel_id=1, source_target_pairs={{4,8},{5,9},{6,10},{7,11},{8,4},{9,5},{10,6},{11,7},{12,16},{13,17... | collective-permute-start | bytes 98312 | tf_op jit(solution)/shard_map/ppermute | solution.py:87
  1.6 6.0 %collective-permute-start.1 = (bf16[1,16,1024]{2,1,0:T(8,128)(2,1)S(1)}, bf16[1,16,1024]{2,1,0:T(8,128)(2,1)S(1)}, u32[]{:S(2)}, u32[]{:S(2)}) collective-permute-start(bf16[1,16,1024]{2,1,0:T(8,128)(2,1)S(1)} %get-tuple-element.23), channel_id=1, source_target_pairs={{0,4},{1,5},{2,6},{3,7},{4,0},{5,1},{6,2},{7,3},{8,12},{9,13},{10,... | collective-permute-start | bytes 98312 | tf_op jit(solution)/shard_map/ppermute | solution.py:87
  5.6 1.9 %collective-permute-start.2 = (bf16[4,1,1024]{2,1,0:T(2,128)(2,1)S(1)}, bf16[4,1,1024]{2,1,0:T(2,128)(2,1)S(1)}, u32[]{:S(2)}, u32[]{:S(2)}) collective-permute-start(bf16[4,1,1024]{2,1,0:T(2,128)(2,1)S(1)} %get-tuple-element.24), channel_id=1, source_target_pairs={{0,3},{1,0},{2,1},{3,2},{4,7},{5,4},{6,5},{7,6},{8,11},{9,8},{10,9... | collective-permute-start | bytes 24584 | tf_op jit(solution)/shard_map/ppermute | solution.py:92
  6.0 3.2 %collective-permute-start.3 = (bf16[4,1,1024]{2,1,0:T(2,128)(2,1)S(1)}, bf16[4,1,1024]{2,1,0:T(2,128)(2,1)S(1)}, u32[]{:S(2)}, u32[]{:S(2)}) collective-permute-start(bf16[4,1,1024]{2,1,0:T(2,128)(2,1)S(1)} %get-tuple-element.28), channel_id=1, source_target_pairs={{0,1},{1,2},{2,3},{3,0},{4,5},{5,6},{6,7},{7,4},{8,9},{9,10},{10,1... | collective-permute-start | bytes 24584 | tf_op jit(solution)/shard_map/ppermute | solution.py:92

commit v8 on v7

--- a/solution.py
+++ b/solution.py
@@ -67,9 +67,10 @@
     density_copy.wait()
     plane_near[...] = density_ref[pl.ds((1 - odd_brick) * (planes - 1), 1)]
     plane_far[...] = density_ref[pl.ds(odd_brick * (planes - 1), 1)]
-    head, tail = density_ref[:, 0, :], density_ref[:, height - 1, :]
-    row_tail[:, 0, :] = tail
-    row_head[:, 0, :] = head
+    for p in range(planes):
+        rows = density_ref[p].astype(jnp.float32)
+        row_tail[p] = rows[height - 1 : height, :].astype(row_tail.dtype)
+        row_head[p] = rows[0:1, :].astype(row_head.dtype)
     table_copy.wait()
     table_ref[:, : small_ref.shape[1]] = small_ref[...]
     order_copy.wait()

time: 21.9 us -> 21.9 us (level)
  no operation moved by 1% of the time
where the time goes in v8:
time: 21.9 us; the launch traced here: 21.8 us
  blocking collectives  11.8 us (54%)
  starting transfers between devices  5.06 us (23%)
  Pallas kernels  3.73 us (17%)
  waiting for transfers between devices  1.09 us (5%)
    all_to_all x1, blocking collectives, per_device(): words = lax.all_to_all(words, 'depth', 0, 0, tiled=True)  11.8 us
    ppermute x2, starting transfers between devices, swap_planes(): return lax.ppermute(cells, ('depth', 'strip'), flat)  4.55 us
    pallas_call x5, Pallas kernels, call(): pl.pallas_call(kernel, out_shape=out_shape, in_specs=[pl.BlockSpec(memory...  3.73 us
    ppermute x2, waiting for transfers between devices, rotate_rows(): lax.ppermute(cells, 'strip', [(i, (i + step) % strips) for i in range(str...  1.08 us
    ppermute x2, starting transfers between devices, rotate_rows(): lax.ppermute(cells, 'strip', [(i, (i + step) % strips) for i in range(str...  0.51 us
  transfers between devices with their start and end apart: 4, of which 1 were waited for; matrix products, arithmetic and copies ran while one was open for 0% of the time, Pallas kernels for 9%

profile of v8, /device:TPU:0, one launch (start us, length us, event | category | flops | bytes accessed | tf_op | source)
XLA Modules:
  0.0 21.8 jit_solution(10883885262900900302)
XLA Ops:
  0.0 1.1 %shard_map.46 = (bf16[4,16,1024]{2,1,0:T(8,128)(2,1)S(1)}, s32[4,16,1024]{2,1,0:T(8,128)S(1)}, f32[4,128]{1,0:T(4,128)S(1)}, s32[1,8]{1,0:T(1,128)S(1)}, bf16[1,...) custom-call(bf16[4,16,1024]{2,1,0:T(8,128)(2,1)} %density_hbm.1, ...), custom_call_target="tpu_custom_call" | custom-call | tf_op jit(solution)/shard_map/pallas_call | solution.py:307
  1.1 0.5 %collective-permute-start = (bf16[1,16,1024]{2,1,0:T(8,128)(2,1)S(1)}, bf16[1,16,1024]{2,1,0:T(8,128)(2,1)S(1)}, u32[]{:S(2)}, u32[]{:S(2)}) collective-permute-start(bf16[1,16,1024]{2,1,0:T(8,128)(2,1)S(1)} %get-tuple-element.22), channel_id=1, source_target_pairs={{4,8},{5,9},{6,10},{7,11},{8,4},{9,5},{10,6},{11,7},{12,16},{13,17... | collective-permute-start | bytes 98312 | tf_op jit(solution)/shard_map/ppermute | solution.py:88
  1.6 4.0 %collective-permute-start.1 = (bf16[1,16,1024]{2,1,0:T(8,128)(2,1)S(1)}, bf16[1,16,1024]{2,1,0:T(8,128)(2,1)S(1)}, u32[]{:S(2)}, u32[]{:S(2)}) collective-permute-start(bf16[1,16,1024]{2,1,0:T(8,128)(2,1)S(1)} %get-tuple-element.23), channel_id=1, source_target_pairs={{0,4},{1,5},{2,6},{3,7},{4,0},{5,1},{6,2},{7,3},{8,12},{9,13},{10,... | collective-permute-start | bytes 98312 | tf_op jit(solution)/shard_map/ppermute | solution.py:88
  5.6 0.4 %collective-permute-start.2 = (bf16[4,1,1024]{2,1,0:T(2,128)(2,1)S(1)}, bf16[4,1,1024]{2,1,0:T(2,128)(2,1)S(1)}, u32[]{:S(2)}, u32[]{:S(2)}) collective-permute-start(bf16[4,1,1024]{2,1,0:T(2,128)(2,1)S(1)} %get-tuple-element.24), channel_id=1, source_target_pairs={{0,3},{1,0},{2,1},{3,2},{4,7},{5,4},{6,5},{7,6},{8,11},{9,8},{10,9... | collective-permute-start | bytes 24584 | tf_op jit(solution)/shard_map/ppermute | solution.py:93
  6.0 0.1 collective-permute-start.3
  6.1 1.4 %shard_map.47 = (f32[4,3,16,1024]{3,2,1,0:T(8,128)S(1)}, f32[4,3,16,1024]{3,2,1,0:T(8,128)S(1)}, s32[16,1024]{1,0:T(8,128)S(1)}, f32[8,8,128]{2,1,0:T(8,128)S(1)}) custom-call(bf16[4,16,1024]{2,1,0:T(8,128)(2,1)S(1)} %get-tuple-element.17.density_ref.refs_3_, s32[4,16,1024]{2,1,0:T(8,128)S(1)} %get-tuple-element.18.bins_ref, ...), custom_call_target="tpu_custom_call" | custom-call | tf_op jit(solution)/shard_map/pallas_call | solution.py:307
  7.5 0.0 collective-permute-done.2.refs_2_
  7.5 0.0 collective-permute-done.refs_0_
  7.5 0.0 collective-permute-done.1.refs_1_
  7.5 0.5 %shard_map.48.refs_8_ = s32[8,2,16,128]{3,2,1,0:T(8,128)S(1)} custom-call(bf16[1,16,1024]{2,1,0:T(8,128)(2,1)S(1)} %collective-permute-done.refs_0_, bf16[1,16,1024]{2,1,0:T(8,128)(2,1)S(1)} %collective-permute-done.1.refs_1_, bf16[4,1,1024]{2,1,0:T(2,128)(2,1)S(1)} %collective-permute-done.2.refs_2_, ...), custom_call_target="tpu_custom_call" | custom-call | tf_op jit(solution)/shard_map/pallas_call | solution.py:307
  8.1 1.1 %collective-permute-done.3.refs_7_ = bf16[4,1,1024]{2,1,0:T(2,128)(2,1)S(1)} collective-permute-done((bf16[4,1,1024]{2,1,0:T(2,128)(2,1)S(1)}, bf16[4,1,1024]{2,1,0:T(2,128)(2,1)S(1)}, u32[]{:S(2)}, u32[]{:S(2)}) %collective-permute-start.3) | collective-permute-done | bytes 8224 | tf_op jit(solution)/shard_map/ppermute | solution.py:93
  9.2 11.8 %all_to_all.5.words_ref = s32[8,2,16,128]{3,2,1,0:T(8,128)S(1)} all-to-all(s32[8,2,16,128]{3,2,1,0:T(8,128)S(1)} %shard_map.49), channel_id=1, replica_groups=mesh['depth'=8,'strip'=4] {'depth'}, dimensions={0} | all-to-all | bytes 262144 | tf_op jit(solution)/shard_map/all_to_all | solution.py:369
  21.0 0.7 %shard_map.50 = f32[4,2048]{1,0:T(4,128)} custom-call(f32[8,8,128]{2,1,0:T(8,128)S(1)} %get-tuple-element.21.before_ref, s32[8,2,16,128]{3,2,1,0:T(8,128)S(1)} %all_to_all.5.words_ref), custom_call_target="tpu_custom_call" | custom-call | tf_op jit(solution)/shard_map/pallas_call | solution.py:307
  (1 shorter events, 0.0 us)
Async XLA Ops:
  1.1 6.5 %collective-permute-start = (bf16[1,16,1024]{2,1,0:T(8,128)(2,1)S(1)}, bf16[1,16,1024]{2,1,0:T(8,128)(2,1)S(1)}, u32[]{:S(2)}, u32[]{:S(2)}) collective-permute-start(bf16[1,16,1024]{2,1,0:T(8,128)(2,1)S(1)} %get-tuple-element.22), channel_id=1, source_target_pairs={{4,8},{5,9},{6,10},{7,11},{8,4},{9,5},{10,6},{11,7},{12,16},{13,17... | collective-permute-start | bytes 98312 | tf_op jit(solution)/shard_map/ppermute | solution.py:88
  1.6 6.0 %collective-permute-start.1 = (bf16[1,16,1024]{2,1,0:T(8,128)(2,1)S(1)}, bf16[1,16,1024]{2,1,0:T(8,128)(2,1)S(1)}, u32[]{:S(2)}, u32[]{:S(2)}) collective-permute-start(bf16[1,16,1024]{2,1,0:T(8,128)(2,1)S(1)} %get-tuple-element.23), channel_id=1, source_target_pairs={{0,4},{1,5},{2,6},{3,7},{4,0},{5,1},{6,2},{7,3},{8,12},{9,13},{10,... | collective-permute-start | bytes 98312 | tf_op jit(solution)/shard_map/ppermute | solution.py:88
  5.6 1.9 %collective-permute-start.2 = (bf16[4,1,1024]{2,1,0:T(2,128)(2,1)S(1)}, bf16[4,1,1024]{2,1,0:T(2,128)(2,1)S(1)}, u32[]{:S(2)}, u32[]{:S(2)}) collective-permute-start(bf16[4,1,1024]{2,1,0:T(2,128)(2,1)S(1)} %get-tuple-element.24), channel_id=1, source_target_pairs={{0,3},{1,0},{2,1},{3,2},{4,7},{5,4},{6,5},{7,6},{8,11},{9,8},{10,9... | collective-permute-start | bytes 24584 | tf_op jit(solution)/shard_map/ppermute | solution.py:93
  6.0 3.2 %collective-permute-start.3 = (bf16[4,1,1024]{2,1,0:T(2,128)(2,1)S(1)}, bf16[4,1,1024]{2,1,0:T(2,128)(2,1)S(1)}, u32[]{:S(2)}, u32[]{:S(2)}) collective-permute-start(bf16[4,1,1024]{2,1,0:T(2,128)(2,1)S(1)} %get-tuple-element.28), channel_id=1, source_target_pairs={{0,1},{1,2},{2,3},{3,0},{4,5},{5,6},{6,7},{7,4},{8,9},{9,10},{10,1... | collective-permute-start | bytes 24584 | tf_op jit(solution)/shard_map/ppermute | solution.py:93

commit v9 on v7

--- a/solution.py
+++ b/solution.py
@@ -54,9 +54,13 @@
     semaphores,
 ):
     density_copy = pltpu.make_async_copy(density_hbm, density_ref, semaphores.at[0])
-    bins_copy = pltpu.make_async_copy(bins_hbm, bins_ref, semaphores.at[1])
     density_copy.start()
-    bins_copy.start()
+    odd_strip = lax.axis_index("strip") % 2 == 1
+
+    @pl.when(odd_strip)
+    def _():
+        pltpu.make_async_copy(bins_hbm, bins_ref, semaphores.at[1]).start()
+
     table_copy = pltpu.make_async_copy(table_hbm, small_ref, semaphores.at[2])
     order_copy = pltpu.make_async_copy(order_hbm, order_ref, semaphores.at[3])
     table_copy.start()
@@ -67,13 +71,18 @@
     density_copy.wait()
     plane_near[...] = density_ref[pl.ds((1 - odd_brick) * (planes - 1), 1)]
     plane_far[...] = density_ref[pl.ds(odd_brick * (planes - 1), 1)]
-    head, tail = density_ref[:, 0, :], density_ref[:, height - 1, :]
-    row_tail[:, 0, :] = tail
-    row_head[:, 0, :] = head
+    wide = [density_ref[p].astype(jnp.float32) for p in range(planes)]
+    tails = jnp.concatenate([rows[height - 1 : height, :] for rows in wide], axis=0)
+    heads = jnp.concatenate([rows[0:1, :] for rows in wide], axis=0)
+    row_tail[...] = tails.astype(row_tail.dtype)
+    row_head[...] = heads.astype(row_head.dtype)
     table_copy.wait()
     table_ref[:, : small_ref.shape[1]] = small_ref[...]
     order_copy.wait()
-    bins_copy.wait()
+
+    @pl.when(odd_strip)
+    def _():
+        pltpu.make_async_copy(bins_hbm, bins_ref, semaphores.at[1]).wait()
 
 
 def swap_planes(cells, start):
@@ -117,10 +126,26 @@
     return [jnp.where(lane < LANES - shift, rolled[t], rolled[t + 1]) for t in range(len(tiles))]
 
 
-def light_kernel(
+def light_kernel(bricks, bins_hbm, bins_vmem, *refs):
+    *refs, bins_scratch, semaphore = refs
+    odd_strip = lax.axis_index("strip") % 2 == 1
+
+    @pl.when(odd_strip)
+    def _():
+        light(bricks, bins_vmem, *refs)
+
+    @pl.when(jnp.logical_not(odd_strip))
+    def _():
+        bins_copy = pltpu.make_async_copy(bins_hbm, bins_scratch, semaphore)
+        bins_copy.start()
+        bins_copy.wait()
+        light(bricks, bins_scratch, *refs)
+
+
+def light(
     bricks,
+    bins_ref,
     density_ref,
-    bins_ref,
     table_ref,
     order_ref,
     first_ref,
@@ -133,8 +158,13 @@
     count = across // LANES
     f32 = jnp.float32
     lane = lax.broadcasted_iota(jnp.int32, (height, LANES), 1)
-    table = [jnp.broadcast_to(table_ref[c : c + 1, :], (height, LANES)) for c in range(4)]
-    table[0] = table[0] * (LOG2E / total_planes)
+    codes = (table_ref[...] * (CODE_MAX / MAX_LOOKED) + 0.5).astype(jnp.int32)
+    table = [
+        jnp.broadcast_to(codes[c : c + 1, :] | (codes[c + 1 : c + 2, :] << 16), (height, LANES))
+        for c in (0, 2)
+    ]
+    colour_unit = MAX_LOOKED / CODE_MAX
+    extinction_unit = colour_unit * LOG2E / total_planes
     depth = [jnp.zeros((height, LANES), f32)] * count
     for p in range(planes):
         plane_index = lax.axis_index("depth") * planes + p
@@ -144,12 +174,12 @@
         bins = lane_shift(tiles_of(bins_ref[p]), lane, shift, LANES - 1)
         fields = [[], [], [], []]
         for t in range(count):
-            looked = [
-                jnp.take_along_axis(entry, bins[t], axis=1, mode="promise_in_bounds")
-                for entry in table
-            ]
-            extinction = looked[0] * (1.0 + cells[t] * cells[t])
-            opacity = 1.0 - jnp.exp2(-extinction)
+            looked = []
+            for entry in table:
+                word = jnp.take_along_axis(entry, bins[t], axis=1, mode="promise_in_bounds")
+                looked += [(word & 0xFFFF).astype(f32), lax.shift_right_logical(word, 16).astype(f32)]
+            extinction = looked[0] * (extinction_unit + extinction_unit * (cells[t] * cells[t]))
+            opacity = colour_unit - colour_unit * jnp.exp2(-extinction)
             fields[0].append(extinction)
             for c in range(3):
                 fields[c + 1].append(looked[c + 1] * opacity)
@@ -201,7 +231,7 @@
     beneath = tiles_of(jnp.where(odd_brick, near, far))
     overhead = tiles_of(jnp.where(odd_brick, far, near))
     strip = lax.axis_index("strip")
-    below = jnp.where(strip < lax.axis_size("strip") - 1, row_below[:, 0, :].astype(f32), 0.0)
+    below = jnp.where(strip < lax.axis_size("strip") - 1, row_below[...].astype(f32), 0.0)
     stack = [beneath]
     stack += [tiles_of(density_ref[p].astype(f32)) for p in range(planes)]
     stack += [overhead]
@@ -268,7 +298,7 @@
 
     @pl.when(lax.axis_index("strip") > 0)
     def _():
-        shade(bricks, row_above[:, 0, :].astype(jnp.float32), *refs, out_ref)
+        shade(bricks, row_above[...].astype(jnp.float32), *refs, out_ref)
 
 
 def merge_kernel(planes, tall, before_ref, words_ref, out_ref):
@@ -321,8 +351,12 @@
     owned = height * across // bricks
     shape = jax.ShapeDtypeStruct
     plane = shape((1, height, across), density.dtype)
-    rows = shape((planes, 1, across), density.dtype)
-    density, tf_bins, table, order, plane_near, plane_far, row_tail, row_head = call(
+    rows = shape((planes, across), density.dtype)
+    arguments = [
+        pltpu.with_memory_space_constraint(argument, pltpu.HBM)
+        for argument in (density, tf_bins, tf_table, brick_order)
+    ]
+    density, bins, table, order, plane_near, plane_far, row_tail, row_head = call(
         edges_kernel,
         [
             shape(density.shape, density.dtype),
@@ -334,10 +368,7 @@
             rows,
             rows,
         ],
-        *[
-            pltpu.with_memory_space_constraint(argument, pltpu.HBM)
-            for argument in (density, tf_bins, tf_table, brick_order)
-        ],
+        *arguments,
         spaces={i: pltpu.HBM for i in range(4)},
         scratch=[pltpu.VMEM(tf_table.shape, tf_table.dtype), pltpu.SemaphoreType.DMA((4,))],
     )
@@ -354,10 +385,13 @@
             shape((height, across), jnp.int32),
             shape((bricks, bricks, LANES), jnp.float32),
         ],
+        arguments[1],
+        bins,
         density,
-        tf_bins,
         table,
         order,
+        spaces={0: pltpu.HBM},
+        scratch=[pltpu.VMEM(tf_bins.shape, tf_bins.dtype), pltpu.SemaphoreType.DMA],
     )
     words_shape = shape((bricks, 2, owned // LANES, LANES), jnp.int32)
     operands = (plane_far, plane_near, row_below, density, first, second, depth)

time: 21.9 us -> 21.9 us (level)
  waiting for transfers between devices: 1.09 us -> 0.42 us
  Pallas kernels: 3.73 us -> 4.31 us
    ppermute x2, waiting for transfers between devices: 1.08 us -> 0.41 us  [rotate_rows(): lax.ppermute(cells, 'strip', [(i, (i + step) % strips) for i in range(str...]
    pallas_call x5, Pallas kernels: 3.73 us -> 4.31 us  [call(): pl.pallas_call(kernel, out_shape=out_shape, in_specs=[pl.BlockSpec(memory...]
  transfers between devices with their start and end apart: 4 -> 4, of which waited for: 1 -> 1; matrix products, arithmetic and copies ran while one was open for 0% -> 0% of each run, Pallas kernels for 9% -> 12%
where the time goes in v9:
time: 21.9 us; the launch traced here: 21.7 us
  blocking collectives  11.8 us (54%)
  starting transfers between devices  5.06 us (23%)
  Pallas kernels  4.31 us (20%)
  waiting for transfers between devices  0.42 us (2%)
    all_to_all x1, blocking collectives, per_device(): words = lax.all_to_all(words, 'depth', 0, 0, tiled=True)  11.8 us
    ppermute x2, starting transfers between devices, swap_planes(): return lax.ppermute(cells, ('depth', 'strip'), flat)  4.55 us
    pallas_call x5, Pallas kernels, call(): pl.pallas_call(kernel, out_shape=out_shape, in_specs=[pl.BlockSpec(memory...  4.31 us
    ppermute x2, starting transfers between devices, rotate_rows(): lax.ppermute(cells, 'strip', [(i, (i + step) % strips) for i in range(str...  0.51 us
  transfers between devices with their start and end apart: 4, of which 1 were waited for; matrix products, arithmetic and copies ran while one was open for 0% of the time, Pallas kernels for 12%

profile of v9, /device:TPU:0, one launch (start us, length us, event | category | flops | bytes accessed | tf_op | source)
XLA Modules:
  0.0 21.7 jit_solution(7301698512431556889)
XLA Ops:
  0.0 1.0 %shard_map.46 = (bf16[4,16,1024]{2,1,0:T(8,128)(2,1)S(1)}, s32[4,16,1024]{2,1,0:T(8,128)S(1)}, f32[4,128]{1,0:T(4,128)S(1)}, s32[1,8]{1,0:T(1,128)S(1)}, bf16[1,...) custom-call(bf16[4,16,1024]{2,1,0:T(8,128)(2,1)} %density_hbm.1, ...), custom_call_target="tpu_custom_call" | custom-call | tf_op jit(solution)/shard_map/pallas_call | solution.py:336
  1.0 0.6 %collective-permute-start = (bf16[1,16,1024]{2,1,0:T(8,128)(2,1)S(1)}, bf16[1,16,1024]{2,1,0:T(8,128)(2,1)S(1)}, u32[]{:S(2)}, u32[]{:S(2)}) collective-permute-start(bf16[1,16,1024]{2,1,0:T(8,128)(2,1)S(1)} %get-tuple-element.22), channel_id=1, source_target_pairs={{4,8},{5,9},{6,10},{7,11},{8,4},{9,5},{10,6},{11,7},{12,16},{13,17... | collective-permute-start | bytes 98312 | tf_op jit(solution)/shard_map/ppermute | solution.py:96
  1.6 4.0 %collective-permute-start.1 = (bf16[1,16,1024]{2,1,0:T(8,128)(2,1)S(1)}, bf16[1,16,1024]{2,1,0:T(8,128)(2,1)S(1)}, u32[]{:S(2)}, u32[]{:S(2)}) collective-permute-start(bf16[1,16,1024]{2,1,0:T(8,128)(2,1)S(1)} %get-tuple-element.23), channel_id=1, source_target_pairs={{0,4},{1,5},{2,6},{3,7},{4,0},{5,1},{6,2},{7,3},{8,12},{9,13},{10,... | collective-permute-start | bytes 98312 | tf_op jit(solution)/shard_map/ppermute | solution.py:96
  5.5 0.5 %collective-permute-start.2 = (bf16[4,1024]{1,0:T(4,128)(2,1)S(1)}, bf16[4,1024]{1,0:T(4,128)(2,1)S(1)}, u32[]{:S(2)}, u32[]{:S(2)}) collective-permute-start(bf16[4,1024]{1,0:T(4,128)(2,1)S(1)} %get-tuple-element.24), channel_id=1, source_target_pairs={{0,3},{1,0},{2,1},{3,2},{4,7},{5,4},{6,5},{7,6},{8,11},{9,8},{10,9... | collective-permute-start | bytes 24584 | tf_op jit(solution)/shard_map/ppermute | solution.py:101
  6.0 0.0 collective-permute-start.3
  6.0 2.0 %shard_map.47 = (f32[4,3,16,1024]{3,2,1,0:T(8,128)S(1)}, f32[4,3,16,1024]{3,2,1,0:T(8,128)S(1)}, s32[16,1024]{1,0:T(8,128)S(1)}, f32[8,8,128]{2,1,0:T(8,128)S(1)}) custom-call(s32[4,16,1024]{2,1,0:T(8,128)} %bins_hbm.3, s32[4,16,1024]{2,1,0:T(8,128)S(1)} %get-tuple-element.17.bins_vmem, bf16[4,16,1024]{2,1,0:T(8,128)(2,1)S(1)} %get-tuple-element.18.refs_0_.refs_3_, ...), custom_call_target="tpu_custom_call" | custom-call | tf_op jit(solution)/shard_map/pallas_call | solution.py:336
  8.1 0.0 collective-permute-done.2.refs_2_
  8.1 0.0 collective-permute-done.refs_0_
  8.1 0.0 collective-permute-done.1.refs_1_
  8.1 0.5 %shard_map.48.refs_8_ = s32[8,2,16,128]{3,2,1,0:T(8,128)S(1)} custom-call(bf16[1,16,1024]{2,1,0:T(8,128)(2,1)S(1)} %collective-permute-done.refs_0_, bf16[1,16,1024]{2,1,0:T(8,128)(2,1)S(1)} %collective-permute-done.1.refs_1_, bf16[4,1024]{1,0:T(4,128)(2,1)S(1)} %collective-permute-done.2.refs_2_, ...), custom_call_target="tpu_custom_call" | custom-call | tf_op jit(solution)/shard_map/pallas_call | solution.py:336
  8.7 0.4 %collective-permute-done.3.refs_7_ = bf16[4,1024]{1,0:T(4,128)(2,1)S(1)} collective-permute-done((bf16[4,1024]{1,0:T(4,128)(2,1)S(1)}, bf16[4,1024]{1,0:T(4,128)(2,1)S(1)}, u32[]{:S(2)}, u32[]{:S(2)}) %collective-permute-start.3) | collective-permute-done | bytes 8224 | tf_op jit(solution)/shard_map/ppermute | solution.py:101
  9.1 11.8 %all_to_all.5.words_ref = s32[8,2,16,128]{3,2,1,0:T(8,128)S(1)} all-to-all(s32[8,2,16,128]{3,2,1,0:T(8,128)S(1)} %shard_map.49), channel_id=1, replica_groups=mesh['depth'=8,'strip'=4] {'depth'}, dimensions={0} | all-to-all | bytes 262144 | tf_op jit(solution)/shard_map/all_to_all | solution.py:402
  20.9 0.7 %shard_map.50 = f32[4,2048]{1,0:T(4,128)} custom-call(f32[8,8,128]{2,1,0:T(8,128)S(1)} %get-tuple-element.21.before_ref, s32[8,2,16,128]{3,2,1,0:T(8,128)S(1)} %all_to_all.5.words_ref), custom_call_target="tpu_custom_call" | custom-call | tf_op jit(solution)/shard_map/pallas_call | solution.py:336
  (1 shorter events, 0.0 us)
Async XLA Ops:
  1.0 7.1 %collective-permute-start = (bf16[1,16,1024]{2,1,0:T(8,128)(2,1)S(1)}, bf16[1,16,1024]{2,1,0:T(8,128)(2,1)S(1)}, u32[]{:S(2)}, u32[]{:S(2)}) collective-permute-start(bf16[1,16,1024]{2,1,0:T(8,128)(2,1)S(1)} %get-tuple-element.22), channel_id=1, source_target_pairs={{4,8},{5,9},{6,10},{7,11},{8,4},{9,5},{10,6},{11,7},{12,16},{13,17... | collective-permute-start | bytes 98312 | tf_op jit(solution)/shard_map/ppermute | solution.py:96
  1.6 6.5 %collective-permute-start.1 = (bf16[1,16,1024]{2,1,0:T(8,128)(2,1)S(1)}, bf16[1,16,1024]{2,1,0:T(8,128)(2,1)S(1)}, u32[]{:S(2)}, u32[]{:S(2)}) collective-permute-start(bf16[1,16,1024]{2,1,0:T(8,128)(2,1)S(1)} %get-tuple-element.23), channel_id=1, source_target_pairs={{0,4},{1,5},{2,6},{3,7},{4,0},{5,1},{6,2},{7,3},{8,12},{9,13},{10,... | collective-permute-start | bytes 98312 | tf_op jit(solution)/shard_map/ppermute | solution.py:96
  5.5 2.6 %collective-permute-start.2 = (bf16[4,1024]{1,0:T(4,128)(2,1)S(1)}, bf16[4,1024]{1,0:T(4,128)(2,1)S(1)}, u32[]{:S(2)}, u32[]{:S(2)}) collective-permute-start(bf16[4,1024]{1,0:T(4,128)(2,1)S(1)} %get-tuple-element.24), channel_id=1, source_target_pairs={{0,3},{1,0},{2,1},{3,2},{4,7},{5,4},{6,5},{7,6},{8,11},{9,8},{10,9... | collective-permute-start | bytes 24584 | tf_op jit(solution)/shard_map/ppermute | solution.py:101
  6.0 3.1 %collective-permute-start.3 = (bf16[4,1024]{1,0:T(4,128)(2,1)S(1)}, bf16[4,1024]{1,0:T(4,128)(2,1)S(1)}, u32[]{:S(2)}, u32[]{:S(2)}) collective-permute-start(bf16[4,1024]{1,0:T(4,128)(2,1)S(1)} %get-tuple-element.28), channel_id=1, source_target_pairs={{0,1},{1,2},{2,3},{3,0},{4,5},{5,6},{6,7},{7,4},{8,9},{9,10},{10,1... | collective-permute-start | bytes 24584 | tf_op jit(solution)/shard_map/ppermute | solution.py:101

commit v10 on v9

--- a/solution.py
+++ b/solution.py
@@ -276,9 +276,10 @@
         top, left = owner * owned // across, owner * owned % across
         for w in range(2):
             for t in range(wide // LANES):
-                out_ref[owner, w, t * tall : (t + 1) * tall, :] = words[w][left // LANES + t][
-                    top : top + tall, :
-                ]
+                for r in range(tall):
+                    out_ref[owner, w, r * (wide // LANES) + t : r * (wide // LANES) + t + 1, :] = words[
+                        w
+                    ][left // LANES + t][top + r : top + r + 1, :]
 
 
 def top_strip_kernel(bricks, *refs):
@@ -301,7 +302,7 @@
         shade(bricks, row_above[...].astype(jnp.float32), *refs, out_ref)
 
 
-def merge_kernel(planes, tall, before_ref, words_ref, out_ref):
+def merge_kernel(planes, before_ref, words_ref, out_ref):
     bricks, _, rows, _ = words_ref.shape
     f32 = jnp.float32
     depth_unit = depth_scale(planes, planes * bricks) / CODE_MAX
@@ -322,12 +323,8 @@
             term = jnp.exp2(codes[b][c].astype(f32) * (1.0 / COLOUR_STEPS) + base)
             colour[c] = colour[c] + jnp.where(codes[b][c] > 0, term, 0.0)
     image = colour + [jnp.exp2(-sum(depth))]
-    wide = rows // tall
     for c in range(4):
-        for r in range(tall):
-            for t in range(wide):
-                at = (r * wide + t) * LANES
-                out_ref[c : c + 1, at : at + LANES] = image[c][t * tall + r : t * tall + r + 1, :]
+        out_ref[pl.ds(c, rows, stride=4), :] = image[c]
 
 
 def call(kernel, out_shape, *operands, spaces=None, scratch=()):
@@ -400,12 +397,14 @@
         functools.partial(other_strips_kernel, bricks), words_shape, *operands, row_above, words
     )
     words = lax.all_to_all(words, "depth", 0, 0, tiled=True)
-    return call(
-        functools.partial(merge_kernel, planes, max(owned // across, 1)),
-        shape((4, owned), jnp.float32),
+    pieces = owned // LANES
+    image = call(
+        functools.partial(merge_kernel, planes),
+        shape((pieces * 4, LANES), jnp.float32),
         before,
         words,
     )
+    return image.reshape(pieces, 4, LANES).transpose(1, 0, 2).reshape(4, owned)
 
 
 def solution(mesh):

time: 21.9 us -> 21.9 us (level)
  no operation moved by 1% of the time
where the time goes in v10:
time: 21.9 us; the launch traced here: 21.7 us
  blocking collectives  11.8 us (54%)
  starting transfers between devices  5.06 us (23%)
  Pallas kernels  4.31 us (20%)
  waiting for transfers between devices  0.41 us (2%)
    all_to_all x1, blocking collectives, per_device(): words = lax.all_to_all(words, 'depth', 0, 0, tiled=True)  11.8 us
    ppermute x2, starting transfers between devices, swap_planes(): return lax.ppermute(cells, ('depth', 'strip'), flat)  4.55 us
    pallas_call x5, Pallas kernels, call(): pl.pallas_call(kernel, out_shape=out_shape, in_specs=[pl.BlockSpec(memory...  4.31 us
    ppermute x2, starting transfers between devices, rotate_rows(): lax.ppermute(cells, 'strip', [(i, (i + step) % strips) for i in range(str...  0.51 us
  transfers between devices with their start and end apart: 4, of which 1 were waited for; matrix products, arithmetic and copies ran while one was open for 0% of the time, Pallas kernels for 12%

profile of v10, /device:TPU:0, one launch (start us, length us, event | category | flops | bytes accessed | tf_op | source)
XLA Modules:
  0.0 21.7 jit_solution(3503056510773424088)
XLA Ops:
  0.0 1.0 %shard_map.46 = (bf16[4,16,1024]{2,1,0:T(8,128)(2,1)S(1)}, s32[4,16,1024]{2,1,0:T(8,128)S(1)}, f32[4,128]{1,0:T(4,128)S(1)}, s32[1,8]{1,0:T(1,128)S(1)}, bf16[1,...) custom-call(bf16[4,16,1024]{2,1,0:T(8,128)(2,1)} %density_hbm.1, ...), custom_call_target="tpu_custom_call" | custom-call | tf_op jit(solution)/shard_map/pallas_call | solution.py:333
  1.0 0.6 %collective-permute-start = (bf16[1,16,1024]{2,1,0:T(8,128)(2,1)S(1)}, bf16[1,16,1024]{2,1,0:T(8,128)(2,1)S(1)}, u32[]{:S(2)}, u32[]{:S(2)}) collective-permute-start(bf16[1,16,1024]{2,1,0:T(8,128)(2,1)S(1)} %get-tuple-element.22), channel_id=1, source_target_pairs={{4,8},{5,9},{6,10},{7,11},{8,4},{9,5},{10,6},{11,7},{12,16},{13,17... | collective-permute-start | bytes 98312 | tf_op jit(solution)/shard_map/ppermute | solution.py:96
  1.6 4.0 %collective-permute-start.1 = (bf16[1,16,1024]{2,1,0:T(8,128)(2,1)S(1)}, bf16[1,16,1024]{2,1,0:T(8,128)(2,1)S(1)}, u32[]{:S(2)}, u32[]{:S(2)}) collective-permute-start(bf16[1,16,1024]{2,1,0:T(8,128)(2,1)S(1)} %get-tuple-element.23), channel_id=1, source_target_pairs={{0,4},{1,5},{2,6},{3,7},{4,0},{5,1},{6,2},{7,3},{8,12},{9,13},{10,... | collective-permute-start | bytes 98312 | tf_op jit(solution)/shard_map/ppermute | solution.py:96
  5.5 0.5 %collective-permute-start.2 = (bf16[4,1024]{1,0:T(4,128)(2,1)S(1)}, bf16[4,1024]{1,0:T(4,128)(2,1)S(1)}, u32[]{:S(2)}, u32[]{:S(2)}) collective-permute-start(bf16[4,1024]{1,0:T(4,128)(2,1)S(1)} %get-tuple-element.24), channel_id=1, source_target_pairs={{0,3},{1,0},{2,1},{3,2},{4,7},{5,4},{6,5},{7,6},{8,11},{9,8},{10,9... | collective-permute-start | bytes 24584 | tf_op jit(solution)/shard_map/ppermute | solution.py:101
  6.0 0.0 collective-permute-start.3
  6.0 2.0 %shard_map.47 = (f32[4,3,16,1024]{3,2,1,0:T(8,128)S(1)}, f32[4,3,16,1024]{3,2,1,0:T(8,128)S(1)}, s32[16,1024]{1,0:T(8,128)S(1)}, f32[8,8,128]{2,1,0:T(8,128)S(1)}) custom-call(s32[4,16,1024]{2,1,0:T(8,128)} %bins_hbm.3, s32[4,16,1024]{2,1,0:T(8,128)S(1)} %get-tuple-element.17.bins_vmem, bf16[4,16,1024]{2,1,0:T(8,128)(2,1)S(1)} %get-tuple-element.18.refs_0_.refs_3_, ...), custom_call_target="tpu_custom_call" | custom-call | tf_op jit(solution)/shard_map/pallas_call | solution.py:333
  8.1 0.0 collective-permute-done.2.refs_2_
  8.1 0.0 collective-permute-done.refs_0_
  8.1 0.0 collective-permute-done.1.refs_1_
  8.1 0.6 %shard_map.48.refs_8_ = s32[8,2,16,128]{3,2,1,0:T(8,128)S(1)} custom-call(bf16[1,16,1024]{2,1,0:T(8,128)(2,1)S(1)} %collective-permute-done.refs_0_, bf16[1,16,1024]{2,1,0:T(8,128)(2,1)S(1)} %collective-permute-done.1.refs_1_, bf16[4,1024]{1,0:T(4,128)(2,1)S(1)} %collective-permute-done.2.refs_2_, ...), custom_call_target="tpu_custom_call" | custom-call | tf_op jit(solution)/shard_map/pallas_call | solution.py:333
  8.7 0.4 %collective-permute-done.3.refs_7_ = bf16[4,1024]{1,0:T(4,128)(2,1)S(1)} collective-permute-done((bf16[4,1024]{1,0:T(4,128)(2,1)S(1)}, bf16[4,1024]{1,0:T(4,128)(2,1)S(1)}, u32[]{:S(2)}, u32[]{:S(2)}) %collective-permute-start.3) | collective-permute-done | bytes 8224 | tf_op jit(solution)/shard_map/ppermute | solution.py:101
  9.1 11.8 %all_to_all.5.words_ref = s32[8,2,16,128]{3,2,1,0:T(8,128)S(1)} all-to-all(s32[8,2,16,128]{3,2,1,0:T(8,128)S(1)} %shard_map.49), channel_id=1, replica_groups=mesh['depth'=8,'strip'=4] {'depth'}, dimensions={0} | all-to-all | bytes 262144 | tf_op jit(solution)/shard_map/all_to_all | solution.py:399
  20.9 0.7 %shard_map.50 = f32[64,128]{1,0:T(8,128)} custom-call(f32[8,8,128]{2,1,0:T(8,128)S(1)} %get-tuple-element.21.before_ref, s32[8,2,16,128]{3,2,1,0:T(8,128)S(1)} %all_to_all.5.words_ref), custom_call_target="tpu_custom_call" | custom-call | tf_op jit(solution)/shard_map/pallas_call | solution.py:333
  (1 shorter events, 0.0 us)
Async XLA Ops:
  1.0 7.1 %collective-permute-start = (bf16[1,16,1024]{2,1,0:T(8,128)(2,1)S(1)}, bf16[1,16,1024]{2,1,0:T(8,128)(2,1)S(1)}, u32[]{:S(2)}, u32[]{:S(2)}) collective-permute-start(bf16[1,16,1024]{2,1,0:T(8,128)(2,1)S(1)} %get-tuple-element.22), channel_id=1, source_target_pairs={{4,8},{5,9},{6,10},{7,11},{8,4},{9,5},{10,6},{11,7},{12,16},{13,17... | collective-permute-start | bytes 98312 | tf_op jit(solution)/shard_map/ppermute | solution.py:96
  1.6 6.5 %collective-permute-start.1 = (bf16[1,16,1024]{2,1,0:T(8,128)(2,1)S(1)}, bf16[1,16,1024]{2,1,0:T(8,128)(2,1)S(1)}, u32[]{:S(2)}, u32[]{:S(2)}) collective-permute-start(bf16[1,16,1024]{2,1,0:T(8,128)(2,1)S(1)} %get-tuple-element.23), channel_id=1, source_target_pairs={{0,4},{1,5},{2,6},{3,7},{4,0},{5,1},{6,2},{7,3},{8,12},{9,13},{10,... | collective-permute-start | bytes 98312 | tf_op jit(solution)/shard_map/ppermute | solution.py:96
  5.5 2.6 %collective-permute-start.2 = (bf16[4,1024]{1,0:T(4,128)(2,1)S(1)}, bf16[4,1024]{1,0:T(4,128)(2,1)S(1)}, u32[]{:S(2)}, u32[]{:S(2)}) collective-permute-start(bf16[4,1024]{1,0:T(4,128)(2,1)S(1)} %get-tuple-element.24), channel_id=1, source_target_pairs={{0,3},{1,0},{2,1},{3,2},{4,7},{5,4},{6,5},{7,6},{8,11},{9,8},{10,9... | collective-permute-start | bytes 24584 | tf_op jit(solution)/shard_map/ppermute | solution.py:101
  6.0 3.1 %collective-permute-start.3 = (bf16[4,1024]{1,0:T(4,128)(2,1)S(1)}, bf16[4,1024]{1,0:T(4,128)(2,1)S(1)}, u32[]{:S(2)}, u32[]{:S(2)}) collective-permute-start(bf16[4,1024]{1,0:T(4,128)(2,1)S(1)} %get-tuple-element.28), channel_id=1, source_target_pairs={{0,1},{1,2},{2,3},{3,0},{4,5},{5,6},{6,7},{7,4},{8,9},{9,10},{10,1... | collective-permute-start | bytes 24584 | tf_op jit(solution)/shard_map/ppermute | solution.py:101

commit v11 on v10

--- a/solution.py
+++ b/solution.py
@@ -126,18 +126,30 @@
     return [jnp.where(lane < LANES - shift, rolled[t], rolled[t + 1]) for t in range(len(tiles))]
 
 
+def slopes_across(density_ref, across_ref):
+    planes, height, across = density_ref.shape
+    lane = lax.broadcasted_iota(jnp.int32, (height, LANES), 1)
+    for p in range(planes):
+        centre = tiles_of(density_ref[p].astype(jnp.float32))
+        ahead, behind = lane_next(centre, lane), lane_previous(centre, lane)
+        for t in range(across // LANES):
+            across_ref[p, :, t * LANES : (t + 1) * LANES] = ahead[t] - behind[t]
+
+
 def light_kernel(bricks, bins_hbm, bins_vmem, *refs):
-    *refs, bins_scratch, semaphore = refs
+    *refs, across_ref, bins_scratch, semaphore = refs
     odd_strip = lax.axis_index("strip") % 2 == 1
 
     @pl.when(odd_strip)
     def _():
+        slopes_across(refs[0], across_ref)
         light(bricks, bins_vmem, *refs)
 
     @pl.when(jnp.logical_not(odd_strip))
     def _():
         bins_copy = pltpu.make_async_copy(bins_hbm, bins_scratch, semaphore)
         bins_copy.start()
+        slopes_across(refs[0], across_ref)
         bins_copy.wait()
         light(bricks, bins_scratch, *refs)
 
@@ -218,6 +230,7 @@
     first_ref,
     second_ref,
     depth_ref,
+    across_ref,
     out_ref,
 ):
     planes, height, across = density_ref.shape
@@ -240,7 +253,6 @@
     for p in range(planes):
         shift = (3 * (lax.axis_index("depth") * planes + p)) // 8
         centre = stack[p + 1]
-        ahead, behind = lane_next(centre, lane), lane_previous(centre, lane)
         shade = []
         for t in range(count):
             cols = slice(t * LANES, (t + 1) * LANES)
@@ -249,7 +261,7 @@
             down = jnp.where(
                 row == height - 1, below[p : p + 1, cols], pltpu.roll(v, height - 1, 0)
             )
-            dx = ahead[t] - behind[t]
+            dx = across_ref[p, :, cols]
             dy = down - up
             dz = stack[p + 2][t] - stack[p][t]
             lit = (LIGHT[0] * gain) * dx + (LIGHT[1] * gain) * dy + (LIGHT[2] * gain) * dz
@@ -374,13 +386,14 @@
     row_below = rotate_rows(row_head, -1)
     row_above = rotate_rows(row_tail, 1)
     sheared = shape((planes, 3, height, across), jnp.float32)
-    first, second, depth, before = call(
+    first, second, depth, before, across_slopes = call(
         functools.partial(light_kernel, bricks),
         [
             sheared,
             sheared,
             shape((height, across), jnp.int32),
             shape((bricks, bricks, LANES), jnp.float32),
+            shape((planes, height, across), jnp.float32),
         ],
         arguments[1],
         bins,
@@ -391,7 +404,7 @@
         scratch=[pltpu.VMEM(tf_bins.shape, tf_bins.dtype), pltpu.SemaphoreType.DMA],
     )
     words_shape = shape((bricks, 2, owned // LANES, LANES), jnp.int32)
-    operands = (plane_far, plane_near, row_below, density, first, second, depth)
+    operands = (plane_far, plane_near, row_below, density, first, second, depth, across_slopes)
     words = call(functools.partial(top_strip_kernel, bricks), words_shape, *operands)
     words = call(
         functools.partial(other_strips_kernel, bricks), words_shape, *operands, row_above, words

time: 21.9 us -> 21.9 us (level)
  no operation moved by 1% of the time
where the time goes in v11:
time: 21.9 us; the launch traced here: 21.7 us
  blocking collectives  11.8 us (54%)
  starting transfers between devices  5.06 us (23%)
  Pallas kernels  4.25 us (19%)
  waiting for transfers between devices  0.47 us (2%)
    all_to_all x1, blocking collectives, per_device(): words = lax.all_to_all(words, 'depth', 0, 0, tiled=True)  11.8 us
    ppermute x2, starting transfers between devices, swap_planes(): return lax.ppermute(cells, ('depth', 'strip'), flat)  4.55 us
    pallas_call x5, Pallas kernels, call(): pl.pallas_call(kernel, out_shape=out_shape, in_specs=[pl.BlockSpec(memory...  4.25 us
    ppermute x2, starting transfers between devices, rotate_rows(): lax.ppermute(cells, 'strip', [(i, (i + step) % strips) for i in range(str...  0.51 us
    ppermute x2, waiting for transfers between devices, rotate_rows(): lax.ppermute(cells, 'strip', [(i, (i + step) % strips) for i in range(str...  0.47 us
  transfers between devices with their start and end apart: 4, of which 1 were waited for; matrix products, arithmetic and copies ran while one was open for 0% of the time, Pallas kernels for 12%

profile of v11, /device:TPU:0, one launch (start us, length us, event | category | flops | bytes accessed | tf_op | source)
XLA Modules:
  0.0 21.7 jit_solution(5053513516770327546)
XLA Ops:
  0.0 1.0 %shard_map.46 = (bf16[4,16,1024]{2,1,0:T(8,128)(2,1)S(1)}, s32[4,16,1024]{2,1,0:T(8,128)S(1)}, f32[4,128]{1,0:T(4,128)S(1)}, s32[1,8]{1,0:T(1,128)S(1)}, bf16[1,...) custom-call(bf16[4,16,1024]{2,1,0:T(8,128)(2,1)} %density_hbm.1, ...), custom_call_target="tpu_custom_call" | custom-call | tf_op jit(solution)/shard_map/pallas_call | solution.py:345
  1.0 0.6 %collective-permute-start = (bf16[1,16,1024]{2,1,0:T(8,128)(2,1)S(1)}, bf16[1,16,1024]{2,1,0:T(8,128)(2,1)S(1)}, u32[]{:S(2)}, u32[]{:S(2)}) collective-permute-start(bf16[1,16,1024]{2,1,0:T(8,128)(2,1)S(1)} %get-tuple-element.23), channel_id=1, source_target_pairs={{4,8},{5,9},{6,10},{7,11},{8,4},{9,5},{10,6},{11,7},{12,16},{13,17... | collective-permute-start | bytes 98312 | tf_op jit(solution)/shard_map/ppermute | solution.py:96
  1.6 4.0 %collective-permute-start.1 = (bf16[1,16,1024]{2,1,0:T(8,128)(2,1)S(1)}, bf16[1,16,1024]{2,1,0:T(8,128)(2,1)S(1)}, u32[]{:S(2)}, u32[]{:S(2)}) collective-permute-start(bf16[1,16,1024]{2,1,0:T(8,128)(2,1)S(1)} %get-tuple-element.24), channel_id=1, source_target_pairs={{0,4},{1,5},{2,6},{3,7},{4,0},{5,1},{6,2},{7,3},{8,12},{9,13},{10,... | collective-permute-start | bytes 98312 | tf_op jit(solution)/shard_map/ppermute | solution.py:96
  5.5 0.5 %collective-permute-start.2 = (bf16[4,1024]{1,0:T(4,128)(2,1)S(1)}, bf16[4,1024]{1,0:T(4,128)(2,1)S(1)}, u32[]{:S(2)}, u32[]{:S(2)}) collective-permute-start(bf16[4,1024]{1,0:T(4,128)(2,1)S(1)} %get-tuple-element.25), channel_id=1, source_target_pairs={{0,3},{1,0},{2,1},{3,2},{4,7},{5,4},{6,5},{7,6},{8,11},{9,8},{10,9... | collective-permute-start | bytes 24584 | tf_op jit(solution)/shard_map/ppermute | solution.py:101
  6.0 0.0 collective-permute-start.3
  6.0 2.1 %shard_map.47 = (f32[4,3,16,1024]{3,2,1,0:T(8,128)S(1)}, f32[4,3,16,1024]{3,2,1,0:T(8,128)S(1)}, s32[16,1024]{1,0:T(8,128)S(1)}, f32[8,8,128]{2,1,0:T(8,128)S(1)}, f32[4,16,1024]{2,1,0:T(8,128)S(1)}) custom-call(s32[4,16,1024]{2,1,0:T(8,128)} %bins_hbm.3, s32[4,16,1024]{2,1,0:T(8,128)S(1)} %get-tuple-element.18.bins_vmem, ...), custom_call_target="tpu_custom_call" | custom-call | tf_op jit(solution)/shard_map/pallas_call | solution.py:345
  8.1 0.0 collective-permute-done.2.refs_2_
  8.1 0.0 collective-permute-done.refs_0_
  8.1 0.0 collective-permute-done.1.refs_1_
  8.1 0.5 %shard_map.48.refs_9_ = s32[8,2,16,128]{3,2,1,0:T(8,128)S(1)} custom-call(bf16[1,16,1024]{2,1,0:T(8,128)(2,1)S(1)} %collective-permute-done.refs_0_, bf16[1,16,1024]{2,1,0:T(8,128)(2,1)S(1)} %collective-permute-done.1.refs_1_, bf16[4,1024]{1,0:T(4,128)(2,1)S(1)} %collective-permute-done.2.refs_2_, ...), custom_call_target="tpu_custom_call" | custom-call | tf_op jit(solution)/shard_map/pallas_call | solution.py:345
  8.6 0.5 %collective-permute-done.3.refs_8_ = bf16[4,1024]{1,0:T(4,128)(2,1)S(1)} collective-permute-done((bf16[4,1024]{1,0:T(4,128)(2,1)S(1)}, bf16[4,1024]{1,0:T(4,128)(2,1)S(1)}, u32[]{:S(2)}, u32[]{:S(2)}) %collective-permute-start.3) | collective-permute-done | bytes 8224 | tf_op jit(solution)/shard_map/ppermute | solution.py:101
  9.1 11.8 %all_to_all.5.words_ref = s32[8,2,16,128]{3,2,1,0:T(8,128)S(1)} all-to-all(s32[8,2,16,128]{3,2,1,0:T(8,128)S(1)} %shard_map.49), channel_id=1, replica_groups=mesh['depth'=8,'strip'=4] {'depth'}, dimensions={0} | all-to-all | bytes 262144 | tf_op jit(solution)/shard_map/all_to_all | solution.py:412
  20.9 0.7 %shard_map.50 = f32[64,128]{1,0:T(8,128)} custom-call(f32[8,8,128]{2,1,0:T(8,128)S(1)} %get-tuple-element.22.before_ref, s32[8,2,16,128]{3,2,1,0:T(8,128)S(1)} %all_to_all.5.words_ref), custom_call_target="tpu_custom_call" | custom-call | tf_op jit(solution)/shard_map/pallas_call | solution.py:345
  (1 shorter events, 0.0 us)
Async XLA Ops:
  1.0 7.1 %collective-permute-start = (bf16[1,16,1024]{2,1,0:T(8,128)(2,1)S(1)}, bf16[1,16,1024]{2,1,0:T(8,128)(2,1)S(1)}, u32[]{:S(2)}, u32[]{:S(2)}) collective-permute-start(bf16[1,16,1024]{2,1,0:T(8,128)(2,1)S(1)} %get-tuple-element.23), channel_id=1, source_target_pairs={{4,8},{5,9},{6,10},{7,11},{8,4},{9,5},{10,6},{11,7},{12,16},{13,17... | collective-permute-start | bytes 98312 | tf_op jit(solution)/shard_map/ppermute | solution.py:96
  1.6 6.5 %collective-permute-start.1 = (bf16[1,16,1024]{2,1,0:T(8,128)(2,1)S(1)}, bf16[1,16,1024]{2,1,0:T(8,128)(2,1)S(1)}, u32[]{:S(2)}, u32[]{:S(2)}) collective-permute-start(bf16[1,16,1024]{2,1,0:T(8,128)(2,1)S(1)} %get-tuple-element.24), channel_id=1, source_target_pairs={{0,4},{1,5},{2,6},{3,7},{4,0},{5,1},{6,2},{7,3},{8,12},{9,13},{10,... | collective-permute-start | bytes 98312 | tf_op jit(solution)/shard_map/ppermute | solution.py:96
  5.5 2.6 %collective-permute-start.2 = (bf16[4,1024]{1,0:T(4,128)(2,1)S(1)}, bf16[4,1024]{1,0:T(4,128)(2,1)S(1)}, u32[]{:S(2)}, u32[]{:S(2)}) collective-permute-start(bf16[4,1024]{1,0:T(4,128)(2,1)S(1)} %get-tuple-element.25), channel_id=1, source_target_pairs={{0,3},{1,0},{2,1},{3,2},{4,7},{5,4},{6,5},{7,6},{8,11},{9,8},{10,9... | collective-permute-start | bytes 24584 | tf_op jit(solution)/shard_map/ppermute | solution.py:101
  6.0 3.1 %collective-permute-start.3 = (bf16[4,1024]{1,0:T(4,128)(2,1)S(1)}, bf16[4,1024]{1,0:T(4,128)(2,1)S(1)}, u32[]{:S(2)}, u32[]{:S(2)}) collective-permute-start(bf16[4,1024]{1,0:T(4,128)(2,1)S(1)} %get-tuple-element.30), channel_id=1, source_target_pairs={{0,1},{1,2},{2,3},{3,0},{4,5},{5,6},{6,7},{7,4},{8,9},{9,10},{10,1... | collective-permute-start | bytes 24584 | tf_op jit(solution)/shard_map/ppermute | solution.py:101

commit v12 on v9

--- a/solution.py
+++ b/solution.py
@@ -330,7 +330,7 @@
                 out_ref[c : c + 1, at : at + LANES] = image[c][t * tall + r : t * tall + r + 1, :]
 
 
-def call(kernel, out_shape, *operands, spaces=None, scratch=()):
+def call(kernel, out_shape, *operands, spaces=None, scratch=(), aliases=None):
     vmem = pl.BlockSpec(memory_space=pltpu.VMEM)
     spaces = spaces or {}
     return pl.pallas_call(
@@ -341,6 +341,7 @@
         ],
         out_specs=jax.tree.map(lambda _: vmem, out_shape),
         scratch_shapes=scratch,
+        input_output_aliases=aliases or {},
         compiler_params=pltpu.CompilerParams(vmem_limit_bytes=VMEM_BYTES),
     )(*operands)
 
@@ -397,7 +398,7 @@
     operands = (plane_far, plane_near, row_below, density, first, second, depth)
     words = call(functools.partial(top_strip_kernel, bricks), words_shape, *operands)
     words = call(
-        functools.partial(other_strips_kernel, bricks), words_shape, *operands, row_above, words
+        functools.partial(other_strips_kernel, bricks), words_shape, *operands, row_above, words, aliases={8: 0}
     )
     words = lax.all_to_all(words, "depth", 0, 0, tiled=True)
     return call(

time: 21.9 us -> 21.9 us (level)
  no operation moved by 1% of the time
where the time goes in v12:
time: 21.9 us; the launch traced here: 21.7 us
  blocking collectives  11.8 us (54%)
  starting transfers between devices  5.06 us (23%)
  Pallas kernels  4.34 us (20%)
  waiting for transfers between devices  0.39 us (2%)
    all_to_all x1, blocking collectives, per_device(): words = lax.all_to_all(words, 'depth', 0, 0, tiled=True)  11.8 us
    ppermute x2, starting transfers between devices, swap_planes(): return lax.ppermute(cells, ('depth', 'strip'), flat)  4.55 us
    pallas_call x5, Pallas kernels, call(): pl.pallas_call(kernel, out_shape=out_shape, in_specs=[pl.BlockSpec(memory...  4.34 us
    ppermute x2, starting transfers between devices, rotate_rows(): lax.ppermute(cells, 'strip', [(i, (i + step) % strips) for i in range(str...  0.51 us
  transfers between devices with their start and end apart: 4, of which 1 were waited for; matrix products, arithmetic and copies ran while one was open for 0% of the time, Pallas kernels for 12%

profile of v12, /device:TPU:0, one launch (start us, length us, event | category | flops | bytes accessed | tf_op | source)
XLA Modules:
  0.0 21.7 jit_solution(7706578171179511289)
XLA Ops:
  0.0 1.0 %shard_map.46 = (bf16[4,16,1024]{2,1,0:T(8,128)(2,1)S(1)}, s32[4,16,1024]{2,1,0:T(8,128)S(1)}, f32[4,128]{1,0:T(4,128)S(1)}, s32[1,8]{1,0:T(1,128)S(1)}, bf16[1,...) custom-call(bf16[4,16,1024]{2,1,0:T(8,128)(2,1)} %density_hbm.1, ...), custom_call_target="tpu_custom_call" | custom-call | tf_op jit(solution)/shard_map/pallas_call | solution.py:336
  1.0 0.6 %collective-permute-start = (bf16[1,16,1024]{2,1,0:T(8,128)(2,1)S(1)}, bf16[1,16,1024]{2,1,0:T(8,128)(2,1)S(1)}, u32[]{:S(2)}, u32[]{:S(2)}) collective-permute-start(bf16[1,16,1024]{2,1,0:T(8,128)(2,1)S(1)} %get-tuple-element.22), channel_id=1, source_target_pairs={{4,8},{5,9},{6,10},{7,11},{8,4},{9,5},{10,6},{11,7},{12,16},{13,17... | collective-permute-start | bytes 98312 | tf_op jit(solution)/shard_map/ppermute | solution.py:96
  1.6 4.0 %collective-permute-start.1 = (bf16[1,16,1024]{2,1,0:T(8,128)(2,1)S(1)}, bf16[1,16,1024]{2,1,0:T(8,128)(2,1)S(1)}, u32[]{:S(2)}, u32[]{:S(2)}) collective-permute-start(bf16[1,16,1024]{2,1,0:T(8,128)(2,1)S(1)} %get-tuple-element.23), channel_id=1, source_target_pairs={{0,4},{1,5},{2,6},{3,7},{4,0},{5,1},{6,2},{7,3},{8,12},{9,13},{10,... | collective-permute-start | bytes 98312 | tf_op jit(solution)/shard_map/ppermute | solution.py:96
  5.5 0.5 %collective-permute-start.2 = (bf16[4,1024]{1,0:T(4,128)(2,1)S(1)}, bf16[4,1024]{1,0:T(4,128)(2,1)S(1)}, u32[]{:S(2)}, u32[]{:S(2)}) collective-permute-start(bf16[4,1024]{1,0:T(4,128)(2,1)S(1)} %get-tuple-element.24), channel_id=1, source_target_pairs={{0,3},{1,0},{2,1},{3,2},{4,7},{5,4},{6,5},{7,6},{8,11},{9,8},{10,9... | collective-permute-start | bytes 24584 | tf_op jit(solution)/shard_map/ppermute | solution.py:101
  6.0 0.0 collective-permute-start.3
  6.0 2.0 %shard_map.47 = (f32[4,3,16,1024]{3,2,1,0:T(8,128)S(1)}, f32[4,3,16,1024]{3,2,1,0:T(8,128)S(1)}, s32[16,1024]{1,0:T(8,128)S(1)}, f32[8,8,128]{2,1,0:T(8,128)S(1)}) custom-call(s32[4,16,1024]{2,1,0:T(8,128)} %bins_hbm.3, s32[4,16,1024]{2,1,0:T(8,128)S(1)} %get-tuple-element.17.bins_vmem, bf16[4,16,1024]{2,1,0:T(8,128)(2,1)S(1)} %get-tuple-element.18.refs_0_.refs_3_, ...), custom_call_target="tpu_custom_call" | custom-call | tf_op jit(solution)/shard_map/pallas_call | solution.py:336
  8.1 0.0 collective-permute-done.2.refs_2_
  8.1 0.0 collective-permute-done.refs_0_
  8.1 0.0 collective-permute-done.1.refs_1_
  8.1 0.6 %shard_map.48.refs_8_ = s32[8,2,16,128]{3,2,1,0:T(8,128)S(1)} custom-call(bf16[1,16,1024]{2,1,0:T(8,128)(2,1)S(1)} %collective-permute-done.refs_0_, bf16[1,16,1024]{2,1,0:T(8,128)(2,1)S(1)} %collective-permute-done.1.refs_1_, bf16[4,1024]{1,0:T(4,128)(2,1)S(1)} %collective-permute-done.2.refs_2_, ...), custom_call_target="tpu_custom_call" | custom-call | tf_op jit(solution)/shard_map/pallas_call | solution.py:336
  8.7 0.4 %collective-permute-done.3.refs_7_ = bf16[4,1024]{1,0:T(4,128)(2,1)S(1)} collective-permute-done((bf16[4,1024]{1,0:T(4,128)(2,1)S(1)}, bf16[4,1024]{1,0:T(4,128)(2,1)S(1)}, u32[]{:S(2)}, u32[]{:S(2)}) %collective-permute-start.3) | collective-permute-done | bytes 8224 | tf_op jit(solution)/shard_map/ppermute | solution.py:101
  9.1 11.8 %all_to_all.5.words_ref = s32[8,2,16,128]{3,2,1,0:T(8,128)S(1)} all-to-all(s32[8,2,16,128]{3,2,1,0:T(8,128)S(1)} %shard_map.49), channel_id=1, replica_groups=mesh['depth'=8,'strip'=4] {'depth'}, dimensions={0} | all-to-all | bytes 262144 | tf_op jit(solution)/shard_map/all_to_all | solution.py:403
  20.9 0.7 %shard_map.50 = f32[4,2048]{1,0:T(4,128)} custom-call(f32[8,8,128]{2,1,0:T(8,128)S(1)} %get-tuple-element.21.before_ref, s32[8,2,16,128]{3,2,1,0:T(8,128)S(1)} %all_to_all.5.words_ref), custom_call_target="tpu_custom_call" | custom-call | tf_op jit(solution)/shard_map/pallas_call | solution.py:336
  (1 shorter events, 0.0 us)
Async XLA Ops:
  1.0 7.1 %collective-permute-start = (bf16[1,16,1024]{2,1,0:T(8,128)(2,1)S(1)}, bf16[1,16,1024]{2,1,0:T(8,128)(2,1)S(1)}, u32[]{:S(2)}, u32[]{:S(2)}) collective-permute-start(bf16[1,16,1024]{2,1,0:T(8,128)(2,1)S(1)} %get-tuple-element.22), channel_id=1, source_target_pairs={{4,8},{5,9},{6,10},{7,11},{8,4},{9,5},{10,6},{11,7},{12,16},{13,17... | collective-permute-start | bytes 98312 | tf_op jit(solution)/shard_map/ppermute | solution.py:96
  1.6 6.5 %collective-permute-start.1 = (bf16[1,16,1024]{2,1,0:T(8,128)(2,1)S(1)}, bf16[1,16,1024]{2,1,0:T(8,128)(2,1)S(1)}, u32[]{:S(2)}, u32[]{:S(2)}) collective-permute-start(bf16[1,16,1024]{2,1,0:T(8,128)(2,1)S(1)} %get-tuple-element.23), channel_id=1, source_target_pairs={{0,4},{1,5},{2,6},{3,7},{4,0},{5,1},{6,2},{7,3},{8,12},{9,13},{10,... | collective-permute-start | bytes 98312 | tf_op jit(solution)/shard_map/ppermute | solution.py:96
  5.5 2.6 %collective-permute-start.2 = (bf16[4,1024]{1,0:T(4,128)(2,1)S(1)}, bf16[4,1024]{1,0:T(4,128)(2,1)S(1)}, u32[]{:S(2)}, u32[]{:S(2)}) collective-permute-start(bf16[4,1024]{1,0:T(4,128)(2,1)S(1)} %get-tuple-element.24), channel_id=1, source_target_pairs={{0,3},{1,0},{2,1},{3,2},{4,7},{5,4},{6,5},{7,6},{8,11},{9,8},{10,9... | collective-permute-start | bytes 24584 | tf_op jit(solution)/shard_map/ppermute | solution.py:101
  6.0 3.1 %collective-permute-start.3 = (bf16[4,1024]{1,0:T(4,128)(2,1)S(1)}, bf16[4,1024]{1,0:T(4,128)(2,1)S(1)}, u32[]{:S(2)}, u32[]{:S(2)}) collective-permute-start(bf16[4,1024]{1,0:T(4,128)(2,1)S(1)} %get-tuple-element.28), channel_id=1, source_target_pairs={{0,1},{1,2},{2,3},{3,0},{4,5},{5,6},{6,7},{7,4},{8,9},{9,10},{10,1... | collective-permute-start | bytes 24584 | tf_op jit(solution)/shard_map/ppermute | solution.py:101

commit v13 on v10

--- a/solution.py
+++ b/solution.py
@@ -302,6 +302,12 @@
         shade(bricks, row_above[...].astype(jnp.float32), *refs, out_ref)
 
 
+def tree_sum(values):
+    while len(values) > 1:
+        values = [sum(values[i : i + 2]) for i in range(0, len(values), 2)]
+    return values[0]
+
+
 def merge_kernel(planes, before_ref, words_ref, out_ref):
     bricks, _, rows, _ = words_ref.shape
     f32 = jnp.float32
@@ -313,16 +319,17 @@
         codes.append(
             [lax.shift_right_logical(low, 16), high & 0xFFFF, lax.shift_right_logical(high, 16)]
         )
-    colour = [jnp.zeros((rows, LANES), f32)] * 3
+    terms = [[], [], []]
     for b in range(bricks):
-        base = jnp.full((rows, LANES), COLOUR_LOW, f32)
-        for other in range(bricks):
-            if other != b:
-                base = base - before_ref[b, other : other + 1, :] * depth[other]
+        ahead = tree_sum(
+            [before_ref[b, other : other + 1, :] * depth[other] for other in range(bricks) if other != b]
+        )
+        base = COLOUR_LOW - ahead
         for c in range(3):
             term = jnp.exp2(codes[b][c].astype(f32) * (1.0 / COLOUR_STEPS) + base)
-            colour[c] = colour[c] + jnp.where(codes[b][c] > 0, term, 0.0)
-    image = colour + [jnp.exp2(-sum(depth))]
+            terms[c].append(jnp.where(codes[b][c] > 0, term, 0.0))
+    colour = [tree_sum(values) for values in terms]
+    image = colour + [jnp.exp2(-tree_sum(depth))]
     for c in range(4):
         out_ref[pl.ds(c, rows, stride=4), :] = image[c]
 

time: 21.9 us -> 21.8 us (level)
  no operation moved by 1% of the time
where the time goes in v13:
time: 21.8 us; the launch traced here: 21.7 us
  blocking collectives  11.8 us (54%)
  starting transfers between devices  5.06 us (23%)
  Pallas kernels  4.31 us (20%)
  waiting for transfers between devices  0.41 us (2%)
    all_to_all x1, blocking collectives, per_device(): words = lax.all_to_all(words, 'depth', 0, 0, tiled=True)  11.8 us
    ppermute x2, starting transfers between devices, swap_planes(): return lax.ppermute(cells, ('depth', 'strip'), flat)  4.55 us
    pallas_call x5, Pallas kernels, call(): pl.pallas_call(kernel, out_shape=out_shape, in_specs=[pl.BlockSpec(memory...  4.31 us
    ppermute x2, starting transfers between devices, rotate_rows(): lax.ppermute(cells, 'strip', [(i, (i + step) % strips) for i in range(str...  0.51 us
  transfers between devices with their start and end apart: 4, of which 1 were waited for; matrix products, arithmetic and copies ran while one was open for 0% of the time, Pallas kernels for 12%

profile of v13, /device:TPU:0, one launch (start us, length us, event | category | flops | bytes accessed | tf_op | source)
XLA Modules:
  0.0 21.7 jit_solution(2186414059335262928)
XLA Ops:
  0.0 1.0 %shard_map.46 = (bf16[4,16,1024]{2,1,0:T(8,128)(2,1)S(1)}, s32[4,16,1024]{2,1,0:T(8,128)S(1)}, f32[4,128]{1,0:T(4,128)S(1)}, s32[1,8]{1,0:T(1,128)S(1)}, bf16[1,...) custom-call(bf16[4,16,1024]{2,1,0:T(8,128)(2,1)} %density_hbm.1, ...), custom_call_target="tpu_custom_call" | custom-call | tf_op jit(solution)/shard_map/pallas_call | solution.py:340
  1.0 0.6 %collective-permute-start = (bf16[1,16,1024]{2,1,0:T(8,128)(2,1)S(1)}, bf16[1,16,1024]{2,1,0:T(8,128)(2,1)S(1)}, u32[]{:S(2)}, u32[]{:S(2)}) collective-permute-start(bf16[1,16,1024]{2,1,0:T(8,128)(2,1)S(1)} %get-tuple-element.22), channel_id=1, source_target_pairs={{4,8},{5,9},{6,10},{7,11},{8,4},{9,5},{10,6},{11,7},{12,16},{13,17... | collective-permute-start | bytes 98312 | tf_op jit(solution)/shard_map/ppermute | solution.py:96
  1.6 4.0 %collective-permute-start.1 = (bf16[1,16,1024]{2,1,0:T(8,128)(2,1)S(1)}, bf16[1,16,1024]{2,1,0:T(8,128)(2,1)S(1)}, u32[]{:S(2)}, u32[]{:S(2)}) collective-permute-start(bf16[1,16,1024]{2,1,0:T(8,128)(2,1)S(1)} %get-tuple-element.23), channel_id=1, source_target_pairs={{0,4},{1,5},{2,6},{3,7},{4,0},{5,1},{6,2},{7,3},{8,12},{9,13},{10,... | collective-permute-start | bytes 98312 | tf_op jit(solution)/shard_map/ppermute | solution.py:96
  5.5 0.5 %collective-permute-start.2 = (bf16[4,1024]{1,0:T(4,128)(2,1)S(1)}, bf16[4,1024]{1,0:T(4,128)(2,1)S(1)}, u32[]{:S(2)}, u32[]{:S(2)}) collective-permute-start(bf16[4,1024]{1,0:T(4,128)(2,1)S(1)} %get-tuple-element.24), channel_id=1, source_target_pairs={{0,3},{1,0},{2,1},{3,2},{4,7},{5,4},{6,5},{7,6},{8,11},{9,8},{10,9... | collective-permute-start | bytes 24584 | tf_op jit(solution)/shard_map/ppermute | solution.py:101
  6.0 0.0 collective-permute-start.3
  6.0 2.0 %shard_map.47 = (f32[4,3,16,1024]{3,2,1,0:T(8,128)S(1)}, f32[4,3,16,1024]{3,2,1,0:T(8,128)S(1)}, s32[16,1024]{1,0:T(8,128)S(1)}, f32[8,8,128]{2,1,0:T(8,128)S(1)}) custom-call(s32[4,16,1024]{2,1,0:T(8,128)} %bins_hbm.3, s32[4,16,1024]{2,1,0:T(8,128)S(1)} %get-tuple-element.17.bins_vmem, bf16[4,16,1024]{2,1,0:T(8,128)(2,1)S(1)} %get-tuple-element.18.refs_0_.refs_3_, ...), custom_call_target="tpu_custom_call" | custom-call | tf_op jit(solution)/shard_map/pallas_call | solution.py:340
  8.1 0.0 collective-permute-done.2.refs_2_
  8.1 0.0 collective-permute-done.refs_0_
  8.1 0.0 collective-permute-done.1.refs_1_
  8.1 0.6 %shard_map.48.refs_8_ = s32[8,2,16,128]{3,2,1,0:T(8,128)S(1)} custom-call(bf16[1,16,1024]{2,1,0:T(8,128)(2,1)S(1)} %collective-permute-done.refs_0_, bf16[1,16,1024]{2,1,0:T(8,128)(2,1)S(1)} %collective-permute-done.1.refs_1_, bf16[4,1024]{1,0:T(4,128)(2,1)S(1)} %collective-permute-done.2.refs_2_, ...), custom_call_target="tpu_custom_call" | custom-call | tf_op jit(solution)/shard_map/pallas_call | solution.py:340
  8.7 0.4 %collective-permute-done.3.refs_7_ = bf16[4,1024]{1,0:T(4,128)(2,1)S(1)} collective-permute-done((bf16[4,1024]{1,0:T(4,128)(2,1)S(1)}, bf16[4,1024]{1,0:T(4,128)(2,1)S(1)}, u32[]{:S(2)}, u32[]{:S(2)}) %collective-permute-start.3) | collective-permute-done | bytes 8224 | tf_op jit(solution)/shard_map/ppermute | solution.py:101
  9.1 11.8 %all_to_all.5.words_ref = s32[8,2,16,128]{3,2,1,0:T(8,128)S(1)} all-to-all(s32[8,2,16,128]{3,2,1,0:T(8,128)S(1)} %shard_map.49), channel_id=1, replica_groups=mesh['depth'=8,'strip'=4] {'depth'}, dimensions={0} | all-to-all | bytes 262144 | tf_op jit(solution)/shard_map/all_to_all | solution.py:406
  20.9 0.7 %shard_map.50 = f32[64,128]{1,0:T(8,128)} custom-call(f32[8,8,128]{2,1,0:T(8,128)S(1)} %get-tuple-element.21.before_ref, s32[8,2,16,128]{3,2,1,0:T(8,128)S(1)} %all_to_all.5.words_ref), custom_call_target="tpu_custom_call" | custom-call | tf_op jit(solution)/shard_map/pallas_call | solution.py:340
  (1 shorter events, 0.0 us)
Async XLA Ops:
  1.0 7.1 %collective-permute-start = (bf16[1,16,1024]{2,1,0:T(8,128)(2,1)S(1)}, bf16[1,16,1024]{2,1,0:T(8,128)(2,1)S(1)}, u32[]{:S(2)}, u32[]{:S(2)}) collective-permute-start(bf16[1,16,1024]{2,1,0:T(8,128)(2,1)S(1)} %get-tuple-element.22), channel_id=1, source_target_pairs={{4,8},{5,9},{6,10},{7,11},{8,4},{9,5},{10,6},{11,7},{12,16},{13,17... | collective-permute-start | bytes 98312 | tf_op jit(solution)/shard_map/ppermute | solution.py:96
  1.6 6.5 %collective-permute-start.1 = (bf16[1,16,1024]{2,1,0:T(8,128)(2,1)S(1)}, bf16[1,16,1024]{2,1,0:T(8,128)(2,1)S(1)}, u32[]{:S(2)}, u32[]{:S(2)}) collective-permute-start(bf16[1,16,1024]{2,1,0:T(8,128)(2,1)S(1)} %get-tuple-element.23), channel_id=1, source_target_pairs={{0,4},{1,5},{2,6},{3,7},{4,0},{5,1},{6,2},{7,3},{8,12},{9,13},{10,... | collective-permute-start | bytes 98312 | tf_op jit(solution)/shard_map/ppermute | solution.py:96
  5.5 2.6 %collective-permute-start.2 = (bf16[4,1024]{1,0:T(4,128)(2,1)S(1)}, bf16[4,1024]{1,0:T(4,128)(2,1)S(1)}, u32[]{:S(2)}, u32[]{:S(2)}) collective-permute-start(bf16[4,1024]{1,0:T(4,128)(2,1)S(1)} %get-tuple-element.24), channel_id=1, source_target_pairs={{0,3},{1,0},{2,1},{3,2},{4,7},{5,4},{6,5},{7,6},{8,11},{9,8},{10,9... | collective-permute-start | bytes 24584 | tf_op jit(solution)/shard_map/ppermute | solution.py:101
  6.0 3.1 %collective-permute-start.3 = (bf16[4,1024]{1,0:T(4,128)(2,1)S(1)}, bf16[4,1024]{1,0:T(4,128)(2,1)S(1)}, u32[]{:S(2)}, u32[]{:S(2)}) collective-permute-start(bf16[4,1024]{1,0:T(4,128)(2,1)S(1)} %get-tuple-element.28), channel_id=1, source_target_pairs={{0,1},{1,2},{2,3},{3,0},{4,5},{5,6},{6,7},{7,4},{8,9},{9,10},{10,1... | collective-permute-start | bytes 24584 | tf_op jit(solution)/shard_map/ppermute | solution.py:101
